TPU v7x, 32 devices: a whole 2x2x4 slice. The times are simulated.
32 devices in a mesh: fsdp: 16 (over z, y, core), rep: 2 (over x).
Axes of the slice: x: 2, y: 2, z: 4, core: 2. Of those that a mesh axis runs over, the one named last changes fastest.
Arguments:
- inputs: bfloat16 [8192, 1536], P(('fsdp', 'rep')), may hold values from -6 to 6
- segment_ids: int32 [32, 256], P(('fsdp', 'rep')), may hold values from 0 to 5, never falling along the last dimension, each value on 1 to 128 neighbouring positions
- norm_one: bfloat16 [1536], P(('fsdp', 'rep')), may hold values from 0.5 to 1.5
- w_query: bfloat16 [1536, 1536], P(('fsdp', 'rep')), may hold values from -0.15625 to 0.15625
- w_key: bfloat16 [1536, 1536], P(('fsdp', 'rep')), may hold values from -0.15625 to 0.15625
- w_value: bfloat16 [1536, 1536], P(('fsdp', 'rep')), may hold values from -0.15625 to 0.15625
- w_gate_out: bfloat16 [1536, 1536], P(('fsdp', 'rep')), may hold values from -0.15625 to 0.15625
- w_forget: bfloat16 [1536, 24], P(('fsdp', 'rep')), may hold values from -0.15625 to 0.15625
- forget_bias: bfloat16 [24], replicated, may hold values from 1 to 7
- w_output: bfloat16 [1536, 1536], P(('fsdp', 'rep')), may hold values from -0.625 to 0.625
- norm_two: bfloat16 [1536], P(('fsdp', 'rep')), may hold values from 0.5 to 1.5
- w_ffn_gate: bfloat16 [1536, 4096], P(('fsdp', 'rep')), may hold values from -0.15625 to 0.15625
- w_ffn_up: bfloat16 [1536, 4096], P(('fsdp', 'rep')), may hold values from -0.15625 to 0.15625
- w_ffn_down: bfloat16 [4096, 1536], P(('fsdp', 'rep')), may hold values from -0.09375 to 0.09375
- out_grad: bfloat16 [8192, 1536], P(('fsdp', 'rep')), may hold values from -6 to 6
Outputs:
- layer_output: bfloat16 [8192, 1536], P(('fsdp', 'rep'))
- input_grad: float32 [8192, 1536], P(('fsdp', 'rep'))
- norm_one_grad: float32 [1536], P(('fsdp', 'rep'))
- query_grad: float32 [1536, 1536], P(('fsdp', 'rep'))
- key_grad: float32 [1536, 1536], P(('fsdp', 'rep'))
- value_grad: float32 [1536, 1536], P(('fsdp', 'rep'))
- gate_out_grad: float32 [1536, 1536], P(('fsdp', 'rep'))
- forget_grad: float32 [1536, 24], P(('fsdp', 'rep'))
- forget_bias_grad: float32 [24], replicated
- w_output_grad: float32 [1536, 1536], P(('fsdp', 'rep'))
- norm_two_grad: float32 [1536], P(('fsdp', 'rep'))
- ffn_gate_grad: float32 [1536, 4096], P(('fsdp', 'rep'))
- ffn_up_grad: float32 [1536, 4096], P(('fsdp', 'rep'))
- ffn_down_grad: float32 [4096, 1536], P(('fsdp', 'rep'))
Inputs may be any that keep to these rules, and one draw needn't show every extreme that they name: `segment_ids`: segment numbers never fall along a sequence; each document spans 1 to 128 tokens, and one spans exactly 128.
All inputs are finite; a program needn't handle non-finite values.
Results may differ from a plain program's by a relative error of at most 0.014.
Values may be sent and summed in bfloat16 or wider, within the bound.
No kernel may reach another device: no remote copies, remote signals or barrier semaphores. Data moves between devices by JAX's collectives and lax.ppermute only.
A program may use at most 384 MiB of HBM per device.

v0:
```python
import jax
import jax.numpy as jnp
from jax import lax
from jax.sharding import PartitionSpec as P

H = 24
HEAD = 64


epsilon = 1e-06
negative_big = -1e30
block_heads = 4


def row_norm(tokens):
    inverse_rms = lax.rsqrt(jnp.mean(tokens * tokens, -1, keepdims=True) + epsilon)
    return (tokens * inverse_rms, inverse_rms)


def norm_back(grad_hat, normed, inverse_rms):
    return inverse_rms * (grad_hat - normed * jnp.mean(grad_hat * normed, -1, keepdims=True))


def product(left, right):
    return jnp.dot(left, right, preferred_element_type=jnp.float32)


def product_nt(left, right):
    return lax.dot_general(
        left, right, (((1,), (1,)), ((), ())), preferred_element_type=jnp.float32
    )


def product_tn(left, right):
    return lax.dot_general(
        left, right, (((0,), (0,)), ((), ())), preferred_element_type=jnp.float32
    )


def heads_first(matrix):
    rows_count = matrix.shape[0]
    split_rows = matrix.reshape(rows_count, H, HEAD).transpose(1, 0, 2)
    return split_rows.reshape(H // block_heads, block_heads, rows_count, HEAD)


def heads_back(matrix):
    groups_count, inner_count, rows_count, head_width = matrix.shape
    merged = matrix.reshape(groups_count * inner_count, rows_count, head_width).transpose(1, 0, 2)
    return merged.reshape(rows_count, groups_count * inner_count * head_width)


def score_block(query_group, key_group, decay_group, allowed):
    scores = (
        jnp.einsum("gid,gjd->gij", query_group, key_group, preferred_element_type=jnp.float32)
        * 0.125
    )
    scores = scores + decay_group[:, :, None] - decay_group[:, None, :]
    return jnp.where(allowed[None], scores, negative_big)


def attend(group_items, allowed):
    query_group, key_group, value_group, decay_group = group_items
    scores = score_block(query_group, key_group, decay_group, allowed)
    row_max = jnp.max(scores, -1, keepdims=True)
    shifted = jnp.exp(scores - row_max)
    row_total = jnp.sum(shifted, -1, keepdims=True)
    att_probs = (shifted / row_total).astype(jnp.bfloat16)
    attended = jnp.einsum(
        "gij,gjd->gid", att_probs, value_group, preferred_element_type=jnp.float32
    )
    return (attended, (row_max + jnp.log(row_total))[..., 0])


def attend_back(group_items, allowed):
    query_group, key_group, value_group, decay_group, log_total, grad_group = group_items
    scores = score_block(query_group, key_group, decay_group, allowed)
    att_probs = jnp.exp(scores - log_total[..., None])
    grad_prob = jnp.einsum(
        "gid,gjd->gij", grad_group, value_group, preferred_element_type=jnp.float32
    )
    row_delta = jnp.sum(att_probs * grad_prob, -1, keepdims=True)
    grad_scores = (att_probs * (grad_prob - row_delta)).astype(jnp.bfloat16)
    grad_query = (
        jnp.einsum("gij,gjd->gid", grad_scores, key_group, preferred_element_type=jnp.float32)
        * 0.125
    ).astype(jnp.bfloat16)
    grad_key = (
        jnp.einsum("gij,gid->gjd", grad_scores, query_group, preferred_element_type=jnp.float32)
        * 0.125
    ).astype(jnp.bfloat16)
    grad_value = jnp.einsum(
        "gij,gid->gjd",
        att_probs.astype(jnp.bfloat16),
        grad_group,
        preferred_element_type=jnp.float32,
    ).astype(jnp.bfloat16)
    scores_wide = grad_scores.astype(jnp.float32)
    grad_decay = jnp.sum(scores_wide, -1) - jnp.sum(scores_wide, -2)
    return (grad_query, grad_key, grad_value, grad_decay)


def shards(
    inputs,
    segment_ids,
    norm_one,
    w_query,
    w_key,
    w_value,
    w_gate_out,
    w_forget,
    forget_bias,
    w_output,
    norm_two,
    w_ffn_gate,
    w_ffn_up,
    w_ffn_down,
    out_grad,
):
    tokens = inputs.astype(jnp.float32)
    length = tokens.shape[0]
    width = tokens.shape[1]
    heads_count = w_forget.shape[1]
    hidden_count = w_ffn_gate.shape[1]
    segment = segment_ids[0]
    places = jnp.arange(length)
    allowed = (segment[:, None] == segment[None, :]) & (places[None, :] <= places[:, None])
    normed, inv_one = row_norm(tokens)
    attn_full = (
        lax.all_gather(norm_one, ("fsdp", "rep"), axis=0, tiled=True),
        lax.all_gather(w_query, ("fsdp", "rep"), axis=0, tiled=True),
        lax.all_gather(w_key, ("fsdp", "rep"), axis=0, tiled=True),
        lax.all_gather(w_value, ("fsdp", "rep"), axis=0, tiled=True),
        lax.all_gather(w_gate_out, ("fsdp", "rep"), axis=0, tiled=True),
        lax.all_gather(w_forget, ("fsdp", "rep"), axis=0, tiled=True),
        lax.all_gather(w_output, ("fsdp", "rep"), axis=0, tiled=True),
    )
    hidden_one = (normed * attn_full[0].astype(jnp.float32)).astype(jnp.bfloat16)
    query_rows = product(hidden_one, attn_full[1]).astype(jnp.bfloat16)
    key_rows = product(hidden_one, attn_full[2]).astype(jnp.bfloat16)
    value_rows = product(hidden_one, attn_full[3]).astype(jnp.bfloat16)
    out_gate = jax.nn.sigmoid(product(hidden_one, attn_full[4]))
    forget_pre = product(hidden_one, attn_full[5]) + forget_bias.astype(jnp.float32)
    decay_sum = jnp.cumsum(jax.nn.log_sigmoid(forget_pre), axis=0)
    query_heads = heads_first(query_rows)
    key_heads = heads_first(key_rows)
    value_heads = heads_first(value_rows)
    decay_heads = decay_sum.T.reshape(H // block_heads, block_heads, length)
    attended_heads, log_total = lax.map(
        lambda group_items: attend(group_items, allowed),
        (query_heads, key_heads, value_heads, decay_heads),
    )
    attended = heads_back(attended_heads)
    gated_att = (attended * out_gate).astype(jnp.bfloat16)
    middle = tokens + product(gated_att, attn_full[6])
    normed_two, inv_two = row_norm(middle)
    ffn_full = (
        lax.all_gather(norm_two, ("fsdp", "rep"), axis=0, tiled=True),
        lax.all_gather(w_ffn_gate, ("fsdp", "rep"), axis=0, tiled=True),
        lax.all_gather(w_ffn_up, ("fsdp", "rep"), axis=0, tiled=True),
        lax.all_gather(w_ffn_down, ("fsdp", "rep"), axis=0, tiled=True),
    )
    hidden_two = (normed_two * ffn_full[0].astype(jnp.float32)).astype(jnp.bfloat16)
    gate_ffn = product(hidden_two, ffn_full[1])
    up_ffn = product(hidden_two, ffn_full[2])
    sigmoid_gate = jax.nn.sigmoid(gate_ffn)
    activation = (gate_ffn * sigmoid_gate * up_ffn).astype(jnp.bfloat16)
    layer_output = (middle + product(activation, ffn_full[3])).astype(jnp.bfloat16)
    grad_out = out_grad.astype(jnp.float32)
    ffn_back = (
        lax.all_gather(norm_two, ("fsdp", "rep"), axis=0, tiled=True),
        lax.all_gather(w_ffn_gate, ("fsdp", "rep"), axis=0, tiled=True),
        lax.all_gather(w_ffn_up, ("fsdp", "rep"), axis=0, tiled=True),
        lax.all_gather(w_ffn_down, ("fsdp", "rep"), axis=0, tiled=True),
    )
    grad_act = product_nt(out_grad, ffn_back[3])
    grad_gate = (grad_act * up_ffn * sigmoid_gate * (1.0 + gate_ffn * (1.0 - sigmoid_gate))).astype(
        jnp.bfloat16
    )
    grad_up = (grad_act * gate_ffn * sigmoid_gate).astype(jnp.bfloat16)
    grad_hidden_two = product_nt(grad_gate, ffn_back[1]) + product_nt(grad_up, ffn_back[2])
    grad_hat_two = grad_hidden_two * ffn_back[0].astype(jnp.float32)
    ffn_rows_term = jnp.concatenate(
        (
            jnp.sum(grad_hidden_two * normed_two, 0)[:, None],
            product_tn(hidden_two, grad_gate),
            product_tn(hidden_two, grad_up),
        ),
        1,
    )
    ffn_terms = (ffn_rows_term, product_tn(activation, out_grad))
    ffn_reduced = (
        lax.psum_scatter(ffn_terms[0], ("fsdp", "rep"), scatter_dimension=0, tiled=True),
        lax.psum_scatter(ffn_terms[1], ("fsdp", "rep"), scatter_dimension=0, tiled=True),
    )
    ffn_rows_sum = ffn_reduced[0]
    norm_two_grad = ffn_rows_sum[:, 0]
    ffn_gate_grad = ffn_rows_sum[:, 1 : 1 + hidden_count]
    ffn_up_grad = ffn_rows_sum[:, 1 + hidden_count : 1 + 2 * hidden_count]
    grad_middle = grad_out + norm_back(grad_hat_two, normed_two, inv_two)
    grad_branch = grad_middle.astype(jnp.bfloat16)
    attn_back = (
        lax.all_gather(norm_one, ("fsdp", "rep"), axis=0, tiled=True),
        lax.all_gather(w_query, ("fsdp", "rep"), axis=0, tiled=True),
        lax.all_gather(w_key, ("fsdp", "rep"), axis=0, tiled=True),
        lax.all_gather(w_value, ("fsdp", "rep"), axis=0, tiled=True),
        lax.all_gather(w_gate_out, ("fsdp", "rep"), axis=0, tiled=True),
        lax.all_gather(w_forget, ("fsdp", "rep"), axis=0, tiled=True),
        lax.all_gather(w_output, ("fsdp", "rep"), axis=0, tiled=True),
    )
    grad_gated = product_nt(grad_branch, attn_back[6])
    grad_att = (grad_gated * out_gate).astype(jnp.bfloat16)
    grad_gate_pre = (grad_gated * attended * out_gate * (1.0 - out_gate)).astype(jnp.bfloat16)
    back_heads = lax.map(
        lambda group_items: attend_back(group_items, allowed),
        (query_heads, key_heads, value_heads, decay_heads, log_total, heads_first(grad_att)),
    )
    grad_query = heads_back(back_heads[0])
    grad_key = heads_back(back_heads[1])
    grad_value = heads_back(back_heads[2])
    grad_decay = back_heads[3].reshape(H, length).T
    grad_later = jnp.flip(jnp.cumsum(jnp.flip(grad_decay, 0), 0), 0)
    grad_forget = (grad_later * jax.nn.sigmoid(-forget_pre)).astype(jnp.bfloat16)
    forget_bias_grad = lax.psum(jnp.sum(grad_forget.astype(jnp.float32), 0), ("fsdp", "rep"))
    grad_hidden_one = (
        product_nt(grad_query, attn_back[1])
        + product_nt(grad_key, attn_back[2])
        + product_nt(grad_value, attn_back[3])
        + product_nt(grad_gate_pre, attn_back[4])
        + product_nt(grad_forget, attn_back[5])
    )
    grad_hat_one = grad_hidden_one * attn_back[0].astype(jnp.float32)
    attn_terms = jnp.concatenate(
        (
            jnp.sum(grad_hidden_one * normed, 0)[:, None],
            product_tn(hidden_one, grad_query),
            product_tn(hidden_one, grad_key),
            product_tn(hidden_one, grad_value),
            product_tn(hidden_one, grad_gate_pre),
            product_tn(hidden_one, grad_forget),
            product_tn(gated_att, grad_branch),
        ),
        1,
    )
    attn_reduced = lax.psum_scatter(attn_terms, ("fsdp", "rep"), scatter_dimension=0, tiled=True)
    norm_one_grad = attn_reduced[:, 0]
    query_grad = attn_reduced[:, 1 : 1 + width]
    key_grad = attn_reduced[:, 1 + width : 1 + 2 * width]
    value_grad = attn_reduced[:, 1 + 2 * width : 1 + 3 * width]
    gate_out_grad = attn_reduced[:, 1 + 3 * width : 1 + 4 * width]
    forget_grad = attn_reduced[:, 1 + 4 * width : 1 + 4 * width + heads_count]
    w_output_grad = attn_reduced[:, 1 + 4 * width + heads_count :]
    input_grad = grad_middle + norm_back(grad_hat_one, normed, inv_one)
    return (
        layer_output,
        input_grad,
        norm_one_grad,
        query_grad,
        key_grad,
        value_grad,
        gate_out_grad,
        forget_grad,
        forget_bias_grad,
        w_output_grad,
        norm_two_grad,
        ffn_gate_grad,
        ffn_up_grad,
        ffn_reduced[1],
    )


def solution(mesh):
    in_specs = (
        P(("fsdp", "rep"), None),
        P(("fsdp", "rep"), None),
        P(("fsdp", "rep")),
        P(("fsdp", "rep"), None),
        P(("fsdp", "rep"), None),
        P(("fsdp", "rep"), None),
        P(("fsdp", "rep"), None),
        P(("fsdp", "rep"), None),
        P(),
        P(("fsdp", "rep"), None),
        P(("fsdp", "rep")),
        P(("fsdp", "rep"), None),
        P(("fsdp", "rep"), None),
        P(("fsdp", "rep"), None),
        P(("fsdp", "rep"), None),
    )
    out_specs = (
        P(("fsdp", "rep"), None),
        P(("fsdp", "rep"), None),
        P(("fsdp", "rep")),
        P(("fsdp", "rep"), None),
        P(("fsdp", "rep"), None),
        P(("fsdp", "rep"), None),
        P(("fsdp", "rep"), None),
        P(("fsdp", "rep"), None),
        P(),
        P(("fsdp", "rep"), None),
        P(("fsdp", "rep")),
        P(("fsdp", "rep"), None),
        P(("fsdp", "rep"), None),
        P(("fsdp", "rep"), None),
    )
    return jax.shard_map(shards, mesh=mesh, in_specs=in_specs, out_specs=out_specs, check_vma=False)
```

profile of v0, /device:TPU:0, one launch (start us, length us, event | category | flops | bytes accessed | tf_op | source)
XLA Modules:
  0.0 2031.9 jit_solution(3232582284194372395)
XLA Ops:
  13.3 42.2 %all-reduce.2 = (bf16[1536]{0:T(1024)(128)(2,1)S(1)}, bf16[1536]{0:T(1024)(128)(2,1)S(1)}) all-reduce(bf16[1536]{0:T(1024)(128)(2,1)S(1)} %dynamic-update-slice, bf16[1536]{0:T(1024)(128)(2,1)S(1)} %dynamic-update-slice.1), channel_id=1, replica_groups=mesh['fsdp'=16,'rep'=2] {'fsdp','rep'}, use_global_device_ids=true, to_apply=%add | all-reduce | flops 3072 | bytes 12288
  55.6 67.5 %all-gather = bf16[32,48,24]{1,2,0:T(8,128)(2,1)S(1)} all-gather(bf16[1,48,24]{1,2,0:T(8,128)(2,1)S(1)} %bitcast.242), channel_id=1, replica_groups=mesh['fsdp'=16,'rep'=2] {'fsdp','rep'}, dimensions={0}, use_global_device_ids=true | all-gather | bytes 76032 | tf_op jit(solution)/shard_map/all_gather | solution.py:134
  125.0 3.8 convolution_convert_fusion.2
  129.1 14.9 all-gather.14.cloned.1.call-done
  143.9 3.8 convolution_convert_fusion.1
  148.0 61.4 %all-gather.10.cloned.1.call-done = bf16[1536,1536]{1,0:T(8,128)(2,1)} async-done(((bf16[48,1536]{1,0:T(8,128)(2,1)}), bf16[1536,1536]{1,0:T(8,128)(2,1)}) %all-gather.10.cloned.1.call-update) | async-done | bytes 4718608 | tf_op jit(solution)/shard_map/all_gather | solution.py:130
  209.3 4.6 convolution_convert_fusion.3
  215.4 10.7 while.30
  227.3 1.9 copy.76
  229.2 45.4 %all-gather.16.cloned.1.call-done = bf16[1536,1536]{1,0:T(8,128)(2,1)} async-done(((bf16[48,1536]{1,0:T(8,128)(2,1)}), bf16[1536,1536]{1,0:T(8,128)(2,1)}) %all-gather.16.cloned.1.call-update) | async-done | bytes 4718608 | tf_op jit(solution)/shard_map/all_gather | solution.py:133
  274.6 5.2 multiply_convert_fusion.7
  279.8 60.0 %all-gather.18.cloned.1.call-done = bf16[1536,1536]{1,0:T(8,128)(2,1)} async-done(((bf16[48,1536]{1,0:T(8,128)(2,1)}), bf16[1536,1536]{1,0:T(8,128)(2,1)}) %all-gather.18.cloned.1.call-update) | async-done | bytes 4718608 | tf_op jit(solution)/shard_map/all_gather | solution.py:135
  339.8 4.1 multiply_reduce_fusion.3
  344.1 93.3 %all-gather.22.cloned.1.call-done = bf16[1536,4096]{1,0:T(8,128)(2,1)} async-done(((bf16[48,4096]{1,0:T(8,128)(2,1)}), bf16[1536,4096]{1,0:T(8,128)(2,1)}) %all-gather.22.cloned.1.call-update) | async-done | bytes 12582928 | tf_op jit(solution)/shard_map/all_gather | solution.py:159
  437.4 9.5 fusion.99
  446.9 87.7 %all-gather.20.cloned.1.call-done = bf16[1536,4096]{1,0:T(8,128)(2,1)} async-done(((bf16[48,4096]{1,0:T(8,128)(2,1)}), bf16[1536,4096]{1,0:T(8,128)(2,1)}) %all-gather.20.cloned.1.call-update) | async-done | bytes 12582928 | tf_op jit(solution)/shard_map/all_gather | solution.py:158
  534.6 9.5 fusion.98
  544.1 87.6 %all-gather.24.cloned.1.call-done = bf16[4096,1536]{1,0:T(8,128)(2,1)} async-done(((bf16[128,1536]{1,0:T(8,128)(2,1)}), bf16[4096,1536]{1,0:T(8,128)(2,1)}) %all-gather.24.cloned.1.call-update) | async-done | bytes 12582928 | tf_op jit(solution)/shard_map/all_gather | solution.py:160
  631.7 11.0 multiply_convert_fusion.1
  642.8 8.0 fusion.100
  650.8 6.9 multiply_reduce_fusion.1
  658.9 5.2 fusion.70
  664.1 2.4 multiply_convert_fusion.4
  666.8 47.2 %while.31 = (s32[]{:T(128)}, bf16[6,4,256,64]{2,3,1,0:T(8,128)(2,1)}, bf16[6,4,256,64]{2,3,1,0:T(8,128)(2,1)}, bf16[6,4,256,64]{2,3,1,0:T(8,128)(2,1)}, f32[6,4,...) while((s32[]{:T(128)}, ...), condition=%wide.region_13.14_spmd.clone, body=%wide.region_9.13_spmd.clone.sunk | while | flops 171964416 | bytes 9369741 | solution.py:213
  668.2 1.6 multiply_reduce_fusion.5
  671.1 1.8 fusion.185
  673.0 1.8 fusion.184
  676.1 1.6 multiply_reduce_fusion.5
  679.0 1.8 fusion.185
  680.8 1.8 fusion.184
  684.0 1.6 multiply_reduce_fusion.5
  686.9 1.8 fusion.185
  688.7 1.8 fusion.184
  691.8 1.6 multiply_reduce_fusion.5
  694.7 1.8 fusion.185
  696.6 1.8 fusion.184
  699.7 1.6 multiply_reduce_fusion.5
  702.6 1.8 fusion.185
  704.4 1.8 fusion.184
  707.6 1.6 multiply_reduce_fusion.5
  710.5 1.8 fusion.185
  712.3 1.8 fusion.184
  716.5 5.2 fusion.82
  721.6 5.2 fusion.88
  726.8 6.0 fusion.86
  732.9 5.1 fusion.84
  739.5 1.4 convolution_add_fusion.3
  740.9 1.4 convolution_add_fusion.2
  743.8 1.7 fusion.68
  745.6 121.2 %concatenate.6 = f32[1536,7705]{0,1:T(8,128)} concatenate(f32[1536,1]{0,1:T(1,128)S(1)} %broadcast_in_dim.68, f32[1536,1536]{0,1:T(8,128)} %fusion.84, f32[1536,1536]{0,1:T(8,128)} %fusion.86, f32[1536,1536]{0,1:T(8,128)} %fusion.88, f32[1536,1536]{0,1:T(8,128)} %fusion.82, f32[1536,24]{0,1:T(8,128)S(1)} %fusion.80, f32[1536,1536]{0,1:T(8,128)} %fusion.70), dimensions={1} | concatenate | bytes 94679040 | tf_op jit(solution)/shard_map/concatenate | solution.py:232
  866.8 46.9 %copy.91 = f32[1536,7705]{1,0:T(8,128)} copy(f32[1536,7705]{0,1:T(8,128)} %concatenate.6) | data formatting | bytes 94679040
  914.0 16.2 fusion.103
  930.3 15.1 fusion.102
  945.4 66.1 %concatenate.7 = f32[1536,8193]{1,0:T(8,128)} concatenate(f32[1536,1]{1,0:T(8,128)S(1)} %broadcast_in_dim.78, f32[1536,4096]{1,0:T(8,128)} %fusion.102, f32[1536,4096]{1,0:T(8,128)} %fusion.103), dimensions={1} | concatenate | bytes 100675584 | tf_op jit(solution)/shard_map/concatenate | solution.py:182
  1011.5 1.5 copy-done.7
  1013.0 11.9 fusion.104
  1025.6 42.2 %psum.7 = f32[24]{0:T(128)} all-reduce(f32[24]{0:T(128)S(1)} %copy-done.24), channel_id=1, replica_groups=mesh['fsdp'=16,'rep'=2] {'fsdp','rep'}, use_global_device_ids=true, to_apply=%region_20.21 | all-reduce | flops 24 | bytes 192 | tf_op jit(solution)/shard_map/psum | solution.py:223
  1067.9 3.1 fusion.67
  1071.0 7.7 fusion.58
  1078.7 248.1 %reduce-scatter.10.cloned.1.call-done = f32[48,7705]{1,0:T(8,128)} async-done(((f32[1536,7705]{1,0:T(8,128)}), f32[48,7705]{1,0:T(8,128)}) %reduce-scatter.10.cloned.1.call-update) | async-done | bytes 1479376
  1329.6 2.9 fusion.97
  1332.5 440.1 %reduce-scatter.6.cloned.1.call-done = f32[48,8193]{1,0:T(8,128)} async-done(((f32[1536,8193]{1,0:T(8,128)}), f32[48,8193]{1,0:T(8,128)}) %reduce-scatter.6.cloned.1.call-update) | async-done | bytes 1573072 | tf_op jit(solution)/shard_map/reduce_scatter | solution.py:192
  1773.9 3.0 fusion.96
  1776.9 248.3 %reduce-scatter.8.cloned.1.call-done = f32[128,1536]{1,0:T(8,128)} async-done(((f32[4096,1536]{1,0:T(8,128)}), f32[128,1536]{1,0:T(8,128)}) %reduce-scatter.8.cloned.1.call-update) | async-done | bytes 786448 | tf_op jit(solution)/shard_map/reduce_scatter | solution.py:193
  (230 shorter events, 49.6 us)
Async XLA Ops:
  7.2 5.6 copy-start.25
  7.2 5.6 copy-start.26
  7.2 5.9 copy-start.27
  7.2 48.3 %copy-start.23 = (bf16[48,24]{0,1:T(8,128)(2,1)S(1)}, bf16[48,24]{0,1:T(8,128)(2,1)}, u32[]{:S(2)}) copy-start(bf16[48,24]{0,1:T(8,128)(2,1)} %param.26) | copy-start | bytes 6916
  7.2 116.1 %copy-start = (bf16[256,1536]{1,0:T(8,128)(2,1)S(1)}, bf16[256,1536]{1,0:T(8,128)(2,1)}, u32[]{:S(2)}) copy-start(bf16[256,1536]{1,0:T(8,128)(2,1)} %param.19) | copy-start | bytes 2359300
  7.2 117.8 %all-gather.12.cloned.1.call-start = ((), (), s32[]{:S(2)}) async-start(), calls=%async_computation.4 | async-start | bytes 4866048 | tf_op jit(solution)/shard_map/all_gather | solution.py:131
  8.0 136.0 %all-gather.14.cloned.1.call-start = ((), (), s32[]{:S(2)}) async-start(), calls=%async_computation.5 | async-start | bytes 4866048 | tf_op jit(solution)/shard_map/all_gather | solution.py:132
  8.7 200.6 %all-gather.10.cloned.1.call-start = ((), (), s32[]{:S(2)}) async-start(), calls=%async_computation.3 | async-start | bytes 4866048 | tf_op jit(solution)/shard_map/all_gather | solution.py:130
  9.4 265.1 %all-gather.16.cloned.1.call-start = ((), (), s32[]{:S(2)}) async-start(), calls=%async_computation.6 | async-start | bytes 4866048 | tf_op jit(solution)/shard_map/all_gather | solution.py:133
  10.0 329.8 %all-gather.18.cloned.1.call-start = ((), (), s32[]{:S(2)}) async-start(), calls=%async_computation.7 | async-start | bytes 4866048 | tf_op jit(solution)/shard_map/all_gather | solution.py:135
  10.6 426.8 %all-gather.22.cloned.1.call-start = ((), (), s32[]{:S(2)}) async-start(), calls=%async_computation.9 | async-start | bytes 12976128 | tf_op jit(solution)/shard_map/all_gather | solution.py:159
  11.2 523.4 %all-gather.20.cloned.1.call-start = ((), (), s32[]{:S(2)}) async-start(), calls=%async_computation.8 | async-start | bytes 12976128 | tf_op jit(solution)/shard_map/all_gather | solution.py:158
  11.9 619.8 %all-gather.24.cloned.1.call-start = ((), (), s32[]{:S(2)}) async-start(), calls=%async_computation.10 | async-start | bytes 12976128 | tf_op jit(solution)/shard_map/all_gather | solution.py:160
  12.7 1314.1 %reduce-scatter.10.cloned.1.call-start = ((), (), s32[]{:S(2)}) async-start(), calls=%async_computation.13 | async-start | bytes 49471488
  214.0 1.4 copy-start.22
  226.1 0.9 copy-start.11
  226.1 1.2 copy-start.12
  226.1 3.1 copy-start.13
  229.2 50.7 %copy-start.5 = (f32[256,1536]{1,0:T(8,128)}, f32[256,1536]{1,0:T(8,128)S(1)}, u32[]{:S(2)}) copy-start(f32[256,1536]{1,0:T(8,128)S(1)} %copy.76) | copy-start | bytes 4718596
  343.9 313.8 %copy-start.3 = (f32[256,1536]{1,0:T(8,128)}, f32[256,1536]{1,0:T(8,128)S(1)}, u32[]{:S(2)}) copy-start(f32[256,1536]{1,0:T(8,128)S(1)} %get-tuple-element.288) | copy-start | bytes 4718596
  642.8 8.0 copy-start.14
  642.8 8.0 copy-start.16
  650.8 6.9 copy-start.9
  657.7 1.1 copy-start.21
  657.8 6.3 slice-start
  658.9 5.2 copy-start.1
  658.9 5.2 copy-start.6
  658.9 5.2 slice-start.1
  658.9 5.2 copy-start.17
  714.1 2.4 copy-start.10
  716.4 5.2 copy-start.18
  721.6 5.2 copy-start.19
  726.8 6.0 copy-start.20
  726.8 11.1 slice-start.8
  726.8 12.6 slice-start.2
  732.9 5.1 slice-start.9
  732.9 6.5 slice-start.3
  738.0 2.9 slice-start.4
  739.4 1.5 slice-start.5
  739.4 2.9 slice-start.6
  740.9 1.5 slice-start.7
  913.7 858.8 %reduce-scatter.6.cloned.1.call-start = ((), (), s32[]{:S(2)}) async-start(), calls=%async_computation.11 | async-start | bytes 52715520 | tf_op jit(solution)/shard_map/reduce_scatter | solution.py:192
  914.0 16.2 copy-start.15
  1011.4 1.6 copy-start.7
  1011.4 1013.7 %reduce-scatter.8.cloned.1.call-start = ((), (), s32[]{:S(2)}) async-start(), calls=%async_computation.12 | async-start | bytes 25952256 | tf_op jit(solution)/shard_map/reduce_scatter | solution.py:193
  1025.0 0.7 copy-start.24
  1025.0 42.9 %copy-start.2 = (f32[256,1536]{1,0:T(8,128)S(1)}, f32[256,1536]{1,0:T(8,128)}, u32[]{:S(2)}) copy-start(f32[256,1536]{1,0:T(8,128)} %copy-done.1) | copy-start | bytes 4718596
  1067.9 3.1 copy-start.4
  1067.9 3.1 copy-start.8
Sparse Core Ops, SparseCore 0:
  11.0 67.2 all-gather.11
  81.2 62.6 all-gather.13
  146.8 62.4 all-gather.9
  212.1 62.4 all-gather.15
  277.4 62.4 all-gather.17
  342.6 94.7 all-gather.21
  440.3 94.2 all-gather.19
  537.5 94.2 all-gather.23
  913.8 412.9 reduce-scatter.9
  1333.0 439.4 reduce-scatter.5
  1780.7 244.4 reduce-scatter.7
where the time goes:
time: 2050 us; the launch traced here: 2030 us
  waiting for transfers between devices  1390 us (68%)
  local copies, waits for them, and re-layouts  254 us (12%)
  matrix products  208 us (10%)
  blocking collectives  152 us (7%)
    reduce_scatter x1, waiting for transfers between devices, shards(): lax.psum_scatter(ffn_terms[0], ('fsdp', 'rep'), scatter_dimension=0, tile...  440 us
    unnamed x12, waiting for transfers between devices  253 us
    reduce_scatter x1, waiting for transfers between devices, shards(): lax.psum_scatter(ffn_terms[1], ('fsdp', 'rep'), scatter_dimension=0, tile...  248 us
    concatenate x1, local copies, waits for them, and re-layouts, shards(): jnp.concatenate((jnp.sum(grad_hidden_one * normed, 0)[:, None], product_t...  121 us
    all_gather x1, waiting for transfers between devices, shards(): lax.all_gather(w_ffn_up, ('fsdp', 'rep'), axis=0, tiled=True)  93.3 us
    all_gather x1, waiting for transfers between devices, shards(): lax.all_gather(w_ffn_gate, ('fsdp', 'rep'), axis=0, tiled=True)  87.7 us
    all_gather x1, waiting for transfers between devices, shards(): lax.all_gather(w_ffn_down, ('fsdp', 'rep'), axis=0, tiled=True)  87.6 us
    dot_general x9, matrix products, product_tn(): lax.dot_general(left, right, (((0,), (0,)), ((), ())), preferred_element_...  70.3 us
  transfers between devices with their start and end apart: 11, of which 10 were waited for; matrix products, arithmetic and copies ran while one was open for 9% of the time, Pallas kernels for 0%

commit v1 on v0

v1 whole, which is shorter than its diff:
```python
import math

import jax
import jax.numpy as jnp
from jax import lax
from jax.experimental import pallas as pl
from jax.experimental.pallas import tpu as pltpu
from jax.sharding import Mesh
from jax.sharding import PartitionSpec as P

H = 24
HEAD = 64
Z = 4
GROUP = 4
LANES = 128
TILE = 256
LOCAL_HEADS = H // GROUP

epsilon = 1e-06
negative_big = -1e30
bf16 = jnp.bfloat16
f32 = jnp.float32
ALL = ("z", "w", "y", "c", "r", "x")
REST = ("w", "r")
ANY = pl.BlockSpec(memory_space=pl.ANY)
kernel_params = pltpu.CompilerParams(vmem_limit_bytes=48 * 1024 * 1024)


def row_norm(tokens):
    inverse_rms = lax.rsqrt(jnp.mean(tokens * tokens, -1, keepdims=True) + epsilon)
    return (tokens * inverse_rms, inverse_rms)


def norm_back(grad_hat, normed, inverse_rms):
    return inverse_rms * (grad_hat - normed * jnp.mean(grad_hat * normed, -1, keepdims=True))


def product(left, right):
    return jnp.dot(left, right, preferred_element_type=f32)


def product_nt(left, right, precision=None):
    return lax.dot_general(
        left, right, (((1,), (1,)), ((), ())), preferred_element_type=f32, precision=precision
    )


def product_tn(left, right, precision=None):
    return lax.dot_general(
        left, right, (((0,), (0,)), ((), ())), preferred_element_type=f32, precision=precision
    )


def place_in_ring(index):
    return index ^ (index >> 1)


def found_at(step):
    return place_in_ring((place_in_ring(lax.axis_index("z")) - step) & 3)


def along_z(block):
    return lax.ppermute(block, "z", [(0, 1), (1, 3), (3, 2), (2, 0)])


def swap(value, axis):
    return lax.ppermute(value, axis, [(0, 1), (1, 0)])


def has_rest():
    return lax.axis_size("w") * lax.axis_size("r") > 1


def over_rest(block):
    if not has_rest():
        return block[None, None]
    return lax.all_gather(lax.all_gather(block, "r"), "w")


def sum_over_rest(total):
    if not has_rest():
        return total[0, 0]
    return lax.psum_scatter(lax.psum_scatter(total, "w"), "r")


def order(values, after):
    count = len(values)
    if has_rest():
        return values
    return pl.pallas_call(
        lambda *refs: None,
        in_specs=[ANY] * (count + len(after)),
        out_specs=[ANY] * count,
        out_shape=[jax.ShapeDtypeStruct(value.shape, value.dtype) for value in values],
        input_output_aliases={at: at for at in range(count)},
        name="order",
    )(*values, *after)


def halves(part, axis):
    mine = lax.axis_index(axis)
    return [
        (part(found_at(step), 1 - mine), lambda step=step: part(found_at(step), mine).astype(f32))
        for step in range(1, Z + 1)
    ]


def arrange(arrivals, axis, shape, reorder, spots):
    mine = lax.axis_index(axis)
    blocks = [block for _, _, block in arrivals]
    if has_rest():
        whole = jnp.zeros((Z, 2, *blocks[0].shape), blocks[0].dtype)
        for step, other, block in arrivals:
            at = (found_at(step), mine ^ other)
            whole = lax.dynamic_update_slice(whole, block[None, None], (*at, *[0] * block.ndim))
        return reorder(whole)
    blocks = [block.reshape(-1, block.shape[-1]) for block in blocks]
    places = jnp.stack([found_at(step) for step in range(Z)] + [mine, 1 - mine]).astype(jnp.int32)

    def kernel(places_ref, *refs):
        block_refs, outs, sems = refs[: len(blocks)], refs[len(blocks) : -1], refs[-1]
        copies = []
        for at, (step, other, _) in enumerate(arrivals):
            for out, first, rows, spot in spots(outs, places_ref[step], places_ref[Z + other]):
                source = block_refs[at].at[pl.ds(first, rows)]
                copies.append(pltpu.make_async_copy(source, spot, sems.at[len(copies)]))
        for copy in copies:
            copy.start()
        for copy in copies:
            copy.wait()

    return pl.pallas_call(
        kernel,
        in_specs=[pl.BlockSpec(memory_space=pltpu.SMEM)]
        + [pl.BlockSpec(memory_space=pltpu.VMEM)] * len(blocks),
        out_specs=[ANY] * len(shape),
        out_shape=[jax.ShapeDtypeStruct(one, bf16) for one in shape],
        scratch_shapes=[pltpu.SemaphoreType.DMA((8 * len(blocks),))],
        compiler_params=kernel_params,
        name="arrange",
    )(places, *blocks)


def group_gather(own, axis):
    over = swap(own, axis)
    return jnp.concatenate((own, over, swap(own, "c"), swap(over, "c")), 0)


def group_scatter(partial, axis):
    rows = partial.shape[0] // GROUP
    from_core = swap(partial[2 * rows :], "c").astype(f32)
    near = partial[: 2 * rows].astype(f32) + from_core
    return near[:rows] + swap(near[rows:].astype(bf16), axis).astype(f32)


def exchange(shares, axes):
    return lax.all_to_all(shares, axes, 0, 0, tiled=True)


def transpose_quarters(block):
    return lax.ppermute(
        block, ("z", "c", "x"), [(i * GROUP + j, j * GROUP + i) for i in range(Z) for j in range(GROUP)]
    )


def pack_heads(weights):
    rows, width = weights[0].shape
    part = width // GROUP

    def kernel(*refs):
        for at, ref in enumerate(refs[:-1]):
            for to in range(GROUP):
                refs[-1][to, :, at * part : (at + 1) * part] = ref[:, to * part : (to + 1) * part]

    return pl.pallas_call(
        kernel, out_shape=jax.ShapeDtypeStruct((GROUP, rows, len(weights) * part), bf16), name="pack_heads"
    )(*weights)


def unpack_heads(shares, count):
    rows, part = shares.shape[1], shares.shape[2] // count

    def kernel(ref, *outs):
        for at, out in enumerate(outs):
            for to in range(GROUP):
                out[:, to * part : (to + 1) * part] = ref[to, :, at * part : (at + 1) * part].astype(f32)

    whole = jax.ShapeDtypeStruct((rows, GROUP * part), f32)
    return pl.pallas_call(kernel, out_shape=[whole] * count, name="unpack_heads")(shares)


def unit_chunks(unit):
    for at_z in range(Z):
        for place in range(GROUP):
            for at_x in range(2):
                here = (at_z * 2 + at_x) * unit
                yield place, here // TILE * 2 * TILE + here % TILE, ((at_z * GROUP + place) * 2 + at_x) * unit


def pack_units(gate, up, unit):
    rows, hidden = gate.shape
    part = hidden // GROUP
    if has_rest():
        size = (rows, Z, lax.axis_size("w"), 2, 2, lax.axis_size("r"), 2, unit)
        both = [
            one.reshape(size).transpose(3, 4, 0, 1, 6, 2, 5, 7).reshape(GROUP, rows, part // TILE, TILE)
            for one in (gate, up)
        ]
        return jnp.stack(both, 3).reshape(GROUP, rows, 2 * part)

    def kernel(gate_ref, up_ref, out):
        for place, here, there in unit_chunks(unit):
            out[place, :, here : here + unit] = gate_ref[:, there : there + unit]
            out[place, :, here + TILE : here + TILE + unit] = up_ref[:, there : there + unit]

    return pl.pallas_call(
        kernel, out_shape=jax.ShapeDtypeStruct((GROUP, rows, 2 * part), bf16), name="pack_units"
    )(gate, up)


def unpack_units(shares, unit):
    rows, part = shares.shape[1], shares.shape[2] // 2
    if has_rest():
        size = (2, 2, rows, Z, 2, lax.axis_size("w"), lax.axis_size("r"), unit)
        both = shares.reshape(GROUP, rows, part // TILE, 2, TILE)
        return [
            both[:, :, :, at].reshape(size).transpose(2, 3, 5, 0, 1, 6, 4, 7).reshape(rows, GROUP * part).astype(f32)
            for at in range(2)
        ]

    def kernel(ref, gate_ref, up_ref):
        for place, here, there in unit_chunks(unit):
            gate_ref[:, there : there + unit] = ref[place, :, here : here + unit].astype(f32)
            up_ref[:, there : there + unit] = ref[place, :, here + TILE : here + TILE + unit].astype(f32)

    whole = jax.ShapeDtypeStruct((rows, GROUP * part), f32)
    return pl.pallas_call(kernel, out_shape=[whole, whole], name="unpack_units")(shares)


def triangle(length):
    rows = lax.broadcasted_iota(jnp.int32, (length, length), 0)
    cols = lax.broadcasted_iota(jnp.int32, (length, length), 1)
    return rows >= cols


def decays(forget_pre, tri):
    log_gate = jax.nn.log_sigmoid(forget_pre)
    highest = lax.Precision.HIGHEST
    down = jnp.dot(tri, log_gate, preferred_element_type=f32, precision=highest)
    across = lax.dot_general(
        log_gate, tri, (((0,), (1,)), ((), ())), preferred_element_type=f32, precision=highest
    )
    return down, across


def half_mask(half):
    lane = lax.broadcasted_iota(jnp.int32, (1, LANES), 1)
    return (lane >= HEAD) == bool(half)


def attend_kernel(q_ref, k_ref, v_ref, gate_ref, forget_ref, seg_col, seg_row, gated_ref, attended_ref, log_ref):
    length = q_ref.shape[0]
    causal = triangle(length)
    down, across = decays(forget_ref[...], causal.astype(f32))
    bias = jnp.where(causal & (seg_col[...] == seg_row[0]), 0.0, negative_big)
    lane = lax.broadcasted_iota(jnp.int32, (length, LANES), 1)
    logs = jnp.zeros((length, LANES), f32)
    for pair in range(LOCAL_HEADS // 2):
        cols = slice(pair * LANES, (pair + 1) * LANES)
        query, key, value = q_ref[:, cols], k_ref[:, cols], v_ref[:, cols].astype(bf16)
        both = []
        for half in range(2):
            head = 2 * pair + half
            mine = half_mask(half)
            scaled = jnp.where(mine, query, 0) * jnp.asarray(0.125, bf16)
            scores = product_nt(scaled, key) + down[:, head : head + 1] - across[head : head + 1, :] + bias
            top = jnp.max(scores, -1, keepdims=True)
            shifted = jnp.exp(scores - top)
            total = jnp.sum(shifted, -1, keepdims=True)
            probs = (shifted * (1.0 / total)).astype(bf16)
            both.append(jnp.where(mine, product(probs, value), 0.0))
            logs = jnp.where(lane == head, top + jnp.log(total), logs)
        attended = both[0] + both[1]
        attended_ref[:, cols] = attended
        gated_ref[:, cols] = (attended * jax.nn.sigmoid(gate_ref[:, cols])).astype(bf16)
    log_ref[...] = logs


def attend_back_kernel(
    q_ref, k_ref, v_ref, gate_ref, forget_ref, seg_col, seg_row, attended_ref, log_ref, grad_ref,
    dq_ref, dk_ref, dv_ref, dgate_ref, dforget_ref,
):
    length = q_ref.shape[0]
    causal = triangle(length)
    tri = causal.astype(f32)
    down, across = decays(forget_ref[...], tri)
    bias = jnp.where(causal & (seg_col[...] == seg_row[0]), 0.0, negative_big)
    lane = lax.broadcasted_iota(jnp.int32, (length, LANES), 1)
    grad_decay = jnp.zeros((length, LANES), f32)
    for pair in range(LOCAL_HEADS // 2):
        cols = slice(pair * LANES, (pair + 1) * LANES)
        query, key, value = q_ref[:, cols], k_ref[:, cols], v_ref[:, cols].astype(bf16)
        out_gate = jax.nn.sigmoid(gate_ref[:, cols])
        grad_gated = grad_ref[:, cols]
        grad_att = (grad_gated * out_gate).astype(bf16)
        dgate_ref[:, cols] = (
            grad_gated * attended_ref[:, cols] * out_gate * (1.0 - out_gate)
        ).astype(bf16)
        dq, dk, dv = [], [], []
        for half in range(2):
            head = 2 * pair + half
            mine = half_mask(half)
            scaled = jnp.where(mine, query, 0) * jnp.asarray(0.125, bf16)
            scores = product_nt(scaled, key) + down[:, head : head + 1] - across[head : head + 1, :] + bias
            probs = jnp.exp(scores - log_ref[:, head : head + 1])
            grad_prob = product_nt(jnp.where(mine, grad_att, 0), value)
            delta = jnp.sum(probs * grad_prob, -1, keepdims=True)
            grad_scores = (probs * (grad_prob - delta)).astype(bf16)
            dq.append(product(grad_scores, key))
            dk.append(product_tn(grad_scores, query))
            dv.append(product_tn(probs.astype(bf16), grad_att))
            one = (lane == head).astype(bf16)
            grad_decay = grad_decay + product(grad_scores, one) - product_tn(grad_scores, one)
        first = half_mask(0)
        dq_ref[:, cols] = (jnp.where(first, dq[0], dq[1]) * 0.125).astype(bf16)
        dk_ref[:, cols] = (jnp.where(first, dk[0], dk[1]) * 0.125).astype(bf16)
        dv_ref[:, cols] = jnp.where(first, dv[0], dv[1]).astype(bf16)
    later = product_tn(tri, grad_decay, lax.Precision.HIGHEST)
    dforget_ref[...] = (later * jax.nn.sigmoid(-forget_ref[...])).astype(bf16)


def attention_specs(length, width):
    def columns(at):
        return pl.BlockSpec((length, width), lambda i: (i, at))

    lanes = pl.BlockSpec((length, LANES), lambda i: (i, 0))
    seg_col = pl.BlockSpec((length, 1), lambda i: (i, 0))
    seg_row = pl.BlockSpec((1, 1, length), lambda i: (i, 0, 0))
    return columns, lanes, seg_col, seg_row


def attend(query_key, value_gate, forget_pre, seg_col, seg_row, length):
    tokens, width = query_key.shape[0], query_key.shape[1] // 2
    columns, lanes, col_spec, row_spec = attention_specs(length, width)
    return pl.pallas_call(
        attend_kernel,
        grid=(tokens // length,),
        in_specs=[columns(0), columns(1), columns(0), columns(1), lanes, col_spec, row_spec],
        out_specs=[columns(0), columns(0), lanes],
        out_shape=[
            jax.ShapeDtypeStruct((tokens, width), bf16),
            jax.ShapeDtypeStruct((tokens, width), f32),
            jax.ShapeDtypeStruct((tokens, LANES), f32),
        ],
        compiler_params=kernel_params,
        cost_estimate=pl.CostEstimate(
            flops=4 * tokens * length * width, bytes_accessed=14 * tokens * width, transcendentals=0
        ),
        name="attend",
    )(query_key, query_key, value_gate, value_gate, forget_pre, seg_col, seg_row)


def attend_back(query_key, value_gate, forget_pre, seg_col, seg_row, attended, logs, grad_gated, length):
    tokens, width = query_key.shape[0], query_key.shape[1] // 2
    columns, lanes, col_spec, row_spec = attention_specs(length, width)
    whole = jax.ShapeDtypeStruct((tokens, width), bf16)
    return pl.pallas_call(
        attend_back_kernel,
        grid=(tokens // length,),
        in_specs=[
            columns(0), columns(1), columns(0), columns(1), lanes, col_spec, row_spec,
            columns(0), lanes, columns(0),
        ],
        out_specs=[columns(0), columns(0), columns(0), columns(0), lanes],
        out_shape=[whole, whole, whole, whole, jax.ShapeDtypeStruct((tokens, LANES), bf16)],
        compiler_params=kernel_params,
        cost_estimate=pl.CostEstimate(
            flops=10 * tokens * length * width, bytes_accessed=28 * tokens * width, transcendentals=0
        ),
        name="attend_back",
    )(query_key, query_key, value_gate, value_gate, forget_pre, seg_col, seg_row, attended, logs, grad_gated)


def ffn_kernel(hidden_ref, out_grad_ref, both_ref, down_ref, act_ref, dboth_ref, dhidden_ref, total):
    step = pl.program_id(0)
    both_weight, down_weight = both_ref[...], down_ref[...]
    both = product(hidden_ref[...], both_weight)
    gate_ffn, up_ffn = both[:, :TILE], both[:, TILE:]
    grad_act = product_nt(out_grad_ref[...], down_weight)
    sigmoid_gate = jax.nn.sigmoid(gate_ffn)
    silu = gate_ffn * sigmoid_gate
    act_ref[...] = (silu * up_ffn).astype(bf16)
    grad_gate = grad_act * up_ffn * sigmoid_gate * (1.0 + gate_ffn * (1.0 - sigmoid_gate))
    dboth_ref[:, :TILE] = grad_gate.astype(bf16)
    dboth_ref[:, TILE:] = (grad_act * silu).astype(bf16)
    term = product_nt(dboth_ref[...], both_weight)

    @pl.when(step == 0)
    def _():
        total[...] = term

    @pl.when(step > 0)
    def _():
        total[...] += term

    @pl.when(step == pl.num_programs(0) - 1)
    def _():
        dhidden_ref[...] = total[...].astype(bf16)


def feed_forward(hidden, out_grad, weight_both, weight_down):
    tokens, width = hidden.shape
    units = weight_down.shape[0]
    whole = pl.BlockSpec((tokens, width), lambda j: (0, 0))
    return pl.pallas_call(
        ffn_kernel,
        grid=(units // TILE,),
        in_specs=[
            whole,
            whole,
            pl.BlockSpec((width, 2 * TILE), lambda j: (0, j)),
            pl.BlockSpec((TILE, width), lambda j: (j, 0)),
        ],
        out_specs=[
            pl.BlockSpec((tokens, TILE), lambda j: (0, j)),
            pl.BlockSpec((tokens, 2 * TILE), lambda j: (0, j)),
            whole,
        ],
        out_shape=[
            jax.ShapeDtypeStruct((tokens, units), bf16),
            jax.ShapeDtypeStruct((tokens, 2 * units), bf16),
            jax.ShapeDtypeStruct((tokens, width), bf16),
        ],
        scratch_shapes=[pltpu.VMEM((tokens, width), f32)],
        compiler_params=kernel_params,
        cost_estimate=pl.CostEstimate(
            flops=10 * tokens * width * units, bytes_accessed=16 * tokens * width, transcendentals=0
        ),
        name="feed_forward",
    )(hidden, out_grad, weight_both, weight_down)


def shards(
    inputs,
    segment_ids,
    norm_one,
    w_query,
    w_key,
    w_value,
    w_gate_out,
    w_forget,
    forget_bias,
    w_output,
    norm_two,
    w_ffn_gate,
    w_ffn_up,
    w_ffn_down,
    out_grad,
):
    length, width = inputs.shape
    rows, unit = norm_one.shape[0], w_ffn_down.shape[0]
    size_w, size_r = lax.axis_size("w"), lax.axis_size("r")
    devices = math.prod(lax.axis_size(axis) for axis in ALL)
    place = lax.axis_index("c") * 2 + lax.axis_index("x")
    part = width // GROUP
    units = w_ffn_gate.shape[1] // GROUP

    heads_block = exchange(pack_heads((w_query, w_key, w_value, w_gate_out)), ("c", "x"))
    output_block = transpose_quarters(w_output)
    units_block = exchange(pack_units(w_ffn_gate, w_ffn_up, unit), ("y", "c"))
    seg_all = group_gather(segment_ids.astype(f32), "x")
    seg_col, seg_row = seg_all.reshape(-1, 1), seg_all[:, None, :]

    small = jnp.concatenate(
        (w_forget, norm_one[:, None], norm_two[:, None], jnp.zeros((rows, LANES - H - 2), bf16)), 1
    )
    small = exchange(jnp.broadcast_to(small[None], (devices, rows, LANES)), ALL).reshape(width, LANES)
    gain_one, gain_two = small[:, H].astype(f32), small[:, H + 1].astype(f32)
    forget_weight = lax.dynamic_slice(small, (0, place * LOCAL_HEADS), (width, LOCAL_HEADS))
    forget_weight = jnp.pad(forget_weight, ((0, 0), (0, LANES - LOCAL_HEADS)))
    bias_part = lax.dynamic_slice(forget_bias, (place * LOCAL_HEADS,), (LOCAL_HEADS,)).astype(f32)
    bias_part = jnp.pad(bias_part, (0, LANES - LOCAL_HEADS))

    attn = [jnp.concatenate((over_rest(heads_block.reshape(4 * rows, width)), over_rest(output_block)), 2)]
    down = [over_rest(w_ffn_down)]
    both = [over_rest(units_block.reshape(4 * rows, 2 * units))]
    attn_y, down_x, both_x = [], [swap(down[0], "x")], []

    down.append(along_z(down[0]))
    attn.append(along_z(attn[0]))
    attn_y.append(swap(attn[0], "y"))
    inputs_x = swap(inputs, "x")

    attn[1], both[0] = order((attn[1], both[0]), (attn_y[0], down[1]))
    attn.append(along_z(attn[1]))
    attn_y.append(swap(attn[1], "y"))
    both_x.append(swap(both[0], "x"))

    attn[2], down[1] = order((attn[2], down[1]), (attn_y[1], inputs_x))
    attn.append(along_z(attn[2]))
    attn_y.append(swap(attn[2], "y"))
    down_x.append(swap(down[1], "x"))

    attn[3], both[0] = order((attn[3], both[0]), (attn_y[2], both_x[0]))
    attn_y.append(swap(attn[3], "y"))
    both.append(along_z(both[0]))
    down.append(along_z(down[1]))
    out_grad_y = swap(out_grad, "y")

    both[1], down[2] = order((both[1], down[2]), (attn_y[3], down_x[1]))
    both.append(along_z(both[1]))
    both_x.append(swap(both[1], "x"))

    def arrivals(own, across):
        return [(step, other, (own, across)[other][step]) for step in range(Z) for other in range(2)]

    def attn_order(whole):
        heads = whole[:, :, :, :, : 4 * rows].reshape(Z, 2, size_w, size_r, 2, 2, rows, width)
        out = whole[:, :, :, :, 4 * rows :].reshape(2, 2, 2, size_w, size_r, rows, width)
        return (
            heads.transpose(0, 2, 1, 4, 3, 5, 6, 7).reshape(width, width),
            out.transpose(3, 2, 0, 4, 1, 5, 6).reshape(part, width),
        )

    def attn_spots(outs, at_z, at_y):
        yield outs[0], 0, 4 * rows, outs[0].at[pl.ds(pl.multiple_of((at_z * 2 + at_y) * 4 * rows, rows), 4 * rows)]
        yield outs[1], 4 * rows, rows, outs[1].at[pl.ds(pl.multiple_of((at_y * 4 + at_z) * rows, rows), rows)]

    weight_heads, weight_out = arrange(
        arrivals(attn, attn_y), "y", ((width, width), (part, width)), attn_order, attn_spots
    )

    inputs_all = jnp.concatenate((inputs, inputs_x, swap(inputs, "c"), swap(inputs_x, "c")), 0)
    out_grad_all = jnp.concatenate((out_grad, out_grad_y, swap(out_grad, "c"), swap(out_grad_y, "c")), 0)
    hidden_one = (row_norm(inputs_all.astype(f32))[0] * gain_one).astype(bf16)
    query_key = product(hidden_one, weight_heads[:, : 2 * part]).astype(bf16)
    value_gate = product(hidden_one, weight_heads[:, 2 * part :])
    forget_pre = product(hidden_one, forget_weight) + bias_part

    both[2], down[2], query_key = order((both[2], down[2], query_key), (both_x[1],))
    both.append(along_z(both[2]))
    down.append(along_z(down[2]))
    both_x.append(swap(both[2], "x"))

    gated_att, attended, logs = attend(query_key, value_gate, forget_pre, seg_col, seg_row, length)
    tokens = inputs.astype(f32)
    middle = tokens + group_scatter(product(gated_att, weight_out).astype(bf16), "x")
    normed_two, inv_two = row_norm(middle)
    hidden_own = (normed_two * gain_two).astype(bf16)

    both[3], down[2], down[3] = order((both[3], down[2], down[3]), (hidden_own, both_x[2]))
    both_x.append(swap(both[3], "x"))
    down_x += [swap(down[2], "x"), swap(down[3], "x")]
    hidden_two = group_gather(hidden_own, "y")

    def down_order(whole):
        return (whole.reshape(units, width),)

    def down_spots(outs, at_z, at_x):
        yield outs[0], 0, unit, outs[0].at[pl.ds(pl.multiple_of((at_z * 2 + at_x) * unit, unit), unit)]

    (weight_down,) = arrange(arrivals(down, down_x), "x", ((units, width),), down_order, down_spots)

    def both_order(whole):
        split = whole.reshape(Z, 2, size_w, size_r, 2, 2, rows, 2 * units)
        return (split.transpose(0, 2, 4, 5, 3, 1, 6, 7).reshape(width, 2 * units),)

    def both_spots(outs, at_z, at_x):
        for at in range(GROUP):
            first = pl.multiple_of(((at_z * GROUP + at) * 2 + at_x) * rows, rows)
            yield outs[0], at * rows, rows, outs[0].at[pl.ds(first, rows)]

    (weight_both,) = arrange(arrivals(both, both_x), "x", ((width, 2 * units),), both_order, both_spots)

    activation, grad_both, grad_hidden = feed_forward(hidden_two, out_grad_all, weight_both, weight_down)

    def down_part(term):
        split = term.reshape(Z, 2, size_w, size_r, unit, width)
        return lambda at_z, at_x: lax.dynamic_slice(
            split, (at_z, at_x, 0, 0, 0, 0), (1, 1, *split.shape[2:])
        )[0, 0]

    def both_part(term):
        split = term.reshape(Z, size_w, 4, size_r, 2, rows, 2 * units)

        def piece(at_z, at_x):
            size = (1, size_w, 4, size_r, 1, rows, 2 * units)
            found = lax.dynamic_slice(split, (at_z, 0, 0, 0, at_x, 0, 0), size)[0, :, :, :, 0]
            return found.transpose(0, 2, 1, 3, 4).reshape(size_w, size_r, 4 * rows, 2 * units)

        return piece

    quarter = grad_hidden.shape[0] // GROUP
    near = grad_hidden[: 2 * quarter].astype(f32) + swap(grad_hidden[2 * quarter :], "c").astype(f32)
    near_own, near_sent = near[:quarter], near[quarter:].astype(bf16)
    down_halves = halves(down_part(product_tn(activation, out_grad_all).astype(bf16)), "x")
    down_got = [swap(down_halves[0][0], "x")]
    near_sent, grad_both = order((near_sent, grad_both), (down_halves[0][0],))
    grad_hidden_two = near_own + swap(near_sent, "y").astype(f32)
    both_halves = halves(both_part(product_tn(hidden_two, grad_both).astype(bf16)), "x")
    both_got = [swap(both_halves[0][0], "x")]
    layer_partial = product(activation, weight_down).astype(bf16)

    grad_middle = out_grad.astype(f32) + norm_back(grad_hidden_two * gain_two, normed_two, inv_two)
    grad_branch = grad_middle.astype(bf16)
    branch_x = swap(grad_branch, "x")
    down_total = down_halves[0][1]() + down_got[0].astype(f32)
    both_total = both_halves[0][1]() + both_got[0].astype(f32)
    down_sent, both_sent, layer_partial = order(
        (down_total.astype(bf16), both_total.astype(bf16), layer_partial), (grad_branch,)
    )
    down_z, both_z = along_z(down_sent), along_z(both_sent)
    layer_output = (middle + group_scatter(layer_partial, "y")).astype(bf16)

    sent = order((down_halves[1][0], both_halves[1][0]), (branch_x,))
    down_got.append(swap(sent[0], "x"))
    both_got.append(swap(sent[1], "x"))
    grad_branch = jnp.concatenate((grad_branch, branch_x, swap(grad_branch, "c"), swap(branch_x, "c")), 0)

    grad_gated = product_nt(grad_branch, weight_out)
    grad_gated, down_z, both_z = order((grad_gated, down_z, both_z), ())
    grad_query, grad_key, grad_value, grad_gate_pre, grad_forget = attend_back(
        query_key, value_gate, forget_pre, seg_col, seg_row, attended, logs, grad_gated, length
    )

    down_total = down_halves[1][1]() + down_got[1].astype(f32) + down_z.astype(f32)
    both_total = both_halves[1][1]() + both_got[1].astype(f32) + both_z.astype(f32)
    sent = order(
        (down_total.astype(bf16), both_total.astype(bf16), down_halves[2][0], both_halves[2][0]), (grad_query,)
    )
    down_z, both_z = along_z(sent[0]), along_z(sent[1])
    down_got.append(swap(sent[2], "x"))
    both_got.append(swap(sent[3], "x"))

    grad_heads = jnp.concatenate((grad_query, grad_key, grad_value, grad_gate_pre), 1)
    heads_term = product_tn(hidden_one, grad_heads).astype(bf16)
    out_term = product_tn(gated_att, grad_branch).astype(bf16)

    def attn_part(at_z, at_y):
        heads = heads_term.reshape(Z, size_w, 2, 2, size_r, 2, rows, width)
        heads = lax.dynamic_slice(heads, (at_z, 0, at_y, 0, 0, 0, 0, 0), (1, size_w, 1, 2, size_r, 2, rows, width))
        heads = heads[0, :, 0].transpose(0, 2, 1, 3, 4, 5).reshape(size_w, size_r, 4 * rows, width)
        out = out_term.reshape(size_w, 2, 2, size_r, 2, rows, width)
        out = lax.dynamic_slice(out, (0, at_y, at_z // 2, 0, at_z % 2, 0, 0), (size_w, 1, 1, size_r, 1, rows, width))
        return jnp.concatenate((heads, out.reshape(size_w, size_r, rows, width)), 2)

    attn_halves = halves(attn_part, "y")
    attn_got = [swap(send, "y") for send, _ in attn_halves]
    hidden_partial = product_nt(grad_heads, weight_heads) + product_nt(grad_forget, forget_weight)
    grad_hidden_one = group_scatter(hidden_partial.astype(bf16), "x")

    for step in (2, 3):
        down_total = down_halves[step][1]() + down_got[step].astype(f32) + down_z.astype(f32)
        both_total = both_halves[step][1]() + both_got[step].astype(f32) + both_z.astype(f32)
        if step == 2:
            sent = (down_total.astype(bf16), both_total.astype(bf16), down_halves[3][0], both_halves[3][0])
            down_z, both_z = along_z(sent[0]), along_z(sent[1])
            down_got.append(swap(sent[2], "x"))
            both_got.append(swap(sent[3], "x"))
    ffn_down_grad = sum_over_rest(down_total)
    both_block = sum_over_rest(both_total).astype(bf16).reshape(4, rows, 2 * units)
    ffn_gate_grad, ffn_up_grad = unpack_units(exchange(both_block, ("y", "c")), unit)

    attn_total = attn_halves[0][1]() + attn_got[0].astype(f32)
    for step in range(1, Z):
        attn_z = along_z(attn_total.astype(bf16))
        attn_total = attn_halves[step][1]() + attn_got[step].astype(f32) + attn_z.astype(f32)
    attn_sum = sum_over_rest(attn_total).astype(bf16)
    w_output_grad = transpose_quarters(attn_sum[4 * rows :]).astype(f32)
    query_grad, key_grad, value_grad, gate_out_grad = unpack_heads(
        exchange(attn_sum[: 4 * rows].reshape(4, rows, width), ("c", "x")), 4
    )

    def scatter_vector(partial, extra=None):
        sent = partial.reshape(devices, rows)
        if extra is not None:
            sent = jnp.concatenate((sent, jnp.broadcast_to(extra[None], (devices, extra.shape[0]))), 1)
        return jnp.sum(exchange(sent, ALL), 0)

    norm_two_grad = scatter_vector(jnp.sum(grad_hidden_two * normed_two, 0))
    forget_term = product_tn(grad_forget, hidden_one)[:8]

    forget_got = exchange(forget_term.reshape(8, devices, rows).transpose(1, 0, 2), ALL)
    forget_got = forget_got.reshape(Z, size_w, 2, 2, size_r, 2, 8, rows).sum((0, 1, 2, 4))
    forget_grad = forget_got[:, :, :LOCAL_HEADS].reshape(H, rows).T

    bias_sum = jnp.sum(grad_forget.astype(f32), 0)[:LOCAL_HEADS]
    bias_sum = lax.dynamic_update_slice(jnp.zeros((H,), f32), bias_sum, (place * LOCAL_HEADS,))
    normed, inv_one = row_norm(tokens)
    last = scatter_vector(jnp.sum(grad_hidden_one * normed, 0), bias_sum)
    norm_one_grad, forget_bias_grad = last[:rows], last[rows:]
    input_grad = grad_middle + norm_back(grad_hidden_one * gain_one, normed, inv_one)
    return (
        layer_output,
        input_grad,
        norm_one_grad,
        query_grad,
        key_grad,
        value_grad,
        gate_out_grad,
        forget_grad,
        forget_bias_grad,
        w_output_grad,
        norm_two_grad,
        ffn_gate_grad,
        ffn_up_grad,
        ffn_down_grad,
    )


def solution(mesh):
    fsdp, rep = mesh.shape["fsdp"], mesh.shape["rep"]
    finer = Mesh(mesh.devices.reshape(Z, fsdp // 16, 2, 2, rep // 2, 2), ALL)
    rows, line = P(ALL, None), P(ALL)
    in_specs = (
        rows, rows, line, rows, rows, rows, rows, rows, P(), rows, line, rows, rows, rows, rows,
    )
    out_specs = (
        rows, rows, line, rows, rows, rows, rows, rows, P(), rows, line, rows, rows, rows,
    )
    return jax.shard_map(shards, mesh=finer, in_specs=in_specs, out_specs=out_specs, check_vma=False)
```

time: 2050 us -> 597 us (0.29)
  waiting for transfers between devices: 1390 us -> 242 us
  local copies, waits for them, and re-layouts: 254 us -> 53.4 us
  blocking collectives: 152 us -> 0 us
  matrix products: 208 us -> 57.9 us
  starting transfers between devices: 0.43 us -> 97.5 us
  Pallas kernels: 0 us -> 77.6 us
  other arithmetic: 10.5 us -> 59.8 us
    reduce_scatter x2 -> x0, waiting for transfers between devices: 688 us -> none  [the longest x1 440 us: shards(): lax.psum_scatter(ffn_terms[0], ('fsdp', 'rep'), scatter_dimension=0, tile...]
    all_gather x8 -> x0, waiting for transfers between devices: 450 us -> none  [the longest x1 93.3 us: shards(): lax.all_gather(w_ffn_up, ('fsdp', 'rep'), axis=0, tiled=True)]
    unnamed x12 -> x0, waiting for transfers between devices: 253 us -> none
    ppermute x0 -> x67, waiting for transfers between devices: none -> 213 us  [the longest x47 141 us: swap(): return lax.ppermute(value, axis, [(0, 1), (1, 0)])]
    concatenate x2 -> x5, local copies, waits for them, and re-layouts: 187 us -> 4.05 us  [the longest x1 2.08 us: shards(): jnp.concatenate((out_grad, out_grad_y, swap(out_grad, 'c'), swap(out_grad...]
    dot_general x51 -> x5, matrix products: 102 us -> 18.4 us  [product(): return jnp.dot(left, right, preferred_element_type=f32)]
    pallas_call x0 -> x21, Pallas kernels: none -> 77.6 us  [the longest x1 28.4 us: feed_forward(): pl.pallas_call(ffn_kernel, grid=(units // TILE,), in_specs=[whole, whole,...]
    all_gather x1 -> x0, blocking collectives: 67.5 us -> none  [shards(): lax.all_gather(w_forget, ('fsdp', 'rep'), axis=0, tiled=True)]
  transfers between devices with their start and end apart: 11 -> 75, of which waited for: 10 -> 36; matrix products, arithmetic and copies ran while one was open for 9% -> 24% of each run, Pallas kernels for 0% -> 6%
where the time goes in v1:
time: 597 us; the launch traced here: 590 us
  waiting for transfers between devices  242 us (41%)
  starting transfers between devices  97.5 us (16%)
  Pallas kernels  77.6 us (13%)
  other arithmetic  59.8 us (10%)
  matrix products  57.9 us (10%)
  local copies, waits for them, and re-layouts  53.4 us (9%)
    ppermute x47, waiting for transfers between devices, swap(): return lax.ppermute(value, axis, [(0, 1), (1, 0)])  141 us
    ppermute x18, waiting for transfers between devices, along_z(): return lax.ppermute(block, 'z', [(0, 1), (1, 3), (3, 2), (2, 0)])  71.6 us
    all_to_all x8, starting transfers between devices, exchange(): return lax.all_to_all(shares, axes, 0, 0, tiled=True)  36.4 us
    ppermute x47, starting transfers between devices, swap(): return lax.ppermute(value, axis, [(0, 1), (1, 0)])  35 us
    unnamed x203, local copies, waits for them, and re-layouts  29.5 us
    all_to_all x8, waiting for transfers between devices, exchange(): return lax.all_to_all(shares, axes, 0, 0, tiled=True)  28.9 us
    pallas_call x1, Pallas kernels, feed_forward(): pl.pallas_call(ffn_kernel, grid=(units // TILE,), in_specs=[whole, whole,...  28.4 us
    dot_general x5, matrix products, product_tn(): lax.dot_general(left, right, (((0,), (0,)), ((), ())), preferred_element_...  24.9 us
  transfers between devices with their start and end apart: 75, of which 36 were waited for; matrix products, arithmetic and copies ran while one was open for 24% of the time, Pallas kernels for 6%

profile of v1, /device:TPU:0, one launch (start us, length us, event | category | flops | bytes accessed | tf_op | source)
XLA Modules:
  0.0 590.3 jit_solution(18348640675539209520)
XLA Ops:
  2.6 4.3 all-to-all-start
  8.6 8.0 %all-to-all-done = bf16[4,48,1536]{2,1,0:T(8,128)(2,1)S(1)} async-done(((bf16[4,48,1536]{2,1,0:T(8,128)(2,1)}), bf16[4,48,1536]{2,1,0:T(8,128)(2,1)S(1)}, u32[]{:S(2)}, u32[]{:S(2)}) %all-to-all-start) | async-done | bytes 589856 | tf_op jit(solution)/shard_map/all_to_all | solution.py:157
  19.7 4.7 collective-permute-start.1
  26.5 3.6 all-to-all-start.1
  30.2 2.6 collective-permute-start.3
  33.4 11.1 %all-to-all-done.1 = bf16[4,48,2048]{2,1,0:T(8,128)(2,1)S(1)} async-done(((bf16[4,48,2048]{2,1,0:T(8,128)(2,1)}), bf16[4,48,2048]{2,1,0:T(8,128)(2,1)S(1)}, u32[]{:S(2)}, u32[]{:S(2)}) %all-to-all-start.1) | async-done | bytes 786464 | tf_op jit(solution)/shard_map/all_to_all | solution.py:157
  45.3 8.4 %all-to-all-start.2 = ((bf16[32,48,128]{2,1,0:T(8,128)(2,1)}), bf16[32,48,128]{2,1,0:T(8,128)(2,1)}, u32[]{:S(2)}, u32[]{:S(2)}) async-start(bf16[32,48,128]{2,1,0:T(8,128)(2,1)} %broadcast_in_dim.23), calls=%async_computation.2 | async-start | bytes 786432 | tf_op jit(solution)/shard_map/all_to_all | solution.py:157
  66.4 10.8 %collective-permute-done.5.refs_2_ = bf16[1,1,240,1536]{3,2,1,0:T(8,128)(2,1)S(1)} collective-permute-done((bf16[1,1,240,1536]{3,2,1,0:T(8,128)(2,1)}, bf16[1,1,240,1536]{3,2,1,0:T(8,128)(2,1)S(1)}, u32[]{:S(2)}, u32[]{:S(2)}) %collective-permute-start.5) | collective-permute-done | bytes 737312 | tf_op jit(solution)/shard_map/ppermute | solution.py:67
  77.2 4.5 collective-permute-done.4.refs_0_
  93.5 7.3 %collective-permute-done.8.refs_2_ = bf16[1,1,240,1536]{3,2,1,0:T(8,128)(2,1)S(1)} collective-permute-done((bf16[1,1,240,1536]{3,2,1,0:T(8,128)(2,1)}, bf16[1,1,240,1536]{3,2,1,0:T(8,128)(2,1)S(1)}, u32[]{:S(2)}, u32[]{:S(2)}) %collective-permute-start.8) | collective-permute-done | bytes 737312 | tf_op jit(solution)/shard_map/ppermute | solution.py:67
  100.7 3.9 collective-permute-done.7.refs_0_
  108.6 11.4 %collective-permute-done.12.refs_2_ = bf16[1,1,240,1536]{3,2,1,0:T(8,128)(2,1)S(1)} collective-permute-done((bf16[1,1,240,1536]{3,2,1,0:T(8,128)(2,1)}, bf16[1,1,240,1536]{3,2,1,0:T(8,128)(2,1)S(1)}, u32[]{:S(2)}, u32[]{:S(2)}) %collective-permute-start.12) | collective-permute-done | bytes 737312 | tf_op jit(solution)/shard_map/ppermute | solution.py:67
  120.0 4.4 arrange.3
  124.5 3.6 collective-permute-done.10.refs_0_
  130.8 6.5 %fusion.10.refs_2_ = bf16[1024,768]{1,0:T(8,128)(2,1)} fusion(bf16[1024,1536]{1,0:T(8,128)(2,1)} %copy-done.44, bf16[1536,1536]{1,0:T(8,128)(2,1)} %get-tuple-element.69), kind=kOutput, calls=%fused_computation.29 | convolution fusion | flops 2416705536 | bytes 7077888 | tf_op jit(solution)/shard_map/dot_general | solution.py:39
  137.3 4.3 fusion.3.v_ref.gate_ref
  141.6 5.5 collective-permute-done.17.refs_3_
  151.8 9.1 %attend.1 = (bf16[1024,384]{1,0:T(8,128)(2,1)S(1)}, f32[1024,384]{1,0:T(8,128)S(1)}, f32[1024,128]{1,0:T(8,128)S(1)}) custom-call(bf16[1024,768]{1,0:T(8,128)(2,1)S(1)} %copy-done, bf16[1024,768]{1,0:T(8,128)(2,1)S(1)} %copy-done, f32[1024,768]{1,0:T(8,128)} %fusion.3.v_ref.gate_ref, f32[1024,768]{1,0:T(8,128)} %fusion.3.v_ref.gate_ref, ...), custom_call_target="tpu_custom_call" | custom-call | flops 402653184 | bytes 5505024 | tf_op jit(solution)/shard_map/attend/pallas_call | solution.py:345
  162.9 3.4 collective-permute-done.21
  169.5 17.8 %collective-permute-done.22 = bf16[256,1536]{1,0:T(8,128)(2,1)S(1)} collective-permute-done((bf16[256,1536]{1,0:T(8,128)(2,1)S(1)}, bf16[256,1536]{1,0:T(8,128)(2,1)S(1)}, u32[]{:S(2)}, u32[]{:S(2)}) %collective-permute-start.22) | collective-permute-done | bytes 786464 | tf_op jit(solution)/shard_map/ppermute | solution.py:67
  190.8 9.6 %collective-permute-done.31.refs_2_ = bf16[1,1,128,1536]{3,2,1,0:T(8,128)(2,1)S(1)} collective-permute-done((bf16[1,1,128,1536]{3,2,1,0:T(8,128)(2,1)S(1)}, bf16[1,1,128,1536]{3,2,1,0:T(8,128)(2,1)S(1)}, u32[]{:S(2)}, u32[]{:S(2)}) %collective-permute-start.31) | collective-permute-done | bytes 393248 | tf_op jit(solution)/shard_map/ppermute | solution.py:63
  200.4 3.8 collective-permute-done.29.refs_4_
  205.6 6.3 %collective-permute-done.33 = bf16[1,1,128,1536]{3,2,1,0:T(8,128)(2,1)} collective-permute-done((bf16[1,1,128,1536]{3,2,1,0:T(8,128)(2,1)}, bf16[1,1,128,1536]{3,2,1,0:T(8,128)(2,1)}, u32[]{:S(2)}, u32[]{:S(2)}) %collective-permute-start.33) | collective-permute-done | bytes 393248 | tf_op jit(solution)/shard_map/ppermute | solution.py:67
  222.9 18.1 %collective-permute-done.34 = bf16[1,1,128,1536]{3,2,1,0:T(8,128)(2,1)S(1)} collective-permute-done((bf16[1,1,128,1536]{3,2,1,0:T(8,128)(2,1)S(1)}, bf16[1,1,128,1536]{3,2,1,0:T(8,128)(2,1)S(1)}, u32[]{:S(2)}, u32[]{:S(2)}) %collective-permute-start.34) | collective-permute-done | bytes 393248 | tf_op jit(solution)/shard_map/ppermute | solution.py:67
  241.0 6.7 %collective-permute-done.35 = bf16[1,1,128,1536]{3,2,1,0:T(8,128)(2,1)S(1)} collective-permute-done((bf16[1,1,128,1536]{3,2,1,0:T(8,128)(2,1)S(1)}, bf16[1,1,128,1536]{3,2,1,0:T(8,128)(2,1)S(1)}, u32[]{:S(2)}, u32[]{:S(2)}) %collective-permute-start.35) | collective-permute-done | bytes 393248 | tf_op jit(solution)/shard_map/ppermute | solution.py:67
  247.8 3.7 arrange.5.down_ref
  251.6 4.4 arrange.4.both_ref
  256.0 3.2 pad_maximum_fusion.1.hidden_ref
  259.2 28.4 %feed_forward.1 = (bf16[1024,1024]{1,0:T(8,128)(2,1)S(1)}, bf16[1024,2048]{1,0:T(8,128)(2,1)}, bf16[1024,1536]{1,0:T(8,128)(2,1)S(1)}) custom-call(bf16[1024,1536]{1,0:T(8,128)(2,1)} %pad_maximum_fusion.1.hidden_ref, bf16[1024,1536]{1,0:T(8,128)(2,1)} %constant_dynamic-update-slice_fusion.out_grad_ref, bf16[1536,2048]{1,0:T(8,128)(2,1)} %arrange.4.both_ref, ...), custom_call_target="tpu_custom_call" | custom-call | flops 16106127360 | bytes 25165824 | tf_op jit(solution)/shard_map/feed_forward/pallas_call | solution.py:415
  289.5 3.8 convolution_convert_fusion.4
  296.9 4.8 convolution_convert_fusion.3.refs_2_
  301.7 2.5 collective-permute-done.36
  308.7 9.8 %convolution_convert_fusion.1 = bf16[1536,2048]{1,0:T(8,128)(2,1)S(1)} fusion(bf16[1024,2048]{1,0:T(8,128)(2,1)} %get-tuple-element.81, bf16[256,1536]{1,0:T(8,128)(2,1)} %collective-permute-done.25, bf16[256,1536]{1,0:T(8,128)(2,1)} %collective-permute-done.24, bf16[256,1536]{1,0:T(8,128)(2,1)} %collective-permute-done.23, ...), kind=kOutput, calls=%fused_computation.3 | convolution fusion | flops 6458179584 | bytes 13631488 | tf_op jit(solution)/shard_map/dot_general | solution.py:49
  318.5 2.5 constant_dynamic-slice_fusion.5
  321.6 4.1 collective-permute-done.39
  326.3 3.1 fusion.47
  329.5 8.6 %collective-permute-done.38 = bf16[1,1,192,2048]{3,2,1,0:T(8,128)(2,1)S(1)} collective-permute-done((bf16[1,1,192,2048]{3,2,1,0:T(8,128)(2,1)S(1)}, bf16[1,1,192,2048]{3,2,1,0:T(8,128)(2,1)S(1)}, u32[]{:S(2)}, u32[]{:S(2)}) %collective-permute-start.38) | collective-permute-done | bytes 786464 | tf_op jit(solution)/shard_map/ppermute | solution.py:67
  339.3 2.9 slice.102
  343.7 4.2 all-to-all-start.6
  347.9 14.4 %collective-permute-done.42.refs_2_ = bf16[256,1536]{1,0:T(8,128)(2,1)S(1)} collective-permute-done((bf16[256,1536]{1,0:T(8,128)(2,1)S(1)}, bf16[256,1536]{1,0:T(8,128)(2,1)S(1)}, u32[]{:S(2)}, u32[]{:S(2)}) %collective-permute-start.42) | collective-permute-done | bytes 786464 | tf_op jit(solution)/shard_map/ppermute | solution.py:67
  371.6 4.4 fusion.35.refs_0_
  376.0 16.0 %collective-permute-done.45.refs_1_ = bf16[1,1,128,1536]{3,2,1,0:T(8,128)(2,1)} collective-permute-done((bf16[1,1,128,1536]{3,2,1,0:T(8,128)(2,1)}, bf16[1,1,128,1536]{3,2,1,0:T(8,128)(2,1)}, u32[]{:S(2)}, u32[]{:S(2)}) %collective-permute-start.45) | collective-permute-done | bytes 393248 | tf_op jit(solution)/shard_map/ppermute | solution.py:63
  393.5 19.0 %attend_back.1 = (bf16[1024,384]{1,0:T(8,128)(2,1)S(1)}, bf16[1024,384]{1,0:T(8,128)(2,1)S(1)}, bf16[1024,384]{1,0:T(8,128)(2,1)S(1)}, bf16[1024,384]{1,0:T(8,128)(2,1)S(1)}, bf16[1024,128]{1,0:T(8,128)(2,1)S(1)}) custom-call(bf16[1024,768]{1,0:T(8,128)(2,1)} %get-tuple-element.70.q_ref.k_ref, bf16[1024,768]{1,0:T(8,128)(2,1)} %get-tuple-element.70.q_ref.k_ref, ...), custom_call_target="tpu_custom_call" | custom-call | flops 1006632960 | bytes 11010048 | tf_op jit(solution)/shard_map/attend_back/pallas_call | solution.py:367
  412.5 3.7 fusion.36
  419.9 2.6 fusion.22.refs_1_
  428.4 7.2 %convolution_convert_fusion = bf16[1536,1536]{1,0:T(8,128)(2,1)S(1)} fusion(bf16[1024,1536]{1,0:T(8,128)(2,1)S(1)} %copy-done.47, bf16[1024,1536]{1,0:T(8,128)(2,1)} %constant_dynamic-update-slice_fusion.4), kind=kOutput, calls=%fused_computation.2 | convolution fusion | flops 4834197504 | bytes 11010048 | tf_op jit(solution)/shard_map/dot_general | solution.py:49
  438.3 3.6 convolution_convert_fusion.5
  444.1 6.5 %add_convert_fusion = bf16[1024,1536]{1,0:T(8,128)(2,1)} fusion(f32[1024,1536]{1,0:T(8,128)S(1)} %bitcast.179, bf16[1024,1536]{1,0:T(8,128)(2,1)S(1)} %copy-done.80, bf16[1536,1536]{1,0:T(8,128)(2,1)S(1)} %bitcast.211), kind=kOutput, calls=%fused_computation.7 | convolution fusion | flops 4834983936 | bytes 17301504 | tf_op jit(solution)/shard_map/dot_general | solution.py:43
  451.6 4.2 all-to-all-start.5
  474.8 11.3 %collective-permute-done.60 = bf16[1,1,192,2048]{3,2,1,0:T(8,128)(2,1)S(1)} collective-permute-done((bf16[1,1,192,2048]{3,2,1,0:T(8,128)(2,1)S(1)}, bf16[1,1,192,2048]{3,2,1,0:T(8,128)(2,1)S(1)}, u32[]{:S(2)}, u32[]{:S(2)}) %collective-permute-start.60) | collective-permute-done | bytes 786464 | tf_op jit(solution)/shard_map/ppermute | solution.py:67
  489.5 3.4 collective-permute-start.62
  495.9 12.9 %collective-permute-done.53 = bf16[1,1,240,1536]{3,2,1,0:T(8,128)(2,1)S(1)} collective-permute-done((bf16[1,1,240,1536]{3,2,1,0:T(8,128)(2,1)S(1)}, bf16[1,1,240,1536]{3,2,1,0:T(8,128)(2,1)S(1)}, u32[]{:S(2)}, u32[]{:S(2)}) %collective-permute-start.53) | collective-permute-done | bytes 737312 | tf_op jit(solution)/shard_map/ppermute | solution.py:63
  512.0 11.7 %collective-permute-done.62 = bf16[1,1,192,2048]{3,2,1,0:T(8,128)(2,1)S(1)} collective-permute-done((bf16[1,1,192,2048]{3,2,1,0:T(8,128)(2,1)S(1)}, bf16[1,1,192,2048]{3,2,1,0:T(8,128)(2,1)S(1)}, u32[]{:S(2)}, u32[]{:S(2)}) %collective-permute-start.62) | collective-permute-done | bytes 786464 | tf_op jit(solution)/shard_map/ppermute | solution.py:63
  526.5 3.5 all-to-all-start.7
  530.1 3.4 collective-permute-start.66
  538.5 5.1 collective-permute-done.50
  544.7 2.5 add_convert_fusion.2
  547.9 4.7 collective-permute-done.66
  555.6 2.4 unpack_units.1
  561.9 4.7 all-to-all-start.3
  569.8 3.9 all-to-all-done.3
  573.7 3.5 all-to-all-start.4
  577.2 3.3 fusion.16
  581.9 5.2 all-to-all-done.4.ref
  (409 shorter events, 159.3 us)
Async XLA Ops:
  2.6 13.9 %all-to-all-start = ((bf16[4,48,1536]{2,1,0:T(8,128)(2,1)}), bf16[4,48,1536]{2,1,0:T(8,128)(2,1)S(1)}, u32[]{:S(2)}, u32[]{:S(2)}) async-start(bf16[4,48,1536]{2,1,0:T(8,128)(2,1)} %pack_heads.1), calls=%async_computation | async-start | bytes 1179648 | tf_op jit(solution)/shard_map/all_to_all | solution.py:157
  17.5 36.3 %collective-permute-start.2 = (bf16[1,1,240,1536]{3,2,1,0:T(8,128)(2,1)S(1)}, bf16[1,1,240,1536]{3,2,1,0:T(8,128)(2,1)S(1)}, u32[]{:S(2)}, u32[]{:S(2)}) collective-permute-start(bf16[1,1,240,1536]{3,2,1,0:T(8,128)(2,1)S(1)} %get-tuple-element.148), channel_id=1, source_target_pairs={{0,4},{4,0},{1,5},{5,1},{2,6},{6,2},{3,7},{7,3},{8,12},{12,8},{9,1... | collective-permute-start | bytes 2211848 | tf_op jit(solution)/shard_map/ppermute | solution.py:67
  19.7 34.1 %collective-permute-start.1 = (bf16[1,1,240,1536]{3,2,1,0:T(8,128)(2,1)S(1)}, bf16[1,1,240,1536]{3,2,1,0:T(8,128)(2,1)S(1)}, u32[]{:S(2)}, u32[]{:S(2)}) collective-permute-start(bf16[1,1,240,1536]{3,2,1,0:T(8,128)(2,1)S(1)} %get-tuple-element.148), channel_id=1, source_target_pairs={{0,8},{8,24},{24,16},{16,0},{1,9},{9,25},{25,17},{17,1},{2,10},{10... | collective-permute-start | bytes 2211848 | tf_op jit(solution)/shard_map/ppermute | solution.py:63
  26.5 17.9 %all-to-all-start.1 = ((bf16[4,48,2048]{2,1,0:T(8,128)(2,1)}), bf16[4,48,2048]{2,1,0:T(8,128)(2,1)S(1)}, u32[]{:S(2)}, u32[]{:S(2)}) async-start(bf16[4,48,2048]{2,1,0:T(8,128)(2,1)} %pack_units.1), calls=%async_computation.1 | async-start | bytes 1572864 | tf_op jit(solution)/shard_map/all_to_all | solution.py:157
  30.2 28.0 %collective-permute-start.6 = (bf16[256,1536]{1,0:T(8,128)(2,1)}, bf16[256,1536]{1,0:T(8,128)(2,1)}, u32[]{:S(2)}, u32[]{:S(2)}) collective-permute-start(bf16[256,1536]{1,0:T(8,128)(2,1)} %param.15), channel_id=1, source_target_pairs={{0,1},{1,0},{2,3},{3,2},{4,5},{5,4},{6,7},{7,6},{8,9},{9,8},{10,11... | collective-permute-start | bytes 2359304 | tf_op jit(solution)/shard_map/ppermute | solution.py:67
  30.2 23.5 %collective-permute-start.3 = (bf16[1,1,128,1536]{3,2,1,0:T(8,128)(2,1)}, bf16[1,1,128,1536]{3,2,1,0:T(8,128)(2,1)S(1)}, u32[]{:S(2)}, u32[]{:S(2)}) collective-permute-start(bf16[1,1,128,1536]{3,2,1,0:T(8,128)(2,1)} %bitcast.3), channel_id=1, source_target_pairs={{0,8},{8,24},{24,16},{16,0},{1,9},{9,25},{25,17},{17,1},{2,10},{10... | collective-permute-start | bytes 1179656 | tf_op jit(solution)/shard_map/ppermute | solution.py:63
  45.3 38.6 %all-to-all-start.2 = ((bf16[32,48,128]{2,1,0:T(8,128)(2,1)}), bf16[32,48,128]{2,1,0:T(8,128)(2,1)}, u32[]{:S(2)}, u32[]{:S(2)}) async-start(bf16[32,48,128]{2,1,0:T(8,128)(2,1)} %broadcast_in_dim.23), calls=%async_computation.2 | async-start | bytes 786432 | tf_op jit(solution)/shard_map/all_to_all | solution.py:157
  55.0 22.2 %collective-permute-start.5 = (bf16[1,1,240,1536]{3,2,1,0:T(8,128)(2,1)}, bf16[1,1,240,1536]{3,2,1,0:T(8,128)(2,1)S(1)}, u32[]{:S(2)}, u32[]{:S(2)}) collective-permute-start(bf16[1,1,240,1536]{3,2,1,0:T(8,128)(2,1)} %get-tuple-element.61), channel_id=1, source_target_pairs={{0,4},{4,0},{1,5},{5,1},{2,6},{6,2},{3,7},{7,3},{8,12},{12,8},{9,1... | collective-permute-start | bytes 2211848 | tf_op jit(solution)/shard_map/ppermute | solution.py:67
  56.7 24.9 %collective-permute-start.4 = (bf16[1,1,240,1536]{3,2,1,0:T(8,128)(2,1)}, bf16[1,1,240,1536]{3,2,1,0:T(8,128)(2,1)S(1)}, u32[]{:S(2)}, u32[]{:S(2)}) collective-permute-start(bf16[1,1,240,1536]{3,2,1,0:T(8,128)(2,1)} %get-tuple-element.61), channel_id=1, source_target_pairs={{0,8},{8,24},{24,16},{16,0},{1,9},{9,25},{25,17},{17,1},{2,10},{10... | collective-permute-start | bytes 2211848 | tf_op jit(solution)/shard_map/ppermute | solution.py:63
  58.2 29.5 %collective-permute-start.15 = (bf16[256,1536]{1,0:T(8,128)(2,1)}, bf16[256,1536]{1,0:T(8,128)(2,1)}, u32[]{:S(2)}, u32[]{:S(2)}) collective-permute-start(bf16[256,1536]{1,0:T(8,128)(2,1)} %param.15), channel_id=1, source_target_pairs={{0,2},{2,0},{1,3},{3,1},{4,6},{6,4},{5,7},{7,5},{8,10},{10,8},{9,1... | collective-permute-start | bytes 2359304 | tf_op jit(solution)/shard_map/ppermute | solution.py:67
  58.2 29.5 %collective-permute-start.16 = (bf16[256,1536]{1,0:T(8,128)(2,1)}, bf16[256,1536]{1,0:T(8,128)(2,1)}, u32[]{:S(2)}, u32[]{:S(2)}) collective-permute-start(bf16[256,1536]{1,0:T(8,128)(2,1)} %collective-permute-done.6.refs_3_), channel_id=1, source_target_pairs={{0,2},{2,0},{1,3},{3,1},{4,6},{6,4},{5,7},{7,5},{8,10},{10,8},{9,1... | collective-permute-start | bytes 2359304 | tf_op jit(solution)/shard_map/ppermute | solution.py:67
  64.8 28.6 %collective-permute-start.9 = (bf16[1,1,192,2048]{3,2,1,0:T(8,128)(2,1)}, bf16[1,1,192,2048]{3,2,1,0:T(8,128)(2,1)S(1)}, u32[]{:S(2)}, u32[]{:S(2)}) collective-permute-start(bf16[1,1,192,2048]{3,2,1,0:T(8,128)(2,1)} %get-tuple-element.63.refs_1_), channel_id=1, source_target_pairs={{0,1},{1,0},{2,3},{3,2},{4,5},{5,4},{6,7},{7,6},{8,9},{9,8},{10,11... | collective-permute-start | bytes 2359304 | tf_op jit(solution)/shard_map/ppermute | solution.py:67
  82.5 18.2 %collective-permute-start.8 = (bf16[1,1,240,1536]{3,2,1,0:T(8,128)(2,1)}, bf16[1,1,240,1536]{3,2,1,0:T(8,128)(2,1)S(1)}, u32[]{:S(2)}, u32[]{:S(2)}) collective-permute-start(bf16[1,1,240,1536]{3,2,1,0:T(8,128)(2,1)} %get-tuple-element.62), channel_id=1, source_target_pairs={{0,4},{4,0},{1,5},{5,1},{2,6},{6,2},{3,7},{7,3},{8,12},{12,8},{9,1... | collective-permute-start | bytes 2211848 | tf_op jit(solution)/shard_map/ppermute | solution.py:67
  84.0 20.6 %collective-permute-start.7 = (bf16[1,1,240,1536]{3,2,1,0:T(8,128)(2,1)}, bf16[1,1,240,1536]{3,2,1,0:T(8,128)(2,1)}, u32[]{:S(2)}, u32[]{:S(2)}) collective-permute-start(bf16[1,1,240,1536]{3,2,1,0:T(8,128)(2,1)} %get-tuple-element.62), channel_id=1, source_target_pairs={{0,8},{8,24},{24,16},{16,0},{1,9},{9,25},{25,17},{17,1},{2,10},{10... | collective-permute-start | bytes 2211848 | tf_op jit(solution)/shard_map/ppermute | solution.py:63
  89.9 34.6 %collective-permute-start.13 = (bf16[1,1,128,1536]{3,2,1,0:T(8,128)(2,1)S(1)}, bf16[1,1,128,1536]{3,2,1,0:T(8,128)(2,1)}, u32[]{:S(2)}, u32[]{:S(2)}) collective-permute-start(bf16[1,1,128,1536]{3,2,1,0:T(8,128)(2,1)S(1)} %copy-done.7), channel_id=1, source_target_pairs={{0,1},{1,0},{2,3},{3,2},{4,5},{5,4},{6,7},{7,6},{8,9},{9,8},{10,11... | collective-permute-start | bytes 1179656 | tf_op jit(solution)/shard_map/ppermute | solution.py:67
  91.5 33.0 %collective-permute-start.11 = (bf16[1,1,128,1536]{3,2,1,0:T(8,128)(2,1)S(1)}, bf16[1,1,128,1536]{3,2,1,0:T(8,128)(2,1)S(1)}, u32[]{:S(2)}, u32[]{:S(2)}) collective-permute-start(bf16[1,1,128,1536]{3,2,1,0:T(8,128)(2,1)S(1)} %copy-done.7), channel_id=1, source_target_pairs={{0,8},{8,24},{24,16},{16,0},{1,9},{9,25},{25,17},{17,1},{2,10},{10... | collective-permute-start | bytes 1179656 | tf_op jit(solution)/shard_map/ppermute | solution.py:63
  104.6 15.4 %collective-permute-start.12 = (bf16[1,1,240,1536]{3,2,1,0:T(8,128)(2,1)}, bf16[1,1,240,1536]{3,2,1,0:T(8,128)(2,1)S(1)}, u32[]{:S(2)}, u32[]{:S(2)}) collective-permute-start(bf16[1,1,240,1536]{3,2,1,0:T(8,128)(2,1)} %get-tuple-element.66), channel_id=1, source_target_pairs={{0,4},{4,0},{1,5},{5,1},{2,6},{6,2},{3,7},{7,3},{8,12},{12,8},{9,1... | collective-permute-start | bytes 2211848 | tf_op jit(solution)/shard_map/ppermute | solution.py:67
  105.2 22.9 %collective-permute-start.10 = (bf16[1,1,192,2048]{3,2,1,0:T(8,128)(2,1)}, bf16[1,1,192,2048]{3,2,1,0:T(8,128)(2,1)S(1)}, u32[]{:S(2)}, u32[]{:S(2)}) collective-permute-start(bf16[1,1,192,2048]{3,2,1,0:T(8,128)(2,1)} %get-tuple-element.64), channel_id=1, source_target_pairs={{0,8},{8,24},{24,16},{16,0},{1,9},{9,25},{25,17},{17,1},{2,10},{10... | collective-permute-start | bytes 2359304 | tf_op jit(solution)/shard_map/ppermute | solution.py:63
  129.0 18.1 %collective-permute-start.17 = (bf16[1,1,192,2048]{3,2,1,0:T(8,128)(2,1)}, bf16[1,1,192,2048]{3,2,1,0:T(8,128)(2,1)S(1)}, u32[]{:S(2)}, u32[]{:S(2)}) collective-permute-start(bf16[1,1,192,2048]{3,2,1,0:T(8,128)(2,1)} %get-tuple-element.67), channel_id=1, source_target_pairs={{0,1},{1,0},{2,3},{3,2},{4,5},{5,4},{6,7},{7,6},{8,9},{9,8},{10,11... | collective-permute-start | bytes 2359304 | tf_op jit(solution)/shard_map/ppermute | solution.py:67
  130.5 19.0 %collective-permute-start.14 = (bf16[1,1,192,2048]{3,2,1,0:T(8,128)(2,1)}, bf16[1,1,192,2048]{3,2,1,0:T(8,128)(2,1)S(1)}, u32[]{:S(2)}, u32[]{:S(2)}) collective-permute-start(bf16[1,1,192,2048]{3,2,1,0:T(8,128)(2,1)} %get-tuple-element.67), channel_id=1, source_target_pairs={{0,8},{8,24},{24,16},{16,0},{1,9},{9,25},{25,17},{17,1},{2,10},{10... | collective-permute-start | bytes 2359304 | tf_op jit(solution)/shard_map/ppermute | solution.py:63
  166.9 20.4 %collective-permute-start.22 = (bf16[256,1536]{1,0:T(8,128)(2,1)S(1)}, bf16[256,1536]{1,0:T(8,128)(2,1)S(1)}, u32[]{:S(2)}, u32[]{:S(2)}) collective-permute-start(bf16[256,1536]{1,0:T(8,128)(2,1)S(1)} %slice.180), channel_id=1, source_target_pairs={{0,1},{1,0},{2,3},{3,2},{4,5},{5,4},{6,7},{7,6},{8,9},{9,8},{10,11... | collective-permute-start | bytes 2359304 | tf_op jit(solution)/shard_map/ppermute | solution.py:67
  167.5 22.7 %collective-permute-start.26 = (bf16[256,1536]{1,0:T(8,128)(2,1)}, bf16[256,1536]{1,0:T(8,128)(2,1)}, u32[]{:S(2)}, u32[]{:S(2)}) collective-permute-start(bf16[256,1536]{1,0:T(8,128)(2,1)} %param.29), channel_id=1, source_target_pairs={{0,4},{4,0},{1,5},{5,1},{2,6},{6,2},{3,7},{7,3},{8,12},{12,8},{9,1... | collective-permute-start | bytes 2359304 | tf_op jit(solution)/shard_map/ppermute | solution.py:67
  168.0 36.1 %collective-permute-start.29 = (bf16[1,1,192,2048]{3,2,1,0:T(8,128)(2,1)S(1)}, bf16[1,1,192,2048]{3,2,1,0:T(8,128)(2,1)S(1)}, u32[]{:S(2)}, u32[]{:S(2)}) collective-permute-start(bf16[1,1,192,2048]{3,2,1,0:T(8,128)(2,1)S(1)} %copy-done.11), channel_id=1, source_target_pairs={{0,1},{1,0},{2,3},{3,2},{4,5},{5,4},{6,7},{7,6},{8,9},{9,8},{10,11... | collective-permute-start | bytes 2359304 | tf_op jit(solution)/shard_map/ppermute | solution.py:67
  169.5 34.7 %collective-permute-start.30 = (bf16[1,1,192,2048]{3,2,1,0:T(8,128)(2,1)S(1)}, bf16[1,1,192,2048]{3,2,1,0:T(8,128)(2,1)S(1)}, u32[]{:S(2)}, u32[]{:S(2)}) collective-permute-start(bf16[1,1,192,2048]{3,2,1,0:T(8,128)(2,1)S(1)} %copy-done.11), channel_id=1, source_target_pairs={{0,8},{8,24},{24,16},{16,0},{1,9},{9,25},{25,17},{17,1},{2,10},{10... | collective-permute-start | bytes 2359304 | tf_op jit(solution)/shard_map/ppermute | solution.py:63
  189.1 23.4 %collective-permute-start.23 = (bf16[256,1536]{1,0:T(8,128)(2,1)}, bf16[256,1536]{1,0:T(8,128)(2,1)}, u32[]{:S(2)}, u32[]{:S(2)}) collective-permute-start(bf16[256,1536]{1,0:T(8,128)(2,1)} %multiply_convert_fusion.refs_3_), channel_id=1, source_target_pairs={{0,4},{4,0},{1,5},{5,1},{2,6},{6,2},{3,7},{7,3},{8,12},{12,8},{9,1... | collective-permute-start | bytes 2359304 | tf_op jit(solution)/shard_map/ppermute | solution.py:67
  190.2 21.7 %collective-permute-start.33 = (bf16[1,1,128,1536]{3,2,1,0:T(8,128)(2,1)}, bf16[1,1,128,1536]{3,2,1,0:T(8,128)(2,1)}, u32[]{:S(2)}, u32[]{:S(2)}) collective-permute-start(bf16[1,1,128,1536]{3,2,1,0:T(8,128)(2,1)} %bitcast.3), channel_id=1, source_target_pairs={{0,1},{1,0},{2,3},{3,2},{4,5},{5,4},{6,7},{7,6},{8,9},{9,8},{10,11... | collective-permute-start | bytes 1179656 | tf_op jit(solution)/shard_map/ppermute | solution.py:67
  200.4 16.3 %collective-permute-start.27 = (bf16[256,1536]{1,0:T(8,128)(2,1)}, bf16[256,1536]{1,0:T(8,128)(2,1)}, u32[]{:S(2)}, u32[]{:S(2)}) collective-permute-start(bf16[256,1536]{1,0:T(8,128)(2,1)} %param.29), channel_id=1, source_target_pairs={{0,2},{2,0},{1,3},{3,1},{4,6},{6,4},{5,7},{7,5},{8,10},{10,8},{9,1... | collective-permute-start | bytes 2359304 | tf_op jit(solution)/shard_map/ppermute | solution.py:67
  204.2 14.0 %collective-permute-start.28 = (bf16[256,1536]{1,0:T(8,128)(2,1)}, bf16[256,1536]{1,0:T(8,128)(2,1)}, u32[]{:S(2)}, u32[]{:S(2)}) collective-permute-start(bf16[256,1536]{1,0:T(8,128)(2,1)} %collective-permute-done.26), channel_id=1, source_target_pairs={{0,2},{2,0},{1,3},{3,1},{4,6},{6,4},{5,7},{7,5},{8,10},{10,8},{9,1... | collective-permute-start | bytes 2359304 | tf_op jit(solution)/shard_map/ppermute | solution.py:67
  205.1 50.9 %collective-permute-start.24 = (bf16[256,1536]{1,0:T(8,128)(2,1)}, bf16[256,1536]{1,0:T(8,128)(2,1)}, u32[]{:S(2)}, u32[]{:S(2)}) collective-permute-start(bf16[256,1536]{1,0:T(8,128)(2,1)} %multiply_convert_fusion.refs_3_), channel_id=1, source_target_pairs={{0,2},{2,0},{1,3},{3,1},{4,6},{6,4},{5,7},{7,5},{8,10},{10,8},{9,1... | collective-permute-start | bytes 2359304 | tf_op jit(solution)/shard_map/ppermute | solution.py:67
  211.9 39.6 %collective-permute-start.32 = (bf16[1,1,192,2048]{3,2,1,0:T(8,128)(2,1)}, bf16[1,1,192,2048]{3,2,1,0:T(8,128)(2,1)}, u32[]{:S(2)}, u32[]{:S(2)}) collective-permute-start(bf16[1,1,192,2048]{3,2,1,0:T(8,128)(2,1)} %get-tuple-element.75), channel_id=1, source_target_pairs={{0,1},{1,0},{2,3},{3,2},{4,5},{5,4},{6,7},{7,6},{8,9},{9,8},{10,11... | collective-permute-start | bytes 2359304 | tf_op jit(solution)/shard_map/ppermute | solution.py:67
  212.5 43.5 %collective-permute-start.25 = (bf16[256,1536]{1,0:T(8,128)(2,1)}, bf16[256,1536]{1,0:T(8,128)(2,1)}, u32[]{:S(2)}, u32[]{:S(2)}) collective-permute-start(bf16[256,1536]{1,0:T(8,128)(2,1)} %collective-permute-done.23), channel_id=1, source_target_pairs={{0,2},{2,0},{1,3},{3,1},{4,6},{6,4},{5,7},{7,5},{8,10},{10,8},{9,1... | collective-permute-start | bytes 2359304 | tf_op jit(solution)/shard_map/ppermute | solution.py:67
  216.7 24.3 %collective-permute-start.34 = (bf16[1,1,128,1536]{3,2,1,0:T(8,128)(2,1)S(1)}, bf16[1,1,128,1536]{3,2,1,0:T(8,128)(2,1)S(1)}, u32[]{:S(2)}, u32[]{:S(2)}) collective-permute-start(bf16[1,1,128,1536]{3,2,1,0:T(8,128)(2,1)S(1)} %copy-done.5), channel_id=1, source_target_pairs={{0,1},{1,0},{2,3},{3,2},{4,5},{5,4},{6,7},{7,6},{8,9},{9,8},{10,11... | collective-permute-start | bytes 1179656 | tf_op jit(solution)/shard_map/ppermute | solution.py:67
  218.2 29.5 %collective-permute-start.35 = (bf16[1,1,128,1536]{3,2,1,0:T(8,128)(2,1)S(1)}, bf16[1,1,128,1536]{3,2,1,0:T(8,128)(2,1)S(1)}, u32[]{:S(2)}, u32[]{:S(2)}) collective-permute-start(bf16[1,1,128,1536]{3,2,1,0:T(8,128)(2,1)S(1)} %copy-done.34), channel_id=1, source_target_pairs={{0,1},{1,0},{2,3},{3,2},{4,5},{5,4},{6,7},{7,6},{8,9},{9,8},{10,11... | collective-permute-start | bytes 1179656 | tf_op jit(solution)/shard_map/ppermute | solution.py:67
  287.7 17.3 %collective-permute-start.37 = (bf16[512,1536]{1,0:T(8,128)(2,1)S(1)}, bf16[512,1536]{1,0:T(8,128)(2,1)S(1)}, u32[]{:S(2)}, u32[]{:S(2)}) collective-permute-start(bf16[512,1536]{1,0:T(8,128)(2,1)S(1)} %slice.98), channel_id=1, source_target_pairs={{0,2},{2,0},{1,3},{3,1},{4,6},{6,4},{5,7},{7,5},{8,10},{10,8},{9,1... | collective-permute-start | bytes 4718600 | tf_op jit(solution)/shard_map/ppermute | solution.py:67
  308.2 17.5 %collective-permute-start.39 = (bf16[256,1536]{1,0:T(8,128)(2,1)}, bf16[256,1536]{1,0:T(8,128)(2,1)S(1)}, u32[]{:S(2)}, u32[]{:S(2)}) collective-permute-start(bf16[256,1536]{1,0:T(8,128)(2,1)} %get-tuple-element.82), channel_id=1, source_target_pairs={{0,4},{4,0},{1,5},{5,1},{2,6},{6,2},{3,7},{7,3},{8,12},{12,8},{9,1... | collective-permute-start | bytes 2359304 | tf_op jit(solution)/shard_map/ppermute | solution.py:67
  321.0 17.1 %collective-permute-start.38 = (bf16[1,1,192,2048]{3,2,1,0:T(8,128)(2,1)S(1)}, bf16[1,1,192,2048]{3,2,1,0:T(8,128)(2,1)S(1)}, u32[]{:S(2)}, u32[]{:S(2)}) collective-permute-start(bf16[1,1,192,2048]{3,2,1,0:T(8,128)(2,1)S(1)} %bitcast.199), channel_id=1, source_target_pairs={{0,1},{1,0},{2,3},{3,2},{4,5},{5,4},{6,7},{7,6},{8,9},{9,8},{10,11... | collective-permute-start | bytes 2359304 | tf_op jit(solution)/shard_map/ppermute | solution.py:67
  342.2 21.6 %collective-permute-start.40 = (bf16[512,1536]{1,0:T(8,128)(2,1)}, bf16[512,1536]{1,0:T(8,128)(2,1)}, u32[]{:S(2)}, u32[]{:S(2)}) collective-permute-start(bf16[512,1536]{1,0:T(8,128)(2,1)} %slice.102), channel_id=1, source_target_pairs={{0,2},{2,0},{1,3},{3,1},{4,6},{6,4},{5,7},{7,5},{8,10},{10,8},{9,1... | collective-permute-start | bytes 4718600 | tf_op jit(solution)/shard_map/ppermute | solution.py:67
  342.2 20.1 %collective-permute-start.42 = (bf16[256,1536]{1,0:T(8,128)(2,1)S(1)}, bf16[256,1536]{1,0:T(8,128)(2,1)S(1)}, u32[]{:S(2)}, u32[]{:S(2)}) collective-permute-start(bf16[256,1536]{1,0:T(8,128)(2,1)S(1)} %copy-done.58), channel_id=1, source_target_pairs={{0,1},{1,0},{2,3},{3,2},{4,5},{5,4},{6,7},{7,6},{8,9},{9,8},{10,11... | collective-permute-start | bytes 2359304 | tf_op jit(solution)/shard_map/ppermute | solution.py:67
  342.8 26.5 %collective-permute-start.43 = (bf16[256,1536]{1,0:T(8,128)(2,1)S(1)}, bf16[256,1536]{1,0:T(8,128)(2,1)}, u32[]{:S(2)}, u32[]{:S(2)}) collective-permute-start(bf16[256,1536]{1,0:T(8,128)(2,1)S(1)} %copy-done.58), channel_id=1, source_target_pairs={{0,2},{2,0},{1,3},{3,1},{4,6},{6,4},{5,7},{7,5},{8,10},{10,8},{9,1... | collective-permute-start | bytes 2359304 | tf_op jit(solution)/shard_map/ppermute | solution.py:67
  343.7 19.5 %all-to-all-start.6 = ((f32[32,1,48]{2,1,0:T(1,128)}), f32[32,1,48]{2,1,0:T(1,128)S(1)}, u32[]{:S(2)}, u32[]{:S(2)}) async-start(f32[32,1,48]{2,1,0:T(1,128)} %all_to_all.37), calls=%async_computation.6 | async-start | bytes 32768 | tf_op jit(solution)/shard_map/all_to_all | solution.py:157
  362.3 149.1 %collective-permute-start.57 = (bf16[1,1,192,2048]{3,2,1,0:T(8,128)(2,1)}, bf16[1,1,192,2048]{3,2,1,0:T(8,128)(2,1)}, u32[]{:S(2)}, u32[]{:S(2)}) collective-permute-start(bf16[1,1,192,2048]{3,2,1,0:T(8,128)(2,1)} %bitcast.198), channel_id=1, source_target_pairs={{0,1},{1,0},{2,3},{3,2},{4,5},{5,4},{6,7},{7,6},{8,9},{9,8},{10,11... | collective-permute-start | bytes 2359304 | tf_op jit(solution)/shard_map/ppermute | solution.py:67
  362.9 30.5 %collective-permute-start.46 = (bf16[1,1,192,2048]{3,2,1,0:T(8,128)(2,1)S(1)}, bf16[1,1,192,2048]{3,2,1,0:T(8,128)(2,1)}, u32[]{:S(2)}, u32[]{:S(2)}) collective-permute-start(bf16[1,1,192,2048]{3,2,1,0:T(8,128)(2,1)S(1)} %copy-done.63), channel_id=1, source_target_pairs={{0,8},{8,24},{24,16},{16,0},{1,9},{9,25},{25,17},{17,1},{2,10},{10... | collective-permute-start | bytes 2359304 | tf_op jit(solution)/shard_map/ppermute | solution.py:63
  363.8 28.2 %collective-permute-start.45 = (bf16[1,1,128,1536]{3,2,1,0:T(8,128)(2,1)}, bf16[1,1,128,1536]{3,2,1,0:T(8,128)(2,1)}, u32[]{:S(2)}, u32[]{:S(2)}) collective-permute-start(bf16[1,1,128,1536]{3,2,1,0:T(8,128)(2,1)} %get-tuple-element.86), channel_id=1, source_target_pairs={{0,8},{8,24},{24,16},{16,0},{1,9},{9,25},{25,17},{17,1},{2,10},{10... | collective-permute-start | bytes 1179656 | tf_op jit(solution)/shard_map/ppermute | solution.py:63
  369.3 50.6 %collective-permute-start.59 = (bf16[1,1,192,2048]{3,2,1,0:T(8,128)(2,1)}, bf16[1,1,192,2048]{3,2,1,0:T(8,128)(2,1)}, u32[]{:S(2)}, u32[]{:S(2)}) collective-permute-start(bf16[1,1,192,2048]{3,2,1,0:T(8,128)(2,1)} %get-tuple-element.100), channel_id=1, source_target_pairs={{0,1},{1,0},{2,3},{3,2},{4,5},{5,4},{6,7},{7,6},{8,9},{9,8},{10,11... | collective-permute-start | bytes 2359304 | tf_op jit(solution)/shard_map/ppermute | solution.py:67
  370.8 47.0 %collective-permute-start.58 = (bf16[1,1,128,1536]{3,2,1,0:T(8,128)(2,1)}, bf16[1,1,128,1536]{3,2,1,0:T(8,128)(2,1)}, u32[]{:S(2)}, u32[]{:S(2)}) collective-permute-start(bf16[1,1,128,1536]{3,2,1,0:T(8,128)(2,1)} %get-tuple-element.98), channel_id=1, source_target_pairs={{0,1},{1,0},{2,3},{3,2},{4,5},{5,4},{6,7},{7,6},{8,9},{9,8},{10,11... | collective-permute-start | bytes 1179656 | tf_op jit(solution)/shard_map/ppermute | solution.py:67
  392.0 97.5 %collective-permute-start.41 = (bf16[256,1536]{1,0:T(8,128)(2,1)}, bf16[256,1536]{1,0:T(8,128)(2,1)}, u32[]{:S(2)}, u32[]{:S(2)}) collective-permute-start(bf16[256,1536]{1,0:T(8,128)(2,1)} %slice.178), channel_id=1, source_target_pairs={{0,4},{4,0},{1,5},{5,1},{2,6},{6,2},{3,7},{7,3},{8,12},{12,8},{9,1... | collective-permute-start | bytes 2359304 | tf_op jit(solution)/shard_map/ppermute | solution.py:67
  422.6 44.3 %collective-permute-start.64 = (bf16[1,1,128,1536]{3,2,1,0:T(8,128)(2,1)}, bf16[1,1,128,1536]{3,2,1,0:T(8,128)(2,1)}, u32[]{:S(2)}, u32[]{:S(2)}) collective-permute-start(bf16[1,1,128,1536]{3,2,1,0:T(8,128)(2,1)} %get-tuple-element.106), channel_id=1, source_target_pairs={{0,1},{1,0},{2,3},{3,2},{4,5},{5,4},{6,7},{7,6},{8,9},{9,8},{10,11... | collective-permute-start | bytes 1179656 | tf_op jit(solution)/shard_map/ppermute | solution.py:67
  424.1 44.2 %collective-permute-start.65 = (bf16[1,1,128,1536]{3,2,1,0:T(8,128)(2,1)}, bf16[1,1,128,1536]{3,2,1,0:T(8,128)(2,1)}, u32[]{:S(2)}, u32[]{:S(2)}) collective-permute-start(bf16[1,1,128,1536]{3,2,1,0:T(8,128)(2,1)} %get-tuple-element.107), channel_id=1, source_target_pairs={{0,8},{8,24},{24,16},{16,0},{1,9},{9,25},{25,17},{17,1},{2,10},{10... | collective-permute-start | bytes 1179656 | tf_op jit(solution)/shard_map/ppermute | solution.py:63
  443.5 28.3 %collective-permute-start.52 = (bf16[1,1,240,1536]{3,2,1,0:T(8,128)(2,1)}, bf16[1,1,240,1536]{3,2,1,0:T(8,128)(2,1)}, u32[]{:S(2)}, u32[]{:S(2)}) collective-permute-start(bf16[1,1,240,1536]{3,2,1,0:T(8,128)(2,1)} %pad_maximum_fusion.7), channel_id=1, source_target_pairs={{0,4},{4,0},{1,5},{5,1},{2,6},{6,2},{3,7},{7,3},{8,12},{12,8},{9,1... | collective-permute-start | bytes 2211848 | tf_op jit(solution)/shard_map/ppermute | solution.py:67
  466.8 19.3 %collective-permute-start.60 = (bf16[1,1,192,2048]{3,2,1,0:T(8,128)(2,1)S(1)}, bf16[1,1,192,2048]{3,2,1,0:T(8,128)(2,1)S(1)}, u32[]{:S(2)}, u32[]{:S(2)}) collective-permute-start(bf16[1,1,192,2048]{3,2,1,0:T(8,128)(2,1)S(1)} %copy-done.69), channel_id=1, source_target_pairs={{0,1},{1,0},{2,3},{3,2},{4,5},{5,4},{6,7},{7,6},{8,9},{9,8},{10,11... | collective-permute-start | bytes 2359304 | tf_op jit(solution)/shard_map/ppermute | solution.py:67
  468.2 20.3 %collective-permute-start.61 = (bf16[1,1,192,2048]{3,2,1,0:T(8,128)(2,1)S(1)}, bf16[1,1,192,2048]{3,2,1,0:T(8,128)(2,1)S(1)}, u32[]{:S(2)}, u32[]{:S(2)}) collective-permute-start(bf16[1,1,192,2048]{3,2,1,0:T(8,128)(2,1)S(1)} %copy-done.65), channel_id=1, source_target_pairs={{0,8},{8,24},{24,16},{16,0},{1,9},{9,25},{25,17},{17,1},{2,10},{10... | collective-permute-start | bytes 2359304 | tf_op jit(solution)/shard_map/ppermute | solution.py:63
  471.9 23.5 %collective-permute-start.51 = (bf16[1,1,240,1536]{3,2,1,0:T(8,128)(2,1)}, bf16[1,1,240,1536]{3,2,1,0:T(8,128)(2,1)S(1)}, u32[]{:S(2)}, u32[]{:S(2)}) collective-permute-start(bf16[1,1,240,1536]{3,2,1,0:T(8,128)(2,1)} %pad_maximum_fusion.6), channel_id=1, source_target_pairs={{0,4},{4,0},{1,5},{5,1},{2,6},{6,2},{3,7},{7,3},{8,12},{12,8},{9,1... | collective-permute-start | bytes 2211848 | tf_op jit(solution)/shard_map/ppermute | solution.py:67
  486.1 43.9 %collective-permute-start.47 = (bf16[512,1536]{1,0:T(8,128)(2,1)}, bf16[512,1536]{1,0:T(8,128)(2,1)}, u32[]{:S(2)}, u32[]{:S(2)}) collective-permute-start(bf16[512,1536]{1,0:T(8,128)(2,1)} %slice.129), channel_id=1, source_target_pairs={{0,2},{2,0},{1,3},{3,1},{4,6},{6,4},{5,7},{7,5},{8,10},{10,8},{9,1... | collective-permute-start | bytes 4718600 | tf_op jit(solution)/shard_map/ppermute | solution.py:67
  488.5 20.3 %collective-permute-start.53 = (bf16[1,1,240,1536]{3,2,1,0:T(8,128)(2,1)S(1)}, bf16[1,1,240,1536]{3,2,1,0:T(8,128)(2,1)S(1)}, u32[]{:S(2)}, u32[]{:S(2)}) collective-permute-start(bf16[1,1,240,1536]{3,2,1,0:T(8,128)(2,1)S(1)} %add_convert_fusion.4), channel_id=1, source_target_pairs={{0,8},{8,24},{24,16},{16,0},{1,9},{9,25},{25,17},{17,1},{2,10},{10... | collective-permute-start | bytes 2211848 | tf_op jit(solution)/shard_map/ppermute | solution.py:63
  489.5 34.1 %collective-permute-start.62 = (bf16[1,1,192,2048]{3,2,1,0:T(8,128)(2,1)S(1)}, bf16[1,1,192,2048]{3,2,1,0:T(8,128)(2,1)S(1)}, u32[]{:S(2)}, u32[]{:S(2)}) collective-permute-start(bf16[1,1,192,2048]{3,2,1,0:T(8,128)(2,1)S(1)} %fusion.24), channel_id=1, source_target_pairs={{0,8},{8,24},{24,16},{16,0},{1,9},{9,25},{25,17},{17,1},{2,10},{10... | collective-permute-start | bytes 2359304 | tf_op jit(solution)/shard_map/ppermute | solution.py:63
  495.3 52.6 %collective-permute-start.63 = (bf16[1,1,128,1536]{3,2,1,0:T(8,128)(2,1)}, bf16[1,1,128,1536]{3,2,1,0:T(8,128)(2,1)}, u32[]{:S(2)}, u32[]{:S(2)}) collective-permute-start(bf16[1,1,128,1536]{3,2,1,0:T(8,128)(2,1)} %get-tuple-element.134), channel_id=1, source_target_pairs={{0,1},{1,0},{2,3},{3,2},{4,5},{5,4},{6,7},{7,6},{8,9},{9,8},{10,11... | collective-permute-start | bytes 1179656 | tf_op jit(solution)/shard_map/ppermute | solution.py:67
  508.8 57.8 %collective-permute-start.49 = (bf16[1,1,240,1536]{3,2,1,0:T(8,128)(2,1)}, bf16[1,1,240,1536]{3,2,1,0:T(8,128)(2,1)}, u32[]{:S(2)}, u32[]{:S(2)}) collective-permute-start(bf16[1,1,240,1536]{3,2,1,0:T(8,128)(2,1)} %pad_maximum_fusion.4), channel_id=1, source_target_pairs={{0,4},{4,0},{1,5},{5,1},{2,6},{6,2},{3,7},{7,3},{8,12},{12,8},{9,1... | collective-permute-start | bytes 2211848 | tf_op jit(solution)/shard_map/ppermute | solution.py:67
  511.4 32.2 %collective-permute-start.50 = (bf16[1,1,240,1536]{3,2,1,0:T(8,128)(2,1)S(1)}, bf16[1,1,240,1536]{3,2,1,0:T(8,128)(2,1)}, u32[]{:S(2)}, u32[]{:S(2)}) collective-permute-start(bf16[1,1,240,1536]{3,2,1,0:T(8,128)(2,1)S(1)} %copy-done.78), channel_id=1, source_target_pairs={{0,4},{4,0},{1,5},{5,1},{2,6},{6,2},{3,7},{7,3},{8,12},{12,8},{9,1... | collective-permute-start | bytes 2211848 | tf_op jit(solution)/shard_map/ppermute | solution.py:67
  523.6 21.1 %collective-permute-start.54 = (bf16[1,1,240,1536]{3,2,1,0:T(8,128)(2,1)}, bf16[1,1,240,1536]{3,2,1,0:T(8,128)(2,1)}, u32[]{:S(2)}, u32[]{:S(2)}) collective-permute-start(bf16[1,1,240,1536]{3,2,1,0:T(8,128)(2,1)} %add_convert_fusion.3), channel_id=1, source_target_pairs={{0,8},{8,24},{24,16},{16,0},{1,9},{9,25},{25,17},{17,1},{2,10},{10... | collective-permute-start | bytes 2211848 | tf_op jit(solution)/shard_map/ppermute | solution.py:63
  526.5 28.2 %all-to-all-start.7 = ((bf16[4,48,2048]{2,1,0:T(8,128)(2,1)}), bf16[4,48,2048]{2,1,0:T(8,128)(2,1)S(1)}, u32[]{:S(2)}, u32[]{:S(2)}) async-start(bf16[4,48,2048]{2,1,0:T(8,128)(2,1)} %bitcast.78), calls=%async_computation.7 | async-start | bytes 1572864 | tf_op jit(solution)/shard_map/all_to_all | solution.py:157
  530.1 22.5 %collective-permute-start.66 = (bf16[1,1,128,1536]{3,2,1,0:T(8,128)(2,1)}, bf16[1,1,128,1536]{3,2,1,0:T(8,128)(2,1)S(1)}, u32[]{:S(2)}, u32[]{:S(2)}) collective-permute-start(bf16[1,1,128,1536]{3,2,1,0:T(8,128)(2,1)} %fusion.29), channel_id=1, source_target_pairs={{0,8},{8,24},{24,16},{16,0},{1,9},{9,25},{25,17},{17,1},{2,10},{10... | collective-permute-start | bytes 1179656 | tf_op jit(solution)/shard_map/ppermute | solution.py:63
  543.6 14.7 %collective-permute-start.48 = (bf16[256,1536]{1,0:T(8,128)(2,1)}, bf16[256,1536]{1,0:T(8,128)(2,1)S(1)}, u32[]{:S(2)}, u32[]{:S(2)}) collective-permute-start(bf16[256,1536]{1,0:T(8,128)(2,1)} %slice.177), channel_id=1, source_target_pairs={{0,1},{1,0},{2,3},{3,2},{4,5},{5,4},{6,7},{7,6},{8,9},{9,8},{10,11... | collective-permute-start | bytes 2359304 | tf_op jit(solution)/shard_map/ppermute | solution.py:67
  547.2 19.4 %collective-permute-start.55 = (bf16[1,1,240,1536]{3,2,1,0:T(8,128)(2,1)}, bf16[1,1,240,1536]{3,2,1,0:T(8,128)(2,1)}, u32[]{:S(2)}, u32[]{:S(2)}) collective-permute-start(bf16[1,1,240,1536]{3,2,1,0:T(8,128)(2,1)} %add_convert_fusion.2), channel_id=1, source_target_pairs={{0,8},{8,24},{24,16},{16,0},{1,9},{9,25},{25,17},{17,1},{2,10},{10... | collective-permute-start | bytes 2211848 | tf_op jit(solution)/shard_map/ppermute | solution.py:63
  573.7 13.4 %all-to-all-start.4 = ((bf16[4,48,1536]{2,1,0:T(8,128)(2,1)}), bf16[4,48,1536]{2,1,0:T(8,128)(2,1)S(1)}, u32[]{:S(2)}, u32[]{:S(2)}) async-start(bf16[4,48,1536]{2,1,0:T(8,128)(2,1)} %bitcast.63), calls=%async_computation.4 | async-start | bytes 1179648 | tf_op jit(solution)/shard_map/all_to_all | solution.py:157
  (107 other events, 1004.5 us)

commit v2 on v1

v2 whole, which is shorter than its diff:
```python
import math

import jax
import jax.numpy as jnp
from jax import lax
from jax.experimental import pallas as pl
from jax.experimental.pallas import tpu as pltpu
from jax.sharding import Mesh
from jax.sharding import PartitionSpec as P

H = 24
HEAD = 64
Z = 4
GROUP = 4
LANES = 128
TILE = 256
LOCAL_HEADS = H // GROUP

epsilon = 1e-06
negative_big = -1e30
bf16 = jnp.bfloat16
f32 = jnp.float32
ALL = ("z", "w", "y", "c", "r", "x")
REST = ("w", "r")
ANY = pl.BlockSpec(memory_space=pl.ANY)
kernel_params = pltpu.CompilerParams(vmem_limit_bytes=48 * 1024 * 1024)


def row_norm(tokens):
    inverse_rms = lax.rsqrt(jnp.mean(tokens * tokens, -1, keepdims=True) + epsilon)
    return (tokens * inverse_rms, inverse_rms)


def norm_back(grad_hat, normed, inverse_rms):
    return inverse_rms * (grad_hat - normed * jnp.mean(grad_hat * normed, -1, keepdims=True))


def product(left, right):
    return jnp.dot(left, right, preferred_element_type=f32)


def product_nt(left, right, precision=None):
    return lax.dot_general(
        left, right, (((1,), (1,)), ((), ())), preferred_element_type=f32, precision=precision
    )


def product_tn(left, right, precision=None):
    return lax.dot_general(
        left, right, (((0,), (0,)), ((), ())), preferred_element_type=f32, precision=precision
    )


def place_in_ring(index):
    return index ^ (index >> 1)


def found_at(step):
    return place_in_ring((place_in_ring(lax.axis_index("z")) - step) & 3)


def along_z(block):
    return lax.ppermute(block, "z", [(0, 1), (1, 3), (3, 2), (2, 0)])


def swap(value, axis):
    return lax.ppermute(value, axis, [(0, 1), (1, 0)])


def has_rest():
    return lax.axis_size("w") * lax.axis_size("r") > 1


def over_rest(block):
    if not has_rest():
        return block[None, None]
    return lax.all_gather(lax.all_gather(block, "r"), "w")


def sum_over_rest(total):
    if not has_rest():
        return total[0, 0]
    return lax.psum_scatter(lax.psum_scatter(total, "w"), "r")


def order(values, after):
    count = len(values)
    if has_rest():
        return values
    return pl.pallas_call(
        lambda *refs: None,
        in_specs=[ANY] * (count + len(after)),
        out_specs=[ANY] * count,
        out_shape=[jax.ShapeDtypeStruct(value.shape, value.dtype) for value in values],
        input_output_aliases={at: at for at in range(count)},
        name="order",
    )(*values, *after)


def arrange(arrivals, axis, shape, reorder, spots):
    mine = lax.axis_index(axis)
    blocks = [block for _, _, block in arrivals]
    if has_rest():
        whole = jnp.zeros((Z, 2, *blocks[0].shape), blocks[0].dtype)
        for step, other, block in arrivals:
            at = (found_at(step), mine ^ other)
            whole = lax.dynamic_update_slice(whole, block[None, None], (*at, *[0] * block.ndim))
        return reorder(whole)
    blocks = [block.reshape(-1, block.shape[-1]) for block in blocks]
    places = jnp.stack([found_at(step) for step in range(Z)] + [mine, 1 - mine]).astype(jnp.int32)

    def kernel(places_ref, *refs):
        block_refs, outs, sems = refs[: len(blocks)], refs[len(blocks) : -1], refs[-1]
        copies = []
        for at, (step, other, _) in enumerate(arrivals):
            for out, first, rows, spot in spots(outs, places_ref[step], places_ref[Z + other]):
                source = block_refs[at].at[pl.ds(first, rows)]
                copies.append(pltpu.make_async_copy(source, spot, sems.at[len(copies)]))
        for copy in copies:
            copy.start()
        for copy in copies:
            copy.wait()

    return pl.pallas_call(
        kernel,
        in_specs=[pl.BlockSpec(memory_space=pltpu.SMEM)]
        + [pl.BlockSpec(memory_space=pltpu.VMEM)] * len(blocks),
        out_specs=[ANY] * len(shape),
        out_shape=[jax.ShapeDtypeStruct(one, bf16) for one in shape],
        scratch_shapes=[pltpu.SemaphoreType.DMA((8 * len(blocks),))],
        compiler_params=kernel_params,
        name="arrange",
    )(places, *blocks)


def group_gather(own, axis):
    over = swap(own, axis)
    return jnp.concatenate((own, swap(own, "c"), over, swap(over, "c")), 0)


def near_sum(partial):
    rows = partial.shape[0] // 2
    return partial[:rows].astype(f32) + swap(partial[rows:], "c").astype(f32)


def group_scatter(partial, axis):
    rows = partial.shape[0] // 2
    over = swap(near_sum(partial[rows:]).astype(bf16), axis)
    return near_sum(partial[:rows]) + over.astype(f32)


def exchange(shares, axes):
    return lax.all_to_all(shares, axes, 0, 0, tiled=True)


def transpose_quarters(block):
    return lax.ppermute(
        block, ("z", "c", "x"), [(i * GROUP + j, j * GROUP + i) for i in range(Z) for j in range(GROUP)]
    )


def gather_units(block):
    if has_rest():
        block = lax.all_gather(block, "r", axis=1)
    return lax.all_gather(block.reshape(-1, block.shape[-1]), ("z", "w", "y"), axis=0, tiled=True)


def units_halves(grad):
    if has_rest():
        return grad, None
    parts = grad.reshape(Z, 2, -1, grad.shape[1])
    mine = lax.axis_index("y")
    sent = lax.dynamic_slice_in_dim(parts, 1 - mine, 1, 1).reshape(-1, grad.shape[1])
    return lax.dynamic_slice_in_dim(parts, mine, 1, 1).reshape(-1, grad.shape[1]), sent


def scatter_units(total, halves, rows, axes):
    if not has_rest():
        return lax.psum_scatter(total, axes, scatter_dimension=0, tiled=True)
    kept = lax.psum_scatter(total, ("z", "w", "y"), scatter_dimension=0, tiled=True)
    kept = kept.reshape(halves, -1, halves, rows, kept.shape[-1])
    return lax.psum_scatter(kept, "r", scatter_dimension=1).reshape(-1, kept.shape[-1])


def pack_heads(weights):
    rows, width = weights[0].shape
    part = width // GROUP

    def kernel(*refs):
        for at, ref in enumerate(refs[:-1]):
            for to in range(GROUP):
                refs[-1][to, :, at * part : (at + 1) * part] = ref[:, to * part : (to + 1) * part]

    return pl.pallas_call(
        kernel, out_shape=jax.ShapeDtypeStruct((GROUP, rows, len(weights) * part), bf16), name="pack_heads"
    )(*weights)


def unpack_heads(shares, count):
    rows, part = shares.shape[1], shares.shape[2] // count

    def kernel(ref, *outs):
        for at, out in enumerate(outs):
            for to in range(GROUP):
                out[:, to * part : (to + 1) * part] = ref[to, :, at * part : (at + 1) * part].astype(f32)

    whole = jax.ShapeDtypeStruct((rows, GROUP * part), f32)
    return pl.pallas_call(kernel, out_shape=[whole] * count, name="unpack_heads")(shares)


def unit_chunks(unit):
    for at in range(2 * Z):
        for place in range(GROUP):
            here = at * unit
            yield place, here // TILE * 2 * TILE + here % TILE, (at * GROUP + place) * unit


def pack_units(gate, up, unit):
    rows, hidden = gate.shape
    part = hidden // GROUP
    if has_rest():
        size = (rows, Z, lax.axis_size("w"), 2, 2, lax.axis_size("r"), 2, unit)
        both = [
            one.reshape(size).transpose(4, 6, 0, 1, 2, 3, 5, 7).reshape(GROUP, rows, part // TILE, TILE)
            for one in (gate, up)
        ]
        return jnp.stack(both, 3).reshape(GROUP, rows, 2 * part)

    def kernel(gate_ref, up_ref, out):
        for place, here, there in unit_chunks(unit):
            out[place, :, here : here + unit] = gate_ref[:, there : there + unit]
            out[place, :, here + TILE : here + TILE + unit] = up_ref[:, there : there + unit]

    return pl.pallas_call(
        kernel, out_shape=jax.ShapeDtypeStruct((GROUP, rows, 2 * part), bf16), name="pack_units"
    )(gate, up)


def unpack_units(shares, unit):
    rows, part = shares.shape[1], shares.shape[2] // 2
    if has_rest():
        size = (2, 2, rows, Z, lax.axis_size("w"), 2, lax.axis_size("r"), unit)
        both = shares.reshape(GROUP, rows, part // TILE, 2, TILE)
        return [
            both[:, :, :, at].reshape(size).transpose(2, 3, 4, 5, 0, 6, 1, 7).reshape(rows, GROUP * part).astype(f32)
            for at in range(2)
        ]

    def kernel(ref, gate_ref, up_ref):
        for place, here, there in unit_chunks(unit):
            gate_ref[:, there : there + unit] = ref[place, :, here : here + unit].astype(f32)
            up_ref[:, there : there + unit] = ref[place, :, here + TILE : here + TILE + unit].astype(f32)

    whole = jax.ShapeDtypeStruct((rows, GROUP * part), f32)
    return pl.pallas_call(kernel, out_shape=[whole, whole], name="unpack_units")(shares)


def triangle(length):
    rows = lax.broadcasted_iota(jnp.int32, (length, length), 0)
    cols = lax.broadcasted_iota(jnp.int32, (length, length), 1)
    return rows >= cols


def decays(forget_pre, tri):
    log_gate = jax.nn.log_sigmoid(forget_pre)
    highest = lax.Precision.HIGHEST
    down = jnp.dot(tri, log_gate, preferred_element_type=f32, precision=highest)
    across = lax.dot_general(
        log_gate, tri, (((0,), (1,)), ((), ())), preferred_element_type=f32, precision=highest
    )
    return down, across


def half_mask(half):
    lane = lax.broadcasted_iota(jnp.int32, (1, LANES), 1)
    return (lane >= HEAD) == bool(half)


def attend_kernel(q_ref, k_ref, v_ref, gate_ref, forget_ref, seg_col, seg_row, gated_ref, attended_ref, log_ref):
    length = q_ref.shape[0]
    causal = triangle(length)
    down, across = decays(forget_ref[...], causal.astype(f32))
    bias = jnp.where(causal & (seg_col[...] == seg_row[0]), 0.0, negative_big)
    lane = lax.broadcasted_iota(jnp.int32, (length, LANES), 1)
    logs = jnp.zeros((length, LANES), f32)
    for pair in range(LOCAL_HEADS // 2):
        cols = slice(pair * LANES, (pair + 1) * LANES)
        query, key, value = q_ref[:, cols], k_ref[:, cols], v_ref[:, cols].astype(bf16)
        both = []
        for half in range(2):
            head = 2 * pair + half
            mine = half_mask(half)
            scaled = jnp.where(mine, query, 0) * jnp.asarray(0.125, bf16)
            scores = product_nt(scaled, key) + down[:, head : head + 1] - across[head : head + 1, :] + bias
            top = jnp.max(scores, -1, keepdims=True)
            shifted = jnp.exp(scores - top)
            total = jnp.sum(shifted, -1, keepdims=True)
            probs = (shifted * (1.0 / total)).astype(bf16)
            both.append(jnp.where(mine, product(probs, value), 0.0))
            logs = jnp.where(lane == head, top + jnp.log(total), logs)
        attended = both[0] + both[1]
        attended_ref[:, cols] = attended
        gated_ref[:, cols] = (attended * jax.nn.sigmoid(gate_ref[:, cols])).astype(bf16)
    log_ref[...] = logs


def attend_back_kernel(
    q_ref, k_ref, v_ref, gate_ref, forget_ref, seg_col, seg_row, attended_ref, log_ref, grad_ref, heads_ref, dforget_ref,
):
    length, width = q_ref.shape
    causal = triangle(length)
    tri = causal.astype(f32)
    down, across = decays(forget_ref[...], tri)
    bias = jnp.where(causal & (seg_col[...] == seg_row[0]), 0.0, negative_big)
    lane = lax.broadcasted_iota(jnp.int32, (length, LANES), 1)
    grad_decay = jnp.zeros((length, LANES), f32)
    for pair in range(LOCAL_HEADS // 2):
        cols = slice(pair * LANES, (pair + 1) * LANES)
        query, key, value = q_ref[:, cols], k_ref[:, cols], v_ref[:, cols].astype(bf16)
        out_gate = jax.nn.sigmoid(gate_ref[:, cols])
        grad_gated = grad_ref[:, cols]
        grad_att = (grad_gated * out_gate).astype(bf16)
        grad_gate = (grad_gated * attended_ref[:, cols] * out_gate * (1.0 - out_gate)).astype(bf16)
        dq, dk, dv = [], [], []
        for half in range(2):
            head = 2 * pair + half
            mine = half_mask(half)
            scaled = jnp.where(mine, query, 0) * jnp.asarray(0.125, bf16)
            scores = product_nt(scaled, key) + down[:, head : head + 1] - across[head : head + 1, :] + bias
            probs = jnp.exp(scores - log_ref[:, head : head + 1])
            grad_prob = product_nt(jnp.where(mine, grad_att, 0), value)
            delta = jnp.sum(probs * grad_prob, -1, keepdims=True)
            grad_scores = (probs * (grad_prob - delta)).astype(bf16)
            dq.append(product(grad_scores, key))
            dk.append(product_tn(grad_scores, query))
            dv.append(product_tn(probs.astype(bf16), grad_att))
            one = (lane == head).astype(bf16)
            grad_decay = grad_decay + product(grad_scores, one) - product_tn(grad_scores, one)
        first = half_mask(0)
        found = (
            (jnp.where(first, dq[0], dq[1]) * 0.125).astype(bf16),
            (jnp.where(first, dk[0], dk[1]) * 0.125).astype(bf16),
            jnp.where(first, dv[0], dv[1]).astype(bf16),
            grad_gate,
        )
        for at, one in enumerate(found):
            heads_ref[:, at * width + pair * LANES : at * width + (pair + 1) * LANES] = one
    later = product_tn(tri, grad_decay, lax.Precision.HIGHEST)
    dforget_ref[...] = (later * jax.nn.sigmoid(-forget_ref[...])).astype(bf16)


def attention_specs(length, width, first):
    def columns(at):
        return pl.BlockSpec((length, width), lambda i: (first + i, at))

    lanes = pl.BlockSpec((length, LANES), lambda i: (first + i, 0))
    seg_col = pl.BlockSpec((length, 1), lambda i: (first + i, 0))
    seg_row = pl.BlockSpec((1, 1, length), lambda i: (first + i, 0, 0))
    return columns, lanes, seg_col, seg_row


def attend(query_key, value_gate, forget_pre, seg_col, seg_row, length):
    tokens, width = query_key.shape[0], query_key.shape[1] // 2
    columns, lanes, col_spec, row_spec = attention_specs(length, width, 0)
    return pl.pallas_call(
        attend_kernel,
        grid=(tokens // length,),
        in_specs=[columns(0), columns(1), columns(0), columns(1), lanes, col_spec, row_spec],
        out_specs=[columns(0), columns(0), lanes],
        out_shape=[
            jax.ShapeDtypeStruct((tokens, width), bf16),
            jax.ShapeDtypeStruct((tokens, width), f32),
            jax.ShapeDtypeStruct((tokens, LANES), f32),
        ],
        compiler_params=kernel_params,
        cost_estimate=pl.CostEstimate(
            flops=4 * tokens * length * width, bytes_accessed=14 * tokens * width, transcendentals=0
        ),
        name="attend",
    )(query_key, query_key, value_gate, value_gate, forget_pre, seg_col, seg_row)


def attend_back(query_key, value_gate, forget_pre, seg_col, seg_row, attended, logs, grad_gated, length, first):
    tokens, width = grad_gated.shape
    columns, lanes, col_spec, row_spec = attention_specs(length, width, first)
    own_columns, own_lanes, _, _ = attention_specs(length, width, 0)
    return pl.pallas_call(
        attend_back_kernel,
        grid=(tokens // length,),
        in_specs=[
            columns(0), columns(1), columns(0), columns(1), lanes, col_spec, row_spec,
            columns(0), lanes, own_columns(0),
        ],
        out_specs=[pl.BlockSpec((length, 4 * width), lambda i: (i, 0)), own_lanes],
        out_shape=[
            jax.ShapeDtypeStruct((tokens, 4 * width), bf16),
            jax.ShapeDtypeStruct((tokens, LANES), bf16),
        ],
        compiler_params=kernel_params,
        cost_estimate=pl.CostEstimate(
            flops=0, bytes_accessed=0, transcendentals=0
        ),
        name="attend_back",
    )(query_key, query_key, value_gate, value_gate, forget_pre, seg_col, seg_row, attended, logs, grad_gated)


def attn_terms(hidden, grad_heads, gated, grad_branch, rows):
    tokens, width = hidden.shape
    part, half = gated.shape[1], tokens // 2

    def both(left_ref, right_refs):
        near = product_tn(left_ref[:half, :], right_refs[0][...])
        return (near + product_tn(left_ref[half:, :], right_refs[1][...])).astype(bf16)

    def kernel(hidden_ref, near_ref, far_ref, gated_ref, branch_near, branch_far, out_ref, out_term):
        at_z = pl.program_id(0)

        @pl.when(at_z == 0)
        def _():
            out_term[...] = both(gated_ref, (branch_near, branch_far))

        term = both(hidden_ref, (near_ref, far_ref))
        for at_y in range(2):
            out_ref[at_y, : 4 * rows] = term[at_y * 4 * rows : (at_y + 1) * 4 * rows]
            first = pl.multiple_of((at_y * 4 + at_z) * rows, rows)
            out_ref[at_y, 4 * rows :] = out_term[pl.ds(first, rows), :]

    piece = pl.BlockSpec((half, width), lambda z: (0, 0))
    return pl.pallas_call(
        kernel,
        grid=(Z,),
        in_specs=[
            pl.BlockSpec((tokens, 8 * rows), lambda z: (0, z)),
            piece,
            piece,
            pl.BlockSpec((tokens, part), lambda z: (0, 0)),
            piece,
            piece,
        ],
        out_specs=pl.BlockSpec((2, 5 * rows, width), lambda z: (z, 0, 0)),
        out_shape=jax.ShapeDtypeStruct((2 * Z, 5 * rows, width), bf16),
        scratch_shapes=[pltpu.VMEM((part, width), bf16)],
        compiler_params=kernel_params,
        cost_estimate=pl.CostEstimate(
            flops=2 * tokens * width * (width + part), bytes_accessed=10 * tokens * width, transcendentals=0
        ),
        name="attn_terms",
    )(hidden, *grad_heads, gated, *grad_branch)


def back_through_heads(grad_heads, grad_forget, weight_heads, forget_weight):
    tokens, width = grad_heads.shape
    tile = width // 4

    def kernel(heads_ref, forget_ref, weight_ref, forget_weight_ref, out_ref):
        total = product_nt(heads_ref[...], weight_ref[...]) + product_nt(forget_ref[...], forget_weight_ref[...])
        out_ref[...] = total.astype(bf16)

    return pl.pallas_call(
        kernel,
        grid=(4,),
        in_specs=[
            pl.BlockSpec((tokens, width), lambda j: (0, 0)),
            pl.BlockSpec((tokens, LANES), lambda j: (0, 0)),
            pl.BlockSpec((tile, width), lambda j: (j, 0)),
            pl.BlockSpec((tile, LANES), lambda j: (j, 0)),
        ],
        out_specs=pl.BlockSpec((tokens, tile), lambda j: (0, j)),
        out_shape=jax.ShapeDtypeStruct((tokens, width), bf16),
        compiler_params=kernel_params,
        cost_estimate=pl.CostEstimate(
            flops=2 * tokens * width * width, bytes_accessed=8 * tokens * width, transcendentals=0
        ),
        name="back_through_heads",
    )(grad_heads, grad_forget, weight_heads, forget_weight)


def ffn_tile(hidden_ref, out_grad_ref, both_ref, down_ref, act_ref, dboth_ref):
    both = product(hidden_ref[...], both_ref[...])
    gate_ffn, up_ffn = both[:, :TILE], both[:, TILE:]
    grad_act = product_nt(out_grad_ref[...], down_ref[...])
    sigmoid_gate = jax.nn.sigmoid(gate_ffn)
    silu = gate_ffn * sigmoid_gate
    act_ref[...] = (silu * up_ffn).astype(bf16)
    grad_gate = grad_act * up_ffn * sigmoid_gate * (1.0 + gate_ffn * (1.0 - sigmoid_gate))
    dboth_ref[:, :TILE] = grad_gate.astype(bf16)
    dboth_ref[:, TILE:] = (grad_act * silu).astype(bf16)


def feed_forward(parts, out_grad, weight_both, weight_down):
    tokens, width = out_grad.shape
    units = weight_down.shape[0]
    steps = units // TILE
    whole = pl.BlockSpec((tokens, width), lambda j: (0, 0))
    rows = tokens // GROUP

    def kernel(*refs):
        joined = refs[GROUP + 3]

        @pl.when(pl.program_id(0) == 0)
        def _():
            for at in range(GROUP):
                joined[at * rows : (at + 1) * rows, :] = refs[at][...]

        ffn_tile(joined, *refs[GROUP : GROUP + 3], *refs[GROUP + 4 :])

    first = pl.BlockSpec((rows, width), lambda j: (0, 0))
    return pl.pallas_call(
        kernel,
        grid=(steps,),
        in_specs=[first] * GROUP
        + [
            whole,
            pl.BlockSpec((width, 2 * TILE), lambda j: (0, j)),
            pl.BlockSpec((TILE, width), lambda j: (j, 0)),
        ],
        out_specs=[
            whole,
            pl.BlockSpec((tokens, TILE), lambda j: (0, j)),
            pl.BlockSpec((tokens, 2 * TILE), lambda j: (0, j)),
        ],
        out_shape=[
            jax.ShapeDtypeStruct((tokens, width), bf16),
            jax.ShapeDtypeStruct((tokens, units), bf16),
            jax.ShapeDtypeStruct((tokens, 2 * units), bf16),
        ],
        compiler_params=kernel_params,
        cost_estimate=pl.CostEstimate(
            flops=6 * tokens * width * units, bytes_accessed=12 * tokens * width, transcendentals=0
        ),
        name="feed_forward",
    )(*parts, out_grad, weight_both, weight_down)


def shards(
    inputs,
    segment_ids,
    norm_one,
    w_query,
    w_key,
    w_value,
    w_gate_out,
    w_forget,
    forget_bias,
    w_output,
    norm_two,
    w_ffn_gate,
    w_ffn_up,
    w_ffn_down,
    out_grad,
):
    length, width = inputs.shape
    rows, unit = norm_one.shape[0], w_ffn_down.shape[0]
    size_w, size_r = lax.axis_size("w"), lax.axis_size("r")
    devices = math.prod(lax.axis_size(axis) for axis in ALL)
    place = lax.axis_index("c") * 2 + lax.axis_index("x")
    part = width // GROUP
    units = w_ffn_gate.shape[1] // GROUP
    far = 2 * length
    alone = not has_rest()

    heads_block = exchange(pack_heads((w_query, w_key, w_value, w_gate_out)), ("c", "x"))
    output_block = transpose_quarters(w_output)
    (units_shares,) = order((pack_units(w_ffn_gate, w_ffn_up, unit),), (heads_block,))
    units_block = exchange(units_shares, ("c", "x"))

    attn = [jnp.concatenate((over_rest(heads_block.reshape(4 * rows, width)), over_rest(output_block)), 2)]
    both = [units_block.reshape(4 * rows, 2 * units)]
    if alone:
        down_y = swap(w_ffn_down, "y")
        first = lax.axis_index("y") == 0
        down_pair = jnp.concatenate((jnp.where(first, w_ffn_down, down_y), jnp.where(first, down_y, w_ffn_down)), 0)
    else:
        down_pair = w_ffn_down
    (inputs_sent,) = order((inputs,), (heads_block, down_pair))
    inputs_x = swap(inputs_sent, "x")
    attn_y = [swap(attn[0], "y")]
    attn.append(along_z(attn[0]))

    (attn[1],) = order((attn[1],), (attn_y[0],))
    attn_y.append(swap(attn[1], "y"))
    attn.append(along_z(attn[1]))

    attn[2], out_grad_sent = order((attn[2], out_grad), (attn_y[1], inputs_x))
    out_grad_x = swap(out_grad_sent, "x")
    attn_y.append(swap(attn[2], "y"))
    attn.append(along_z(attn[2]))

    small = jnp.concatenate(
        (w_forget, norm_one[:, None], norm_two[:, None], jnp.zeros((rows, LANES - H - 2), bf16)), 1
    )
    (small,) = order((small,), (units_block,))
    seg_rows = length // LANES
    seg_own = jnp.pad(segment_ids.astype(bf16).reshape(seg_rows, LANES), ((0, 16 - seg_rows), (0, 0)))
    small = jnp.concatenate((small, seg_own), 0)
    small = exchange(jnp.broadcast_to(small[None], (devices, rows + 16, LANES)), ALL)
    small = small.reshape(devices, rows + 16, LANES)
    members = small[:, rows : rows + seg_rows].reshape(Z, size_w, 2, 2, size_r, 2, seg_rows, LANES)

    def member(other_x, other_c):
        at = [lax.axis_index(axis) for axis in ALL]
        at[5], at[3] = at[5] ^ other_x, at[3] ^ other_c
        return lax.dynamic_slice(members, (*at, 0, 0), (1, 1, 1, 1, 1, 1, seg_rows, LANES)).reshape(1, length)

    seg_all = jnp.concatenate((member(0, 0), member(0, 1), member(1, 0), member(1, 1)), 0).astype(f32)
    seg_col, seg_row = seg_all.reshape(-1, 1), seg_all[:, None, :]
    small = small[:, :rows].reshape(width, LANES)
    gain_one, gain_two = small[:, H].astype(f32), small[:, H + 1].astype(f32)
    forget_weight = lax.dynamic_slice(small, (0, place * LOCAL_HEADS), (width, LOCAL_HEADS))
    forget_weight = jnp.pad(forget_weight, ((0, 0), (0, LANES - LOCAL_HEADS)))
    bias_part = lax.dynamic_slice(forget_bias, (place * LOCAL_HEADS,), (LOCAL_HEADS,)).astype(f32)
    bias_part = jnp.pad(bias_part, (0, LANES - LOCAL_HEADS))

    attn[3], both[0], down_pair = order((attn[3], both[0], down_pair), (attn_y[2],))
    attn_y.append(swap(attn[3], "y"))
    both.append(along_z(both[0]))
    if alone:
        weight_down = lax.all_gather(down_pair, "z", axis=0, tiled=True)
    else:
        weight_down = gather_units(down_pair.reshape(1, 1, unit, width))

    def attn_order(whole):
        heads = whole[:, :, :, :, : 4 * rows].reshape(Z, 2, size_w, size_r, 2, 2, rows, width)
        out = whole[:, :, :, :, 4 * rows :].reshape(2, 2, 2, size_w, size_r, rows, width)
        return (
            heads.transpose(0, 2, 1, 4, 3, 5, 6, 7).reshape(width, width),
            out.transpose(3, 2, 0, 4, 1, 5, 6).reshape(part, width),
        )

    def attn_spots(outs, at_z, at_y):
        first = pl.multiple_of((at_z * 2 + at_y) * 4 * rows, 4 * rows)
        yield outs[0], 0, 4 * rows, outs[0].at[pl.ds(first, 4 * rows)]
        yield outs[1], 4 * rows, rows, outs[1].at[pl.ds(pl.multiple_of((at_y * 4 + at_z) * rows, rows), rows)]

    arrivals = [(step, other, (attn, attn_y)[other][step]) for step in range(Z) for other in range(2)]
    weight_heads, weight_out = arrange(arrivals, "y", ((width, width), (part, width)), attn_order, attn_spots)

    inputs_all = jnp.concatenate((inputs, swap(inputs, "c"), inputs_x, swap(inputs_x, "c")), 0)
    out_grad_all = jnp.concatenate((out_grad, swap(out_grad, "c"), out_grad_x, swap(out_grad_x, "c")), 0)
    hidden_one = (row_norm(inputs_all.astype(f32))[0] * gain_one).astype(bf16)

    hidden_one, both[0], both[1] = order((hidden_one, both[0], both[1]), (weight_out, out_grad_x))
    both_y = [None] * Z
    both_y[1] = swap(both[1], "y")
    both.append(along_z(both[1]))
    both_y[0] = swap(both[0], "y")
    query_key = product(hidden_one, weight_heads[:, : 2 * part]).astype(bf16)
    value_gate = product(hidden_one, weight_heads[:, 2 * part :])
    forget_pre = product(hidden_one, forget_weight) + bias_part
    gated_att, attended, logs = attend(query_key, value_gate, forget_pre, seg_col, seg_row, length)
    partial = product(gated_att, weight_out).astype(bf16)

    partial, both[2] = order((partial, both[2]), (both_y[1], out_grad_all))
    both_y[2] = swap(both[2], "y")
    both.append(along_z(both[2]))
    branch_x = swap(near_sum(partial[far:]).astype(bf16), "x")
    branch_near = near_sum(partial[:far])

    branch_x, branch_near, both[3] = order((branch_x, branch_near, both[3]), (both_y[0], both_y[2]))
    both_y[3] = swap(both[3], "y")
    tokens = inputs.astype(f32)
    middle = tokens + (branch_near + branch_x.astype(f32))
    normed_two, inv_two = row_norm(middle)
    hidden_own = (normed_two * gain_two).astype(bf16)
    hidden_x = swap(hidden_own, "x")
    hidden_parts = (hidden_own, swap(hidden_own, "c"), hidden_x, swap(hidden_x, "c"))
    if not alone:
        weight_both = gather_units(both[0].reshape(2, 2, rows, 2 * units))
    else:

        def both_spots(outs, at_z, at_y):
            first = pl.multiple_of((at_z * 2 + at_y) * 4 * rows, 4 * rows)
            yield outs[0], 0, 4 * rows, outs[0].at[pl.ds(first, 4 * rows)]

        arrivals = [(step, other, (both, both_y)[other][step]) for step in range(Z) for other in range(2)]
        (weight_both,) = arrange(arrivals, "y", ((width, 2 * units),), None, both_spots)

    hidden_two, activation, grad_both = feed_forward(hidden_parts, out_grad_all, weight_both, weight_down)
    both_term = product_tn(hidden_two, grad_both).astype(bf16)
    grad_both, activation = order((grad_both, activation), (both_term,))
    both_scattered = scatter_units(both_term, 2, rows, ("z", "y"))
    grad_hidden = product_nt(grad_both, weight_both).astype(bf16)
    near_sent = near_sum(grad_hidden[far:]).astype(bf16)
    grad_hidden_x = swap(near_sent, "x")
    near_own = near_sum(grad_hidden[:far])
    (activation,) = order((activation,), (near_sent,))
    kept_down, sent_down = units_halves(product_tn(activation, out_grad_all).astype(bf16))
    got_down = None if sent_down is None else swap(sent_down, "y")
    layer_partial = product(activation, weight_down).astype(bf16)
    grad_hidden_x, near_own = order(
        (grad_hidden_x, near_own), (layer_partial, kept_down if sent_down is None else sent_down)
    )

    grad_hidden_two = near_own + grad_hidden_x.astype(f32)
    grad_middle = out_grad.astype(f32) + norm_back(grad_hidden_two * gain_two, normed_two, inv_two)
    grad_own = grad_middle.astype(bf16)
    grad_c = swap(grad_own, "c")
    grad_x = swap(grad_own, "x")

    grad_near = jnp.concatenate((grad_own, grad_c), 0)

    def back(grad_branch, first):
        return attend_back(
            query_key, value_gate, forget_pre, seg_col, seg_row,
            attended, logs, product_nt(grad_branch, weight_out), length, first,
        )

    heads_near, forget_near = back(grad_near, 0)
    grad_x, heads_near, layer_partial = order((grad_x, heads_near, layer_partial), ())
    layer_output = (middle + group_scatter(layer_partial, "x")).astype(bf16)
    grad_far = jnp.concatenate((grad_x, swap(grad_x, "c")), 0)
    heads_far, forget_far = back(grad_far, 2)
    total_down = kept_down
    if got_down is not None:
        (got_down,) = order((got_down,), (heads_far,))
        total_down = (kept_down.astype(f32) + got_down.astype(f32)).astype(bf16)
    down_scattered = scatter_units(total_down, 1, unit, ("z",))

    if alone:
        terms = [attn_terms(hidden_one, (heads_near, heads_far), gated_att, (grad_near, grad_far), rows)]

        def attn_part(at_z, at_y):
            return lax.dynamic_index_in_dim(terms[-1], at_z * 2 + at_y, 0)[None]

    else:
        grad_heads = jnp.concatenate((heads_near, heads_far), 0)
        grad_branch = jnp.concatenate((grad_near, grad_far), 0)
        heads_term = product_tn(hidden_one, grad_heads).astype(bf16)
        out_term = product_tn(gated_att, grad_branch).astype(bf16)

        def attn_part(at_z, at_y):
            heads = heads_term.reshape(Z, size_w, 2, 2, size_r, 2, rows, width)
            size = (1, size_w, 1, 2, size_r, 2, rows, width)
            heads = lax.dynamic_slice(heads, (at_z, 0, at_y, 0, 0, 0, 0, 0), size)
            heads = heads[0, :, 0].transpose(0, 2, 1, 3, 4, 5).reshape(size_w, size_r, 4 * rows, width)
            out = out_term.reshape(size_w, 2, 2, size_r, 2, rows, width)
            size = (size_w, 1, 1, size_r, 1, rows, width)
            out = lax.dynamic_slice(out, (0, at_y, at_z // 2, 0, at_z % 2, 0, 0), size)
            return jnp.concatenate((heads, out.reshape(size_w, size_r, rows, width)), 2)

    other_y = 1 - lax.axis_index("y")
    attn_sent = attn_part(found_at(1), other_y)
    attn_got = [swap(attn_sent, "y")]
    heads_near, heads_far, forget_near, forget_far = order(
        (heads_near, heads_far, forget_near, forget_far), (attn_sent,)
    )
    if alone:
        terms += order((terms[0],), (attn_sent,))
    grad_forget = jnp.concatenate((forget_near, forget_far), 0)
    forget_term = product_tn(hidden_one, grad_forget).astype(bf16).reshape(devices, rows, LANES)
    forget_got = exchange(forget_term, ALL)
    bias_sum = jnp.sum(grad_forget.astype(f32), 0)[:LOCAL_HEADS]
    bias_sum = lax.dynamic_update_slice(jnp.zeros((H,), f32), bias_sum, (place * LOCAL_HEADS,))
    attn_later = [attn_part(found_at(step), other_y) for step in range(2, Z + 1)]
    attn_kept = [attn_part(found_at(step), 1 - other_y) for step in range(1, Z + 1)]
    attn_got[0], *attn_later = order((attn_got[0], *attn_later), (forget_term, total_down))
    attn_total = attn_kept[0].astype(f32) + attn_got[0].astype(f32)
    for step in range(1, Z):
        attn_sent = attn_total.astype(bf16)
        attn_z = along_z(attn_sent)
        if step == 1:
            heads_near, heads_far = order((heads_near, heads_far), (attn_sent,))
            grad_heads = jnp.concatenate((heads_near, heads_far), 0)
            hidden_partial = back_through_heads(grad_heads, grad_forget, weight_heads, forget_weight)
        (sent,) = order((attn_later[step - 1],), (attn_got[step - 1],))
        attn_got.append(swap(sent, "y"))
        if step == 1:
            attn_z, hidden_partial, both_scattered = order((attn_z, hidden_partial, both_scattered), (forget_got,))
            hidden_near = near_sum(hidden_partial[:far])
            hidden_x = swap(near_sum(hidden_partial[far:]).astype(bf16), "x")
            both_block = exchange(both_scattered.reshape(GROUP, rows, 2 * units), ("c", "x"))
            ffn_gate_grad, ffn_up_grad = unpack_units(both_block, unit)
        if step == 2:
            attn_z, hidden_x, hidden_near = order((attn_z, hidden_x, hidden_near), (ffn_gate_grad, layer_output))
            grad_hidden_one = hidden_near + hidden_x.astype(f32)
            normed, inv_one = row_norm(tokens)
            norm_one_partial = jnp.sum(grad_hidden_one * normed, 0)
            norm_two_partial = jnp.sum(grad_hidden_two * normed_two, 0)
            vectors = jnp.concatenate(
                (
                    norm_one_partial.reshape(devices, rows),
                    norm_two_partial.reshape(devices, rows),
                    jnp.broadcast_to(bias_sum[None], (devices, H)),
                ),
                1,
            )
            vectors_got = exchange(vectors, ALL)
            input_grad = grad_middle + norm_back(grad_hidden_one * gain_one, normed, inv_one)
        if step == 3:
            attn_z, down_scattered = order((attn_z, down_scattered), (vectors_got,))
        attn_total = attn_kept[step].astype(f32) + attn_got[step].astype(f32) + attn_z.astype(f32)
    ffn_down_grad = down_scattered.astype(f32)
    forget_got = forget_got.astype(f32).reshape(Z * size_w * 2, 2, size_r, 2, rows, LANES).sum((0, 2))
    forget_grad = forget_got[..., :LOCAL_HEADS].reshape(GROUP, rows, LOCAL_HEADS).transpose(1, 0, 2).reshape(rows, H)
    vectors_sum = jnp.sum(vectors_got, 0)
    norm_one_grad, norm_two_grad = vectors_sum[:rows], vectors_sum[rows : 2 * rows]
    forget_bias_grad = vectors_sum[2 * rows :]
    attn_sum = sum_over_rest(attn_total).astype(bf16)
    w_output_grad = transpose_quarters(attn_sum[4 * rows :]).astype(f32)
    query_grad, key_grad, value_grad, gate_out_grad = unpack_heads(
        exchange(attn_sum[: 4 * rows].reshape(4, rows, width), ("c", "x")), 4
    )
    return (
        layer_output,
        input_grad,
        norm_one_grad,
        query_grad,
        key_grad,
        value_grad,
        gate_out_grad,
        forget_grad,
        forget_bias_grad,
        w_output_grad,
        norm_two_grad,
        ffn_gate_grad,
        ffn_up_grad,
        ffn_down_grad,
    )


def solution(mesh):
    fsdp, rep = mesh.shape["fsdp"], mesh.shape["rep"]
    finer = Mesh(mesh.devices.reshape(Z, fsdp // 16, 2, 2, rep // 2, 2), ALL)
    rows, line = P(ALL, None), P(ALL)
    in_specs = (
        rows, rows, line, rows, rows, rows, rows, rows, P(), rows, line, rows, rows, rows, rows,
    )
    out_specs = (
        rows, rows, line, rows, rows, rows, rows, rows, P(), rows, line, rows, rows, rows,
    )
    return jax.shard_map(shards, mesh=finer, in_specs=in_specs, out_specs=out_specs, check_vma=False)
```

time: 597 us -> 528 us (0.88)
  waiting for transfers between devices: 242 us -> 175 us
  starting transfers between devices: 97.5 us -> 68.3 us
  between operations: 2.1 us -> 14.9 us
  local copies, waits for them, and re-layouts: 53.4 us -> 64 us
  Pallas kernels: 77.6 us -> 84.7 us
    ppermute x47 -> x38, waiting for transfers between devices: 141 us -> 85.6 us  [swap(): return lax.ppermute(value, axis, [(0, 1), (1, 0)])]
    ppermute x18 -> x9, waiting for transfers between devices: 71.6 us -> 40.8 us  [along_z(): return lax.ppermute(block, 'z', [(0, 1), (1, 3), (3, 2), (2, 0)])]
    all_to_all x8 -> x7, waiting for transfers between devices: 28.9 us -> 46.4 us  [exchange(): return lax.all_to_all(shares, axes, 0, 0, tiled=True)]
    ppermute x18 -> x9, starting transfers between devices: 23.9 us -> 7 us  [along_z(): return lax.ppermute(block, 'z', [(0, 1), (1, 3), (3, 2), (2, 0)])]
    all_to_all x8 -> x7, starting transfers between devices: 36.4 us -> 26.5 us  [exchange(): return lax.all_to_all(shares, axes, 0, 0, tiled=True)]
    pallas_call x1 -> x3, Pallas kernels: 28.4 us -> 37.2 us  [the longest x1 15.7 us: feed_forward(): pl.pallas_call(kernel, grid=(steps,), in_specs=[first] * GROUP + [whole,...]
    unnamed x203 -> x170, local copies, waits for them, and re-layouts: 29.5 us -> 36.3 us
    dot_general x5 -> x3, matrix products: 24.9 us -> 19.1 us  [product_tn(): lax.dot_general(left, right, (((0,), (0,)), ((), ())), preferred_element_...]
  transfers between devices with their start and end apart: 75 -> 59, of which waited for: 36 -> 26; matrix products, arithmetic and copies ran while one was open for 24% -> 26% of each run, Pallas kernels for 6% -> 13%
where the time goes in v2:
time: 528 us; the launch traced here: 519 us
  waiting for transfers between devices  175 us (33%)
  Pallas kernels  84.7 us (16%)
  starting transfers between devices  68.3 us (13%)
  local copies, waits for them, and re-layouts  64 us (12%)
  other arithmetic  59.4 us (11%)
  matrix products  52.6 us (10%)
  between operations  14.9 us (3%)
    ppermute x38, waiting for transfers between devices, swap(): return lax.ppermute(value, axis, [(0, 1), (1, 0)])  85.6 us
    all_to_all x7, waiting for transfers between devices, exchange(): return lax.all_to_all(shares, axes, 0, 0, tiled=True)  46.4 us
    ppermute x9, waiting for transfers between devices, along_z(): return lax.ppermute(block, 'z', [(0, 1), (1, 3), (3, 2), (2, 0)])  40.8 us
    unnamed x170, local copies, waits for them, and re-layouts  36.3 us
    ppermute x38, starting transfers between devices, swap(): return lax.ppermute(value, axis, [(0, 1), (1, 0)])  33.4 us
    all_to_all x7, starting transfers between devices, exchange(): return lax.all_to_all(shares, axes, 0, 0, tiled=True)  26.5 us
    pallas_call x2, Pallas kernels, attend_back(): pl.pallas_call(attend_back_kernel, grid=(tokens // length,), in_specs=[co...  20.1 us
    dot_general x3, matrix products, product_tn(): lax.dot_general(left, right, (((0,), (0,)), ((), ())), preferred_element_...  19.1 us
  transfers between devices with their start and end apart: 59, of which 26 were waited for; matrix products, arithmetic and copies ran while one was open for 26% of the time, Pallas kernels for 13%

profile of v2, /device:TPU:0, one launch (start us, length us, event | category | flops | bytes accessed | tf_op | source)
XLA Modules:
  0.0 518.9 jit_solution(10034318371672934415)
XLA Ops:
  7.2 3.0 collective-permute-start.1
  12.2 3.6 all-to-all-start
  20.5 6.0 %all-to-all-done.refs_1_ = bf16[4,48,1536]{2,1,0:T(8,128)(2,1)S(1)} async-done(((bf16[4,48,1536]{2,1,0:T(8,128)(2,1)}), bf16[4,48,1536]{2,1,0:T(8,128)(2,1)S(1)}, u32[]{:S(2)}, u32[]{:S(2)}) %all-to-all-start) | async-done | bytes 589856 | tf_op jit(solution)/shard_map/all_to_all | solution.py:153
  34.8 3.6 all-to-all-start.1
  40.2 8.8 %collective-permute-done.6.refs_1_ = bf16[1,1,240,1536]{3,2,1,0:T(8,128)(2,1)S(1)} collective-permute-done((bf16[1,1,240,1536]{3,2,1,0:T(8,128)(2,1)S(1)}, bf16[1,1,240,1536]{3,2,1,0:T(8,128)(2,1)S(1)}, u32[]{:S(2)}, u32[]{:S(2)}) %collective-permute-start.6) | collective-permute-done | bytes 737312 | tf_op jit(solution)/shard_map/ppermute | solution.py:67
  58.5 5.1 all-to-all-start.2
  66.0 2.8 collective-permute-done.8.refs_2_
  68.8 6.1 %collective-permute-done.7.refs_0_ = bf16[1,1,240,1536]{3,2,1,0:T(8,128)(2,1)S(1)} collective-permute-done((bf16[1,1,240,1536]{3,2,1,0:T(8,128)(2,1)}, bf16[1,1,240,1536]{3,2,1,0:T(8,128)(2,1)S(1)}, u32[]{:S(2)}, u32[]{:S(2)}) %collective-permute-start.7) | collective-permute-done | bytes 737312 | tf_op jit(solution)/shard_map/ppermute | solution.py:63
  75.7 3.3 collective-permute-start.9
  86.7 3.9 collective-permute-done.10.refs_3_
  90.6 6.1 %collective-permute-done.9.refs_0_ = bf16[1,1,240,1536]{3,2,1,0:T(8,128)(2,1)} collective-permute-done((bf16[1,1,240,1536]{3,2,1,0:T(8,128)(2,1)}, bf16[1,1,240,1536]{3,2,1,0:T(8,128)(2,1)}, u32[]{:S(2)}, u32[]{:S(2)}) %collective-permute-start.9) | collective-permute-done | bytes 737312 | tf_op jit(solution)/shard_map/ppermute | solution.py:63
  97.5 3.6 fusion.2.refs_0_
  103.4 9.9 %collective-permute-done.12 = bf16[1,1,240,1536]{3,2,1,0:T(8,128)(2,1)S(1)} collective-permute-done((bf16[1,1,240,1536]{3,2,1,0:T(8,128)(2,1)}, bf16[1,1,240,1536]{3,2,1,0:T(8,128)(2,1)S(1)}, u32[]{:S(2)}, u32[]{:S(2)}) %collective-permute-start.12) | collective-permute-done | bytes 737312 | tf_op jit(solution)/shard_map/ppermute | solution.py:67
  113.3 4.5 arrange.2
  118.6 7.1 %fusion.4.v_ref.gate_ref = f32[1024,768]{1,0:T(8,128)} fusion(bf16[1024,1536]{1,0:T(8,128)(2,1)} %get-tuple-element.75.hidden_ref, bf16[1536,1536]{1,0:T(8,128)(2,1)} %get-tuple-element.76.weight_ref), kind=kOutput, calls=%fused_computation.18 | convolution fusion | flops 2415919104 | bytes 8650752 | tf_op jit(solution)/shard_map/dot_general | solution.py:39
  125.7 2.6 fusion.11.q_ref.k_ref
  131.2 9.3 %attend.1 = (bf16[1024,384]{1,0:T(8,128)(2,1)S(1)}, f32[1024,384]{1,0:T(8,128)S(1)}, f32[1024,128]{1,0:T(8,128)S(1)}) custom-call(bf16[1024,768]{1,0:T(8,128)(2,1)S(1)} %fusion.11.q_ref.k_ref, bf16[1024,768]{1,0:T(8,128)(2,1)S(1)} %fusion.11.q_ref.k_ref, f32[1024,768]{1,0:T(8,128)} %fusion.4.v_ref.gate_ref, f32[1024,768]{1,0:T(8,128)} %fusion.4.v_ref.gate_ref, ...), custom_call_target="tpu_custom_call" | custom-call | flops 402653184 | bytes 5505024 | tf_op jit(solution)/shard_map/attend/pallas_call | solution.py:365
  140.5 3.5 convolution_convert_fusion.2.refs_0_
  146.1 2.7 fusion.36
  153.0 3.4 convert_add_fusion.6
  158.1 11.8 %collective-permute-done.22.refs_3_.refs_1_ = bf16[192,2048]{1,0:T(8,128)(2,1)S(1)} collective-permute-done((bf16[192,2048]{1,0:T(8,128)(2,1)S(1)}, bf16[192,2048]{1,0:T(8,128)(2,1)S(1)}, u32[]{:S(2)}, u32[]{:S(2)}) %collective-permute-start.22) | collective-permute-done | bytes 786464 | tf_op jit(solution)/shard_map/ppermute | solution.py:67
  170.8 22.3 %collective-permute-done.21.refs_2_ = bf16[192,2048]{1,0:T(8,128)(2,1)S(1)} collective-permute-done((bf16[192,2048]{1,0:T(8,128)(2,1)}, bf16[192,2048]{1,0:T(8,128)(2,1)S(1)}, u32[]{:S(2)}, u32[]{:S(2)}) %collective-permute-start.21) | collective-permute-done | bytes 786464 | tf_op jit(solution)/shard_map/ppermute | solution.py:63
  194.0 2.3 multiply_reduce_fusion.2
  196.6 5.5 %collective-permute-start.25 = (bf16[256,1536]{1,0:T(8,128)(2,1)S(1)}, bf16[256,1536]{1,0:T(8,128)(2,1)}, u32[]{:S(2)}, u32[]{:S(2)}) collective-permute-start(bf16[256,1536]{1,0:T(8,128)(2,1)S(1)} %multiply_convert_fusion.refs_0_), channel_id=1, source_target_pairs={{0,1},{1,0},{2,3},{3,2},{4,5},{5,4},{6,7},{7,6},{8,9},{9,8},{10,11... | collective-permute-start | bytes 2359304 | tf_op jit(solution)/shard_map/ppermute | solution.py:67
  202.1 10.1 %collective-permute-done.25.refs_2_ = bf16[256,1536]{1,0:T(8,128)(2,1)} collective-permute-done((bf16[256,1536]{1,0:T(8,128)(2,1)S(1)}, bf16[256,1536]{1,0:T(8,128)(2,1)}, u32[]{:S(2)}, u32[]{:S(2)}) %collective-permute-start.25) | collective-permute-done | bytes 786464 | tf_op jit(solution)/shard_map/ppermute | solution.py:67
  215.0 5.1 arrange.3.refs_5_
  225.4 15.7 %feed_forward.1 = (bf16[1024,1536]{1,0:T(8,128)(2,1)}, bf16[1024,1024]{1,0:T(8,128)(2,1)S(1)}, bf16[1024,2048]{1,0:T(8,128)(2,1)}) custom-call(bf16[256,1536]{1,0:T(8,128)(2,1)S(1)} %copy-done.33, bf16[256,1536]{1,0:T(8,128)(2,1)S(1)} %copy-done.40, bf16[256,1536]{1,0:T(8,128)(2,1)} %collective-permute-done.25.refs_2_, ...), custom_call_target="tpu_custom_call" | custom-call | flops 9663676416 | bytes 18874368 | tf_op jit(solution)/shard_map/feed_forward/pallas_call | solution.py:508
  242.4 11.3 %convolution_convert_fusion.refs_2_ = bf16[1536,2048]{1,0:T(8,128)(2,1)} fusion(bf16[1024,1536]{1,0:T(8,128)(2,1)} %get-tuple-element.88, bf16[1024,2048]{1,0:T(8,128)(2,1)} %get-tuple-element.86.refs_0_), kind=kOutput, calls=%fused_computation.2 | convolution fusion | flops 6445596672 | bytes 13631488 | tf_op jit(solution)/shard_map/dot_general | solution.py:49
  253.8 10.6 %convolution_convert_fusion.1 = bf16[1024,1536]{1,0:T(8,128)(2,1)S(1)} fusion(bf16[1024,2048]{1,0:T(8,128)(2,1)} %get-tuple-element.89, bf16[1536,2048]{1,0:T(8,128)(2,1)} %arrange.3.refs_5_), kind=kOutput, calls=%fused_computation.6 | convolution fusion | flops 6444023808 | bytes 13631488 | tf_op jit(solution)/shard_map/dot_general | solution.py:43
  266.8 2.7 collective-permute-done.28
  269.8 3.7 convert_add_fusion.5
  275.8 6.1 %convolution_convert_fusion.3 = bf16[1024,1536]{1,0:T(8,128)(2,1)S(1)} fusion(bf16[1024,1024]{1,0:T(8,128)(2,1)} %order.34, bf16[1024,1536]{1,0:T(8,128)(2,1)} %constant_dynamic-update-slice_fusion.refs_3_.refs_4_), kind=kOutput, calls=%fused_computation.8 | convolution fusion | flops 3222798336 | bytes 8388608 | tf_op jit(solution)/shard_map/dot_general | solution.py:49
  285.7 4.9 convolution_convert_fusion.4.refs_2_
  290.5 3.4 collective-permute-done.29.refs_0_
  294.8 2.8 multiply_reduce_fusion
  298.1 3.1 fusion.32
  305.2 2.8 fusion.31.grad_ref
  308.1 10.1 %attend_back.2 = (bf16[512,1536]{1,0:T(8,128)(2,1)S(1)}, bf16[512,128]{1,0:T(8,128)(2,1)S(1)}) custom-call(bf16[1024,768]{1,0:T(8,128)(2,1)S(1)} %fusion.11.q_ref.k_ref, bf16[1024,768]{1,0:T(8,128)(2,1)S(1)} %fusion.11.q_ref.k_ref, f32[1024,768]{1,0:T(8,128)} %fusion.4.v_ref.gate_ref, f32[1024,768]{1,0:T(8,128)} %fusion.4.v_ref.gate_ref, ...), custom_call_target="tpu_custom_call" | custom-call | tf_op jit(solution)/shard_map/attend_back/pallas_call | solution.py:387
  321.5 2.6 fusion.34
  329.5 10.0 %attend_back.3 = (bf16[512,1536]{1,0:T(8,128)(2,1)S(1)}, bf16[512,128]{1,0:T(8,128)(2,1)S(1)}) custom-call(bf16[1024,768]{1,0:T(8,128)(2,1)S(1)} %fusion.11.q_ref.k_ref, bf16[1024,768]{1,0:T(8,128)(2,1)S(1)} %fusion.11.q_ref.k_ref, f32[1024,768]{1,0:T(8,128)} %fusion.4.v_ref.gate_ref, f32[1024,768]{1,0:T(8,128)} %fusion.4.v_ref.gate_ref, ...), custom_call_target="tpu_custom_call" | custom-call | tf_op jit(solution)/shard_map/attend_back/pallas_call | solution.py:387
  339.6 10.8 %attn_terms.1.refs_0_ = bf16[8,240,1536]{2,1,0:T(8,128)(2,1)} custom-call(bf16[1024,1536]{1,0:T(8,128)(2,1)} %get-tuple-element.75.hidden_ref, bf16[512,1536]{1,0:T(8,128)(2,1)S(1)} %copy-done.2, bf16[512,1536]{1,0:T(8,128)(2,1)S(1)} %get-tuple-element.99.far_ref.refs_1_, bf16[1024,384]{1,0:T(8,128)(2,1)S(1)} %copy-done.38, ...), custom_call_target="tpu_custom_call" | custom-call | flops 6039797760 | bytes 15728640 | tf_op jit(solution)/shard_map/attn_terms/pallas_call | solution.py:429
  352.8 6.4 %collective-permute-done.38.refs_0_ = bf16[512,1536]{1,0:T(8,128)(2,1)} collective-permute-done((bf16[512,1536]{1,0:T(8,128)(2,1)}, bf16[512,1536]{1,0:T(8,128)(2,1)}, u32[]{:S(2)}, u32[]{:S(2)}) %collective-permute-start.38) | collective-permute-done | bytes 1572896 | tf_op jit(solution)/shard_map/ppermute | solution.py:67
  363.0 2.6 all-to-all-start.3
  365.6 3.5 fusion.3.refs_5_
  369.2 3.1 dynamic-slice_bitcast_fusion
  372.3 14.4 %collective-permute-done.37.refs_0_ = bf16[1,1,240,1536]{3,2,1,0:T(8,128)(2,1)} collective-permute-done((bf16[1,1,240,1536]{3,2,1,0:T(8,128)(2,1)}, bf16[1,1,240,1536]{3,2,1,0:T(8,128)(2,1)}, u32[]{:S(2)}, u32[]{:S(2)}) %collective-permute-start.37) | collective-permute-done | bytes 737312 | tf_op jit(solution)/shard_map/ppermute | solution.py:67
  389.4 3.9 pad_maximum_fusion.1.heads_ref
  393.3 10.6 %back_through_heads.1.refs_1_ = bf16[1024,1536]{1,0:T(8,128)(2,1)S(1)} custom-call(bf16[1024,1536]{1,0:T(8,128)(2,1)} %pad_maximum_fusion.1.heads_ref, bf16[1024,128]{1,0:T(8,128)(2,1)S(1)} %constant_dynamic-update-slice_fusion.6.forget_ref, bf16[1536,1536]{1,0:T(8,128)(2,1)} %get-tuple-element.76.weight_ref, bf16[1536,128]{1,0:T(8,128)(2,1)S(1)} %copy-done.36), custom_call_target="tpu_custom_call" | custom-call | flops 4831838208 | bytes 12582912 | tf_op jit(solution)/shard_map/back_through_heads/pallas_call | solution.py:459
  405.6 5.1 collective-permute-done.40.refs_0_
  411.5 2.6 fusion.33
  414.6 2.6 add_convert_fusion.2
  420.7 3.1 convert_add_fusion.3
  424.5 2.5 fusion.26
  427.8 3.5 all-to-all-start.4
  431.3 6.8 %collective-permute-done.35 = bf16[256,1536]{1,0:T(8,128)(2,1)} collective-permute-done((bf16[256,1536]{1,0:T(8,128)(2,1)}, bf16[256,1536]{1,0:T(8,128)(2,1)}, u32[]{:S(2)}, u32[]{:S(2)}) %collective-permute-start.35) | collective-permute-done | bytes 786464 | tf_op jit(solution)/shard_map/ppermute | solution.py:67
  438.0 2.9 add_convert_fusion.1.refs_4_
  442.3 19.9 %all-to-all-done.4.ref = bf16[4,48,2048]{2,1,0:T(8,128)(2,1)S(1)} async-done(((bf16[4,48,2048]{2,1,0:T(8,128)(2,1)}), bf16[4,48,2048]{2,1,0:T(8,128)(2,1)S(1)}, u32[]{:S(2)}, u32[]{:S(2)}) %all-to-all-start.4) | async-done | bytes 786464 | tf_op jit(solution)/shard_map/all_to_all | solution.py:153
  463.1 2.4 unpack_units.1
  466.4 2.9 fusion.21
  471.8 4.6 all-to-all-start.5
  476.4 3.2 fusion.17
  479.7 11.2 %all-to-all-done.5 = f32[32,1,120]{2,1,0:T(1,128)S(1)} async-done(((f32[32,1,120]{2,1,0:T(1,128)}), f32[32,1,120]{2,1,0:T(1,128)S(1)}, u32[]{:S(2)}, u32[]{:S(2)}) %all-to-all-start.5) | async-done | bytes 15392 | tf_op jit(solution)/shard_map/all_to_all | solution.py:153
  495.1 3.5 all-to-all-start.6
  501.5 7.7 %all-to-all-done.6.ref = bf16[4,48,1536]{2,1,0:T(8,128)(2,1)S(1)} async-done(((bf16[4,48,1536]{2,1,0:T(8,128)(2,1)}), bf16[4,48,1536]{2,1,0:T(8,128)(2,1)S(1)}, u32[]{:S(2)}, u32[]{:S(2)}) %all-to-all-start.6) | async-done | bytes 589856 | tf_op jit(solution)/shard_map/all_to_all | solution.py:153
  (354 shorter events, 118.9 us)
Async XLA Ops:
  7.2 12.4 %collective-permute-start.1 = (bf16[128,1536]{1,0:T(8,128)(2,1)}, bf16[128,1536]{1,0:T(8,128)(2,1)S(1)}, u32[]{:S(2)}, u32[]{:S(2)}) collective-permute-start(bf16[128,1536]{1,0:T(8,128)(2,1)} %param.28), channel_id=1, source_target_pairs={{0,4},{4,0},{1,5},{5,1},{2,6},{6,2},{3,7},{7,3},{8,12},{12,8},{9,1... | collective-permute-start | bytes 1179656 | tf_op jit(solution)/shard_map/ppermute | solution.py:67
  12.2 14.3 %all-to-all-start = ((bf16[4,48,1536]{2,1,0:T(8,128)(2,1)}), bf16[4,48,1536]{2,1,0:T(8,128)(2,1)S(1)}, u32[]{:S(2)}, u32[]{:S(2)}) async-start(bf16[4,48,1536]{2,1,0:T(8,128)(2,1)} %pack_heads.1), calls=%async_computation | async-start | bytes 1179648 | tf_op jit(solution)/shard_map/all_to_all | solution.py:153
  15.8 13.6 %collective-permute-start.4 = (bf16[48,1536]{1,0:T(8,128)(2,1)S(1)}, bf16[48,1536]{1,0:T(8,128)(2,1)S(1)}, u32[]{:S(2)}, u32[]{:S(2)}) collective-permute-start(bf16[48,1536]{1,0:T(8,128)(2,1)S(1)} %copy-done.77), channel_id=1, source_target_pairs={{0,0},{1,8},{2,16},{3,24},{8,1},{9,9},{10,17},{11,25},{16,2},{17,1... | collective-permute-start | bytes 442376 | tf_op jit(solution)/shard_map/ppermute | solution.py:157
  27.3 24.7 %collective-permute-start.2 = (bf16[256,1536]{1,0:T(8,128)(2,1)}, bf16[256,1536]{1,0:T(8,128)(2,1)}, u32[]{:S(2)}, u32[]{:S(2)}) collective-permute-start(bf16[256,1536]{1,0:T(8,128)(2,1)} %order.24), channel_id=1, source_target_pairs={{0,1},{1,0},{2,3},{3,2},{4,5},{5,4},{6,7},{7,6},{8,9},{9,8},{10,11... | collective-permute-start | bytes 2359304 | tf_op jit(solution)/shard_map/ppermute | solution.py:67
  30.7 18.3 %collective-permute-start.6 = (bf16[1,1,240,1536]{3,2,1,0:T(8,128)(2,1)S(1)}, bf16[1,1,240,1536]{3,2,1,0:T(8,128)(2,1)S(1)}, u32[]{:S(2)}, u32[]{:S(2)}) collective-permute-start(bf16[1,1,240,1536]{3,2,1,0:T(8,128)(2,1)S(1)} %get-tuple-element.159), channel_id=1, source_target_pairs={{0,4},{4,0},{1,5},{5,1},{2,6},{6,2},{3,7},{7,3},{8,12},{12,8},{9,1... | collective-permute-start | bytes 2211848 | tf_op jit(solution)/shard_map/ppermute | solution.py:67
  30.7 19.4 %collective-permute-start.5 = (bf16[1,1,240,1536]{3,2,1,0:T(8,128)(2,1)S(1)}, bf16[1,1,240,1536]{3,2,1,0:T(8,128)(2,1)}, u32[]{:S(2)}, u32[]{:S(2)}) collective-permute-start(bf16[1,1,240,1536]{3,2,1,0:T(8,128)(2,1)S(1)} %get-tuple-element.159), channel_id=1, source_target_pairs={{0,8},{8,24},{24,16},{16,0},{1,9},{9,25},{25,17},{17,1},{2,10},{10... | collective-permute-start | bytes 2211848 | tf_op jit(solution)/shard_map/ppermute | solution.py:63
  34.8 21.1 %all-to-all-start.1 = ((bf16[4,48,2048]{2,1,0:T(8,128)(2,1)}), bf16[4,48,2048]{2,1,0:T(8,128)(2,1)S(1)}, u32[]{:S(2)}, u32[]{:S(2)}) async-start(bf16[4,48,2048]{2,1,0:T(8,128)(2,1)} %order.25), calls=%async_computation.1 | async-start | bytes 1572864 | tf_op jit(solution)/shard_map/all_to_all | solution.py:153
  38.4 42.4 %collective-permute-start = (bf16[256,1536]{1,0:T(8,128)(2,1)}, bf16[256,1536]{1,0:T(8,128)(2,1)}, u32[]{:S(2)}, u32[]{:S(2)}) collective-permute-start(bf16[256,1536]{1,0:T(8,128)(2,1)} %param.15), channel_id=1, source_target_pairs={{0,2},{2,0},{1,3},{3,1},{4,6},{6,4},{5,7},{7,5},{8,10},{10,8},{9,1... | collective-permute-start | bytes 2359304 | tf_op jit(solution)/shard_map/ppermute | solution.py:67
  38.9 25.9 %collective-permute-start.16 = (bf16[256,1536]{1,0:T(8,128)(2,1)}, bf16[256,1536]{1,0:T(8,128)(2,1)}, u32[]{:S(2)}, u32[]{:S(2)}) collective-permute-start(bf16[256,1536]{1,0:T(8,128)(2,1)} %param.29), channel_id=1, source_target_pairs={{0,2},{2,0},{1,3},{3,1},{4,6},{6,4},{5,7},{7,5},{8,10},{10,8},{9,1... | collective-permute-start | bytes 2359304 | tf_op jit(solution)/shard_map/ppermute | solution.py:67
  50.1 18.6 %collective-permute-start.8 = (bf16[1,1,240,1536]{3,2,1,0:T(8,128)(2,1)}, bf16[1,1,240,1536]{3,2,1,0:T(8,128)(2,1)S(1)}, u32[]{:S(2)}, u32[]{:S(2)}) collective-permute-start(bf16[1,1,240,1536]{3,2,1,0:T(8,128)(2,1)} %order.27), channel_id=1, source_target_pairs={{0,4},{4,0},{1,5},{5,1},{2,6},{6,2},{3,7},{7,3},{8,12},{12,8},{9,1... | collective-permute-start | bytes 2211848 | tf_op jit(solution)/shard_map/ppermute | solution.py:67
  51.7 23.2 %collective-permute-start.7 = (bf16[1,1,240,1536]{3,2,1,0:T(8,128)(2,1)}, bf16[1,1,240,1536]{3,2,1,0:T(8,128)(2,1)S(1)}, u32[]{:S(2)}, u32[]{:S(2)}) collective-permute-start(bf16[1,1,240,1536]{3,2,1,0:T(8,128)(2,1)} %order.27), channel_id=1, source_target_pairs={{0,8},{8,24},{24,16},{16,0},{1,9},{9,25},{25,17},{17,1},{2,10},{10... | collective-permute-start | bytes 2211848 | tf_op jit(solution)/shard_map/ppermute | solution.py:63
  52.0 28.8 %collective-permute-start.3 = (bf16[256,1536]{1,0:T(8,128)(2,1)}, bf16[256,1536]{1,0:T(8,128)(2,1)}, u32[]{:S(2)}, u32[]{:S(2)}) collective-permute-start(bf16[256,1536]{1,0:T(8,128)(2,1)} %collective-permute-done.2.refs_3_), channel_id=1, source_target_pairs={{0,2},{2,0},{1,3},{3,1},{4,6},{6,4},{5,7},{7,5},{8,10},{10,8},{9,1... | collective-permute-start | bytes 2359304 | tf_op jit(solution)/shard_map/ppermute | solution.py:67
  58.5 24.6 %all-to-all-start.2 = ((bf16[32,64,128]{2,1,0:T(8,128)(2,1)}), bf16[32,64,128]{2,1,0:T(8,128)(2,1)S(1)}, u32[]{:S(2)}, u32[]{:S(2)}) async-start(bf16[32,64,128]{2,1,0:T(8,128)(2,1)} %broadcast_in_dim.25), calls=%async_computation.2 | async-start | bytes 1048576 | tf_op jit(solution)/shard_map/all_to_all | solution.py:153
  63.5 159.6 %all-gather.2.cloned.1.call-start = ((), (), s32[]{:S(2)}) async-start(), calls=%async_computation.9 | async-start | bytes 3932160 | tf_op jit(solution)/shard_map/all_gather | solution.py:618
  75.7 14.9 %collective-permute-start.10 = (bf16[1,1,240,1536]{3,2,1,0:T(8,128)(2,1)}, bf16[1,1,240,1536]{3,2,1,0:T(8,128)(2,1)S(1)}, u32[]{:S(2)}, u32[]{:S(2)}) collective-permute-start(bf16[1,1,240,1536]{3,2,1,0:T(8,128)(2,1)} %get-tuple-element.70), channel_id=1, source_target_pairs={{0,4},{4,0},{1,5},{5,1},{2,6},{6,2},{3,7},{7,3},{8,12},{12,8},{9,1... | collective-permute-start | bytes 2211848 | tf_op jit(solution)/shard_map/ppermute | solution.py:67
  75.7 21.0 %collective-permute-start.9 = (bf16[1,1,240,1536]{3,2,1,0:T(8,128)(2,1)}, bf16[1,1,240,1536]{3,2,1,0:T(8,128)(2,1)}, u32[]{:S(2)}, u32[]{:S(2)}) collective-permute-start(bf16[1,1,240,1536]{3,2,1,0:T(8,128)(2,1)} %get-tuple-element.70), channel_id=1, source_target_pairs={{0,8},{8,24},{24,16},{16,0},{1,9},{9,25},{25,17},{17,1},{2,10},{10... | collective-permute-start | bytes 2211848 | tf_op jit(solution)/shard_map/ppermute | solution.py:63
  79.0 22.1 %collective-permute-start.13 = (bf16[256,1536]{1,0:T(8,128)(2,1)}, bf16[256,1536]{1,0:T(8,128)(2,1)}, u32[]{:S(2)}, u32[]{:S(2)}) collective-permute-start(bf16[256,1536]{1,0:T(8,128)(2,1)} %get-tuple-element.74), channel_id=1, source_target_pairs={{0,1},{1,0},{2,3},{3,2},{4,5},{5,4},{6,7},{7,6},{8,9},{9,8},{10,11... | collective-permute-start | bytes 2359304 | tf_op jit(solution)/shard_map/ppermute | solution.py:67
  86.2 221.9 %copy-start.9 = (f32[1,1024]{0,1:T(8,128)}, f32[1,1024]{0,1:T(8,128)S(1)}, u32[]{:S(2)}) copy-start(f32[1,1024]{0,1:T(8,128)S(1)} %copy.118) | copy-start | bytes 12292
  96.7 16.5 %collective-permute-start.12 = (bf16[1,1,240,1536]{3,2,1,0:T(8,128)(2,1)}, bf16[1,1,240,1536]{3,2,1,0:T(8,128)(2,1)S(1)}, u32[]{:S(2)}, u32[]{:S(2)}) collective-permute-start(bf16[1,1,240,1536]{3,2,1,0:T(8,128)(2,1)} %get-tuple-element.72), channel_id=1, source_target_pairs={{0,4},{4,0},{1,5},{5,1},{2,6},{6,2},{3,7},{7,3},{8,12},{12,8},{9,1... | collective-permute-start | bytes 2211848 | tf_op jit(solution)/shard_map/ppermute | solution.py:67
  97.5 20.2 %collective-permute-start.11 = (bf16[192,2048]{1,0:T(8,128)(2,1)}, bf16[192,2048]{1,0:T(8,128)(2,1)S(1)}, u32[]{:S(2)}, u32[]{:S(2)}) collective-permute-start(bf16[192,2048]{1,0:T(8,128)(2,1)} %get-tuple-element.71.refs_1_), channel_id=1, source_target_pairs={{0,8},{8,24},{24,16},{16,0},{1,9},{9,25},{25,17},{17,1},{2,10},{10... | collective-permute-start | bytes 2359304 | tf_op jit(solution)/shard_map/ppermute | solution.py:63
  101.1 42.9 %collective-permute-start.17 = (bf16[256,1536]{1,0:T(8,128)(2,1)}, bf16[256,1536]{1,0:T(8,128)(2,1)}, u32[]{:S(2)}, u32[]{:S(2)}) collective-permute-start(bf16[256,1536]{1,0:T(8,128)(2,1)} %collective-permute-done.13.refs_4_), channel_id=1, source_target_pairs={{0,2},{2,0},{1,3},{3,1},{4,6},{6,4},{5,7},{7,5},{8,10},{10,8},{9,1... | collective-permute-start | bytes 2359304 | tf_op jit(solution)/shard_map/ppermute | solution.py:67
  128.3 17.7 %collective-permute-start.14 = (bf16[192,2048]{1,0:T(8,128)(2,1)S(1)}, bf16[192,2048]{1,0:T(8,128)(2,1)}, u32[]{:S(2)}, u32[]{:S(2)}) collective-permute-start(bf16[192,2048]{1,0:T(8,128)(2,1)S(1)} %copy-done.19), channel_id=1, source_target_pairs={{0,8},{8,24},{24,16},{16,0},{1,9},{9,25},{25,17},{17,1},{2,10},{10... | collective-permute-start | bytes 2359304 | tf_op jit(solution)/shard_map/ppermute | solution.py:63
  128.6 17.5 %collective-permute-start.15 = (bf16[192,2048]{1,0:T(8,128)(2,1)S(1)}, bf16[192,2048]{1,0:T(8,128)(2,1)}, u32[]{:S(2)}, u32[]{:S(2)}) collective-permute-start(bf16[192,2048]{1,0:T(8,128)(2,1)S(1)} %copy-done.19), channel_id=1, source_target_pairs={{0,4},{4,0},{1,5},{5,1},{2,6},{6,2},{3,7},{7,3},{8,12},{12,8},{9,1... | collective-permute-start | bytes 2359304 | tf_op jit(solution)/shard_map/ppermute | solution.py:67
  131.2 176.9 %copy-start.7 = (f32[1024,128]{1,0:T(8,128)}, f32[1024,128]{1,0:T(8,128)S(1)}, u32[]{:S(2)}) copy-start(f32[1024,128]{1,0:T(8,128)S(1)} %convolution_add_fusion.forget_ref) | copy-start | bytes 1572868
  148.8 4.2 collective-permute-start.18
  148.8 4.2 collective-permute-start.20
  149.3 261.3 %reduce-scatter.3.cloned.1.call-start = ((), (), s32[]{:S(2)}) async-start(), calls=%async_computation.10 | async-start | bytes 7077888 | tf_op jit(solution)/shard_map/reduce_scatter | solution.py:179
  149.4 20.5 %collective-permute-start.22 = (bf16[192,2048]{1,0:T(8,128)(2,1)S(1)}, bf16[192,2048]{1,0:T(8,128)(2,1)S(1)}, u32[]{:S(2)}, u32[]{:S(2)}) collective-permute-start(bf16[192,2048]{1,0:T(8,128)(2,1)S(1)} %copy-done.4), channel_id=1, source_target_pairs={{0,4},{4,0},{1,5},{5,1},{2,6},{6,2},{3,7},{7,3},{8,12},{12,8},{9,1... | collective-permute-start | bytes 2359304 | tf_op jit(solution)/shard_map/ppermute | solution.py:67
  151.5 41.6 %collective-permute-start.21 = (bf16[192,2048]{1,0:T(8,128)(2,1)}, bf16[192,2048]{1,0:T(8,128)(2,1)S(1)}, u32[]{:S(2)}, u32[]{:S(2)}) collective-permute-start(bf16[192,2048]{1,0:T(8,128)(2,1)} %get-tuple-element.80.refs_4_), channel_id=1, source_target_pairs={{0,8},{8,24},{24,16},{16,0},{1,9},{9,25},{25,17},{17,1},{2,10},{10... | collective-permute-start | bytes 2359304 | tf_op jit(solution)/shard_map/ppermute | solution.py:63
  152.7 41.3 %collective-permute-start.23 = (bf16[192,2048]{1,0:T(8,128)(2,1)}, bf16[192,2048]{1,0:T(8,128)(2,1)}, u32[]{:S(2)}, u32[]{:S(2)}) collective-permute-start(bf16[192,2048]{1,0:T(8,128)(2,1)} %get-tuple-element.80.refs_4_), channel_id=1, source_target_pairs={{0,4},{4,0},{1,5},{5,1},{2,6},{6,2},{3,7},{7,3},{8,12},{12,8},{9,1... | collective-permute-start | bytes 2359304 | tf_op jit(solution)/shard_map/ppermute | solution.py:67
  156.3 37.7 %collective-permute-start.19 = (bf16[256,1536]{1,0:T(8,128)(2,1)S(1)}, bf16[256,1536]{1,0:T(8,128)(2,1)}, u32[]{:S(2)}, u32[]{:S(2)}) collective-permute-start(bf16[256,1536]{1,0:T(8,128)(2,1)S(1)} %get-tuple-element.152), channel_id=1, source_target_pairs={{0,1},{1,0},{2,3},{3,2},{4,5},{5,4},{6,7},{7,6},{8,9},{9,8},{10,11... | collective-permute-start | bytes 2359304 | tf_op jit(solution)/shard_map/ppermute | solution.py:67
  196.4 18.6 %copy-start.15 = (bf16[192,2048]{1,0:T(8,128)(2,1)S(1)}, bf16[192,2048]{1,0:T(8,128)(2,1)}, u32[]{:S(2)}) copy-start(bf16[192,2048]{1,0:T(8,128)(2,1)} %copy-done.14) | copy-start | bytes 2359300
  196.4 18.6 %copy-start.20 = (bf16[192,2048]{1,0:T(8,128)(2,1)S(1)}, bf16[192,2048]{1,0:T(8,128)(2,1)}, u32[]{:S(2)}) copy-start(bf16[192,2048]{1,0:T(8,128)(2,1)} %get-tuple-element.78.refs_2_) | copy-start | bytes 2359300
  196.6 23.4 %copy-start.32 = (bf16[256,1536]{1,0:T(8,128)(2,1)}, bf16[256,1536]{1,0:T(8,128)(2,1)S(1)}, u32[]{:S(2)}) copy-start(bf16[256,1536]{1,0:T(8,128)(2,1)S(1)} %multiply_convert_fusion.refs_0_) | copy-start | bytes 2359300
  196.6 15.5 %collective-permute-start.25 = (bf16[256,1536]{1,0:T(8,128)(2,1)S(1)}, bf16[256,1536]{1,0:T(8,128)(2,1)}, u32[]{:S(2)}, u32[]{:S(2)}) collective-permute-start(bf16[256,1536]{1,0:T(8,128)(2,1)S(1)} %multiply_convert_fusion.refs_0_), channel_id=1, source_target_pairs={{0,1},{1,0},{2,3},{3,2},{4,5},{5,4},{6,7},{7,6},{8,9},{9,8},{10,11... | collective-permute-start | bytes 2359304 | tf_op jit(solution)/shard_map/ppermute | solution.py:67
  202.1 12.0 %collective-permute-start.27 = (bf16[192,2048]{1,0:T(8,128)(2,1)S(1)}, bf16[192,2048]{1,0:T(8,128)(2,1)S(1)}, u32[]{:S(2)}, u32[]{:S(2)}) collective-permute-start(bf16[192,2048]{1,0:T(8,128)(2,1)S(1)} %copy-done.17), channel_id=1, source_target_pairs={{0,4},{4,0},{1,5},{5,1},{2,6},{6,2},{3,7},{7,3},{8,12},{12,8},{9,1... | collective-permute-start | bytes 2359304 | tf_op jit(solution)/shard_map/ppermute | solution.py:67
  202.1 18.0 %collective-permute-start.24 = (bf16[256,1536]{1,0:T(8,128)(2,1)S(1)}, bf16[256,1536]{1,0:T(8,128)(2,1)S(1)}, u32[]{:S(2)}, u32[]{:S(2)}) collective-permute-start(bf16[256,1536]{1,0:T(8,128)(2,1)S(1)} %multiply_convert_fusion.refs_0_), channel_id=1, source_target_pairs={{0,2},{2,0},{1,3},{3,1},{4,6},{6,4},{5,7},{7,5},{8,10},{10,8},{9,1... | collective-permute-start | bytes 2359304 | tf_op jit(solution)/shard_map/ppermute | solution.py:67
  212.2 11.0 %collective-permute-start.26 = (bf16[256,1536]{1,0:T(8,128)(2,1)}, bf16[256,1536]{1,0:T(8,128)(2,1)}, u32[]{:S(2)}, u32[]{:S(2)}) collective-permute-start(bf16[256,1536]{1,0:T(8,128)(2,1)} %collective-permute-done.25.refs_2_), channel_id=1, source_target_pairs={{0,2},{2,0},{1,3},{3,1},{4,6},{6,4},{5,7},{7,5},{8,10},{10,8},{9,1... | collective-permute-start | bytes 2359304 | tf_op jit(solution)/shard_map/ppermute | solution.py:67
  266.3 3.2 collective-permute-start.28
  266.3 3.5 collective-permute-start.30
  273.5 20.4 %collective-permute-start.29 = (bf16[256,1536]{1,0:T(8,128)(2,1)}, bf16[256,1536]{1,0:T(8,128)(2,1)S(1)}, u32[]{:S(2)}, u32[]{:S(2)}) collective-permute-start(bf16[256,1536]{1,0:T(8,128)(2,1)} %get-tuple-element.148.refs_1_), channel_id=1, source_target_pairs={{0,1},{1,0},{2,3},{3,2},{4,5},{5,4},{6,7},{7,6},{8,9},{9,8},{10,11... | collective-permute-start | bytes 2359304 | tf_op jit(solution)/shard_map/ppermute | solution.py:67
  301.2 4.0 collective-permute-start.32
  301.2 20.3 %collective-permute-start.31 = (bf16[256,1536]{1,0:T(8,128)(2,1)}, bf16[256,1536]{1,0:T(8,128)(2,1)}, u32[]{:S(2)}, u32[]{:S(2)}) collective-permute-start(bf16[256,1536]{1,0:T(8,128)(2,1)} %get-tuple-element.132), channel_id=1, source_target_pairs={{0,1},{1,0},{2,3},{3,2},{4,5},{5,4},{6,7},{7,6},{8,9},{9,8},{10,11... | collective-permute-start | bytes 2359304 | tf_op jit(solution)/shard_map/ppermute | solution.py:67
  304.8 54.4 %collective-permute-start.38 = (bf16[512,1536]{1,0:T(8,128)(2,1)}, bf16[512,1536]{1,0:T(8,128)(2,1)}, u32[]{:S(2)}, u32[]{:S(2)}) collective-permute-start(bf16[512,1536]{1,0:T(8,128)(2,1)} %bitcast.123), channel_id=1, source_target_pairs={{0,4},{4,0},{1,5},{5,1},{2,6},{6,2},{3,7},{7,3},{8,12},{12,8},{9,1... | collective-permute-start | bytes 4718600 | tf_op jit(solution)/shard_map/ppermute | solution.py:67
  321.5 5.9 %collective-permute-start.36 = (bf16[256,1536]{1,0:T(8,128)(2,1)}, bf16[256,1536]{1,0:T(8,128)(2,1)S(1)}, u32[]{:S(2)}, u32[]{:S(2)}) collective-permute-start(bf16[256,1536]{1,0:T(8,128)(2,1)} %get-tuple-element.98), channel_id=1, source_target_pairs={{0,2},{2,0},{1,3},{3,1},{4,6},{6,4},{5,7},{7,5},{8,10},{10,8},{9,1... | collective-permute-start | bytes 2359304 | tf_op jit(solution)/shard_map/ppermute | solution.py:67
  324.1 90.6 %collective-permute-start.34 = (bf16[256,1536]{1,0:T(8,128)(2,1)}, bf16[256,1536]{1,0:T(8,128)(2,1)}, u32[]{:S(2)}, u32[]{:S(2)}) collective-permute-start(bf16[256,1536]{1,0:T(8,128)(2,1)} %get-tuple-element.146), channel_id=1, source_target_pairs={{0,2},{2,0},{1,3},{3,1},{4,6},{6,4},{5,7},{7,5},{8,10},{10,8},{9,1... | collective-permute-start | bytes 2359304 | tf_op jit(solution)/shard_map/ppermute | solution.py:67
  324.6 106.7 %collective-permute-start.33 = (bf16[256,1536]{1,0:T(8,128)(2,1)}, bf16[256,1536]{1,0:T(8,128)(2,1)}, u32[]{:S(2)}, u32[]{:S(2)}) collective-permute-start(bf16[256,1536]{1,0:T(8,128)(2,1)} %get-tuple-element.145), channel_id=1, source_target_pairs={{0,2},{2,0},{1,3},{3,1},{4,6},{6,4},{5,7},{7,5},{8,10},{10,8},{9,1... | collective-permute-start | bytes 2359304 | tf_op jit(solution)/shard_map/ppermute | solution.py:67
  352.5 34.2 %collective-permute-start.37 = (bf16[1,1,240,1536]{3,2,1,0:T(8,128)(2,1)}, bf16[1,1,240,1536]{3,2,1,0:T(8,128)(2,1)}, u32[]{:S(2)}, u32[]{:S(2)}) collective-permute-start(bf16[1,1,240,1536]{3,2,1,0:T(8,128)(2,1)} %dynamic-slice_bitcast_fusion.3.refs_1_.refs_4_), channel_id=1, source_target_pairs={{0,4},{4,0},{1,5},{5,1},{2,6},{6,2},{3,7},{7,3},{8,12},{12,8},{9,1... | collective-permute-start | bytes 2211848 | tf_op jit(solution)/shard_map/ppermute | solution.py:67
  363.0 42.6 %all-to-all-start.3 = ((bf16[32,48,128]{2,1,0:T(8,128)(2,1)}), bf16[32,48,128]{2,1,0:T(8,128)(2,1)S(1)}, u32[]{:S(2)}, u32[]{:S(2)}) async-start(bf16[32,48,128]{2,1,0:T(8,128)(2,1)} %bitcast.124), calls=%async_computation.4 | async-start | bytes 786432 | tf_op jit(solution)/shard_map/all_to_all | solution.py:153
  365.6 125.9 %reduce-scatter.5.cloned.1.call-start = ((), (), s32[]{:S(2)}) async-start(), calls=%async_computation.11 | async-start | bytes 1966080 | tf_op jit(solution)/shard_map/reduce_scatter | solution.py:179
  386.7 32.6 %collective-permute-start.39 = (bf16[1,1,240,1536]{3,2,1,0:T(8,128)(2,1)}, bf16[1,1,240,1536]{3,2,1,0:T(8,128)(2,1)}, u32[]{:S(2)}, u32[]{:S(2)}) collective-permute-start(bf16[1,1,240,1536]{3,2,1,0:T(8,128)(2,1)} %order.41), channel_id=1, source_target_pairs={{0,4},{4,0},{1,5},{5,1},{2,6},{6,2},{3,7},{7,3},{8,12},{12,8},{9,1... | collective-permute-start | bytes 2211848 | tf_op jit(solution)/shard_map/ppermute | solution.py:67
  388.6 22.1 %collective-permute-start.40 = (bf16[1,1,240,1536]{3,2,1,0:T(8,128)(2,1)S(1)}, bf16[1,1,240,1536]{3,2,1,0:T(8,128)(2,1)S(1)}, u32[]{:S(2)}, u32[]{:S(2)}) collective-permute-start(bf16[1,1,240,1536]{3,2,1,0:T(8,128)(2,1)S(1)} %fusion.24.refs_2_), channel_id=1, source_target_pairs={{0,8},{8,24},{24,16},{16,0},{1,9},{9,25},{25,17},{17,1},{2,10},{10... | collective-permute-start | bytes 2211848 | tf_op jit(solution)/shard_map/ppermute | solution.py:63
  414.1 6.6 %collective-permute-start.42 = (bf16[256,1536]{1,0:T(8,128)(2,1)}, bf16[256,1536]{1,0:T(8,128)(2,1)}, u32[]{:S(2)}, u32[]{:S(2)}) collective-permute-start(bf16[256,1536]{1,0:T(8,128)(2,1)} %get-tuple-element.142), channel_id=1, source_target_pairs={{0,2},{2,0},{1,3},{3,1},{4,6},{6,4},{5,7},{7,5},{8,10},{10,8},{9,1... | collective-permute-start | bytes 2359304 | tf_op jit(solution)/shard_map/ppermute | solution.py:67
  414.1 6.6 %collective-permute-start.44 = (bf16[256,1536]{1,0:T(8,128)(2,1)}, bf16[256,1536]{1,0:T(8,128)(2,1)}, u32[]{:S(2)}, u32[]{:S(2)}) collective-permute-start(bf16[256,1536]{1,0:T(8,128)(2,1)} %get-tuple-element.141), channel_id=1, source_target_pairs={{0,2},{2,0},{1,3},{3,1},{4,6},{6,4},{5,7},{7,5},{8,10},{10,8},{9,1... | collective-permute-start | bytes 2359304 | tf_op jit(solution)/shard_map/ppermute | solution.py:67
  417.2 20.8 %collective-permute-start.35 = (bf16[256,1536]{1,0:T(8,128)(2,1)}, bf16[256,1536]{1,0:T(8,128)(2,1)}, u32[]{:S(2)}, u32[]{:S(2)}) collective-permute-start(bf16[256,1536]{1,0:T(8,128)(2,1)} %add_convert_fusion.2), channel_id=1, source_target_pairs={{0,1},{1,0},{2,3},{3,2},{4,5},{5,4},{6,7},{7,6},{8,9},{9,8},{10,11... | collective-permute-start | bytes 2359304 | tf_op jit(solution)/shard_map/ppermute | solution.py:67
  419.2 21.7 %collective-permute-start.45 = (bf16[1,1,240,1536]{3,2,1,0:T(8,128)(2,1)}, bf16[1,1,240,1536]{3,2,1,0:T(8,128)(2,1)}, u32[]{:S(2)}, u32[]{:S(2)}) collective-permute-start(bf16[1,1,240,1536]{3,2,1,0:T(8,128)(2,1)} %order.45), channel_id=1, source_target_pairs={{0,4},{4,0},{1,5},{5,1},{2,6},{6,2},{3,7},{7,3},{8,12},{12,8},{9,1... | collective-permute-start | bytes 2211848 | tf_op jit(solution)/shard_map/ppermute | solution.py:67
  423.9 41.6 %collective-permute-start.43 = (bf16[256,1536]{1,0:T(8,128)(2,1)}, bf16[256,1536]{1,0:T(8,128)(2,1)S(1)}, u32[]{:S(2)}, u32[]{:S(2)}) collective-permute-start(bf16[256,1536]{1,0:T(8,128)(2,1)} %get-tuple-element.140), channel_id=1, source_target_pairs={{0,1},{1,0},{2,3},{3,2},{4,5},{5,4},{6,7},{7,6},{8,9},{9,8},{10,11... | collective-permute-start | bytes 2359304 | tf_op jit(solution)/shard_map/ppermute | solution.py:67
  427.0 38.5 %collective-permute-start.41 = (bf16[1,1,240,1536]{3,2,1,0:T(8,128)(2,1)}, bf16[1,1,240,1536]{3,2,1,0:T(8,128)(2,1)}, u32[]{:S(2)}, u32[]{:S(2)}) collective-permute-start(bf16[1,1,240,1536]{3,2,1,0:T(8,128)(2,1)} %fusion.26), channel_id=1, source_target_pairs={{0,8},{8,24},{24,16},{16,0},{1,9},{9,25},{25,17},{17,1},{2,10},{10... | collective-permute-start | bytes 2211848 | tf_op jit(solution)/shard_map/ppermute | solution.py:63
  427.8 34.4 %all-to-all-start.4 = ((bf16[4,48,2048]{2,1,0:T(8,128)(2,1)}), bf16[4,48,2048]{2,1,0:T(8,128)(2,1)S(1)}, u32[]{:S(2)}, u32[]{:S(2)}) async-start(bf16[4,48,2048]{2,1,0:T(8,128)(2,1)} %bitcast.35), calls=%async_computation.5 | async-start | bytes 1572864 | tf_op jit(solution)/shard_map/all_to_all | solution.py:153
  440.9 51.5 %collective-permute-start.46 = (bf16[1,1,240,1536]{3,2,1,0:T(8,128)(2,1)}, bf16[1,1,240,1536]{3,2,1,0:T(8,128)(2,1)}, u32[]{:S(2)}, u32[]{:S(2)}) collective-permute-start(bf16[1,1,240,1536]{3,2,1,0:T(8,128)(2,1)} %order.46), channel_id=1, source_target_pairs={{0,4},{4,0},{1,5},{5,1},{2,6},{6,2},{3,7},{7,3},{8,12},{12,8},{9,1... | collective-permute-start | bytes 2211848 | tf_op jit(solution)/shard_map/ppermute | solution.py:67
  469.2 22.2 %collective-permute-start.47 = (bf16[1,1,240,1536]{3,2,1,0:T(8,128)(2,1)}, bf16[1,1,240,1536]{3,2,1,0:T(8,128)(2,1)S(1)}, u32[]{:S(2)}, u32[]{:S(2)}) collective-permute-start(bf16[1,1,240,1536]{3,2,1,0:T(8,128)(2,1)} %fusion.21), channel_id=1, source_target_pairs={{0,8},{8,24},{24,16},{16,0},{1,9},{9,25},{25,17},{17,1},{2,10},{10... | collective-permute-start | bytes 2211848 | tf_op jit(solution)/shard_map/ppermute | solution.py:63
  471.8 19.0 %all-to-all-start.5 = ((f32[32,1,120]{2,1,0:T(1,128)}), f32[32,1,120]{2,1,0:T(1,128)S(1)}, u32[]{:S(2)}, u32[]{:S(2)}) async-start(f32[32,1,120]{2,1,0:T(1,128)} %bitcast.36), calls=%async_computation.6 | async-start | bytes 32768 | tf_op jit(solution)/shard_map/all_to_all | solution.py:153
  495.1 14.2 %all-to-all-start.6 = ((bf16[4,48,1536]{2,1,0:T(8,128)(2,1)}), bf16[4,48,1536]{2,1,0:T(8,128)(2,1)S(1)}, u32[]{:S(2)}, u32[]{:S(2)}) async-start(bf16[4,48,1536]{2,1,0:T(8,128)(2,1)} %bitcast.40), calls=%async_computation.8 | async-start | bytes 1179648 | tf_op jit(solution)/shard_map/all_to_all | solution.py:153
  498.6 2.2 collective-permute-start.48
  (75 other events, 324.6 us)
Sparse Core Ops, SparseCore 0:
  149.4 73.6 all-gather.1
  253.9 144.9 reduce-scatter.2
  401.2 62.3 reduce-scatter.4

commit v3 on v2

--- a/solution.py
+++ b/solution.py
@@ -140,7 +140,11 @@
 
 def near_sum(partial):
     rows = partial.shape[0] // 2
-    return partial[:rows].astype(f32) + swap(partial[rows:], "c").astype(f32)
+    return core_sum(partial[:rows], partial[rows:])
+
+
+def core_sum(own, other):
+    return own.astype(f32) + swap(other, "c").astype(f32)
 
 
 def group_scatter(partial, axis):
@@ -163,15 +167,6 @@
     if has_rest():
         block = lax.all_gather(block, "r", axis=1)
     return lax.all_gather(block.reshape(-1, block.shape[-1]), ("z", "w", "y"), axis=0, tiled=True)
-
-
-def units_halves(grad):
-    if has_rest():
-        return grad, None
-    parts = grad.reshape(Z, 2, -1, grad.shape[1])
-    mine = lax.axis_index("y")
-    sent = lax.dynamic_slice_in_dim(parts, 1 - mine, 1, 1).reshape(-1, grad.shape[1])
-    return lax.dynamic_slice_in_dim(parts, mine, 1, 1).reshape(-1, grad.shape[1]), sent
 
 
 def scatter_units(total, halves, rows, axes):
@@ -404,7 +399,8 @@
     )(query_key, query_key, value_gate, value_gate, forget_pre, seg_col, seg_row, attended, logs, grad_gated)
 
 
-def attn_terms(hidden, grad_heads, gated, grad_branch, rows):
+def attn_terms(hidden, grad_heads, gated, grad_branch, down_term, rows):
+    unit = down_term.shape[0] // (2 * Z)
     tokens, width = hidden.shape
     part, half = gated.shape[1], tokens // 2
 
@@ -412,7 +408,7 @@
         near = product_tn(left_ref[:half, :], right_refs[0][...])
         return (near + product_tn(left_ref[half:, :], right_refs[1][...])).astype(bf16)
 
-    def kernel(hidden_ref, near_ref, far_ref, gated_ref, branch_near, branch_far, out_ref, out_term):
+    def kernel(hidden_ref, near_ref, far_ref, gated_ref, branch_near, branch_far, down_ref, out_ref, out_term):
         at_z = pl.program_id(0)
 
         @pl.when(at_z == 0)
@@ -423,7 +419,8 @@
         for at_y in range(2):
             out_ref[at_y, : 4 * rows] = term[at_y * 4 * rows : (at_y + 1) * 4 * rows]
             first = pl.multiple_of((at_y * 4 + at_z) * rows, rows)
-            out_ref[at_y, 4 * rows :] = out_term[pl.ds(first, rows), :]
+            out_ref[at_y, 4 * rows : 5 * rows] = out_term[pl.ds(first, rows), :]
+            out_ref[at_y, 5 * rows :] = down_ref[at_y * unit : (at_y + 1) * unit]
 
     piece = pl.BlockSpec((half, width), lambda z: (0, 0))
     return pl.pallas_call(
@@ -436,25 +433,27 @@
             pl.BlockSpec((tokens, part), lambda z: (0, 0)),
             piece,
             piece,
+            pl.BlockSpec((2 * unit, width), lambda z: (z, 0)),
         ],
-        out_specs=pl.BlockSpec((2, 5 * rows, width), lambda z: (z, 0, 0)),
-        out_shape=jax.ShapeDtypeStruct((2 * Z, 5 * rows, width), bf16),
+        out_specs=pl.BlockSpec((2, 5 * rows + unit, width), lambda z: (z, 0, 0)),
+        out_shape=jax.ShapeDtypeStruct((2 * Z, 5 * rows + unit, width), bf16),
         scratch_shapes=[pltpu.VMEM((part, width), bf16)],
         compiler_params=kernel_params,
         cost_estimate=pl.CostEstimate(
             flops=2 * tokens * width * (width + part), bytes_accessed=10 * tokens * width, transcendentals=0
         ),
         name="attn_terms",
-    )(hidden, *grad_heads, gated, *grad_branch)
+    )(hidden, *grad_heads, gated, *grad_branch, down_term)
 
 
 def back_through_heads(grad_heads, grad_forget, weight_heads, forget_weight):
     tokens, width = grad_heads.shape
-    tile = width // 4
-
-    def kernel(heads_ref, forget_ref, weight_ref, forget_weight_ref, out_ref):
+    tile, rows = width // 4, tokens // GROUP
+
+    def kernel(heads_ref, forget_ref, weight_ref, forget_weight_ref, *outs):
         total = product_nt(heads_ref[...], weight_ref[...]) + product_nt(forget_ref[...], forget_weight_ref[...])
-        out_ref[...] = total.astype(bf16)
+        for at, out in enumerate(outs):
+            out[...] = total[at * rows : (at + 1) * rows].astype(bf16)
 
     return pl.pallas_call(
         kernel,
@@ -465,8 +464,8 @@
             pl.BlockSpec((tile, width), lambda j: (j, 0)),
             pl.BlockSpec((tile, LANES), lambda j: (j, 0)),
         ],
-        out_specs=pl.BlockSpec((tokens, tile), lambda j: (0, j)),
-        out_shape=jax.ShapeDtypeStruct((tokens, width), bf16),
+        out_specs=[pl.BlockSpec((rows, tile), lambda j: (0, j))] * GROUP,
+        out_shape=[jax.ShapeDtypeStruct((rows, width), bf16)] * GROUP,
         compiler_params=kernel_params,
         cost_estimate=pl.CostEstimate(
             flops=2 * tokens * width * width, bytes_accessed=8 * tokens * width, transcendentals=0
@@ -581,7 +580,7 @@
     attn_y.append(swap(attn[1], "y"))
     attn.append(along_z(attn[1]))
 
-    attn[2], out_grad_sent = order((attn[2], out_grad), (attn_y[1], inputs_x))
+    attn[2], out_grad_sent, down_pair = order((attn[2], out_grad, down_pair), (attn_y[1], inputs_x))
     out_grad_x = swap(out_grad_sent, "x")
     attn_y.append(swap(attn[2], "y"))
     attn.append(along_z(attn[2]))
@@ -611,7 +610,7 @@
     bias_part = lax.dynamic_slice(forget_bias, (place * LOCAL_HEADS,), (LOCAL_HEADS,)).astype(f32)
     bias_part = jnp.pad(bias_part, (0, LANES - LOCAL_HEADS))
 
-    attn[3], both[0], down_pair = order((attn[3], both[0], down_pair), (attn_y[2],))
+    attn[3], both[0] = order((attn[3], both[0]), (attn_y[2],))
     attn_y.append(swap(attn[3], "y"))
     both.append(along_z(both[0]))
     if alone:
@@ -684,12 +683,9 @@
     grad_hidden_x = swap(near_sent, "x")
     near_own = near_sum(grad_hidden[:far])
     (activation,) = order((activation,), (near_sent,))
-    kept_down, sent_down = units_halves(product_tn(activation, out_grad_all).astype(bf16))
-    got_down = None if sent_down is None else swap(sent_down, "y")
+    down_term = product_tn(activation, out_grad_all).astype(bf16)
     layer_partial = product(activation, weight_down).astype(bf16)
-    grad_hidden_x, near_own = order(
-        (grad_hidden_x, near_own), (layer_partial, kept_down if sent_down is None else sent_down)
-    )
+    grad_hidden_x, near_own = order((grad_hidden_x, near_own), (layer_partial, down_term))
 
     grad_hidden_two = near_own + grad_hidden_x.astype(f32)
     grad_middle = out_grad.astype(f32) + norm_back(grad_hidden_two * gain_two, normed_two, inv_two)
@@ -707,17 +703,16 @@
 
     heads_near, forget_near = back(grad_near, 0)
     grad_x, heads_near, layer_partial = order((grad_x, heads_near, layer_partial), ())
-    layer_output = (middle + group_scatter(layer_partial, "x")).astype(bf16)
+    layer_x = swap(near_sum(layer_partial[far:]).astype(bf16), "x")
+    layer_near = near_sum(layer_partial[:far])
     grad_far = jnp.concatenate((grad_x, swap(grad_x, "c")), 0)
     heads_far, forget_far = back(grad_far, 2)
-    total_down = kept_down
-    if got_down is not None:
-        (got_down,) = order((got_down,), (heads_far,))
-        total_down = (kept_down.astype(f32) + got_down.astype(f32)).astype(bf16)
-    down_scattered = scatter_units(total_down, 1, unit, ("z",))
-
+    if not alone:
+        down_scattered = scatter_units(down_term, 1, unit, ("z",))
     if alone:
-        terms = [attn_terms(hidden_one, (heads_near, heads_far), gated_att, (grad_near, grad_far), rows)]
+        terms = [attn_terms(
+            hidden_one, (heads_near, heads_far), gated_att, (grad_near, grad_far), down_term, rows
+        )]
 
         def attn_part(at_z, at_y):
             return lax.dynamic_index_in_dim(terms[-1], at_z * 2 + at_y, 0)[None]
@@ -747,13 +742,13 @@
     if alone:
         terms += order((terms[0],), (attn_sent,))
     grad_forget = jnp.concatenate((forget_near, forget_far), 0)
-    forget_term = product_tn(hidden_one, grad_forget).astype(bf16).reshape(devices, rows, LANES)
+    forget_term = product_tn(grad_forget, hidden_one)[:8].reshape(8, devices, rows).transpose(1, 0, 2)
     forget_got = exchange(forget_term, ALL)
     bias_sum = jnp.sum(grad_forget.astype(f32), 0)[:LOCAL_HEADS]
     bias_sum = lax.dynamic_update_slice(jnp.zeros((H,), f32), bias_sum, (place * LOCAL_HEADS,))
     attn_later = [attn_part(found_at(step), other_y) for step in range(2, Z + 1)]
     attn_kept = [attn_part(found_at(step), 1 - other_y) for step in range(1, Z + 1)]
-    attn_got[0], *attn_later = order((attn_got[0], *attn_later), (forget_term, total_down))
+    attn_got[0], *attn_later = order((attn_got[0], *attn_later), (forget_term, layer_x))
     attn_total = attn_kept[0].astype(f32) + attn_got[0].astype(f32)
     for step in range(1, Z):
         attn_sent = attn_total.astype(bf16)
@@ -765,13 +760,13 @@
         (sent,) = order((attn_later[step - 1],), (attn_got[step - 1],))
         attn_got.append(swap(sent, "y"))
         if step == 1:
-            attn_z, hidden_partial, both_scattered = order((attn_z, hidden_partial, both_scattered), (forget_got,))
-            hidden_near = near_sum(hidden_partial[:far])
-            hidden_x = swap(near_sum(hidden_partial[far:]).astype(bf16), "x")
+            attn_z, both_scattered, *hidden_partial = order((attn_z, both_scattered, *hidden_partial), (forget_got,))
+            hidden_near = core_sum(hidden_partial[0], hidden_partial[1])
+            hidden_x = swap(core_sum(hidden_partial[2], hidden_partial[3]).astype(bf16), "x")
             both_block = exchange(both_scattered.reshape(GROUP, rows, 2 * units), ("c", "x"))
             ffn_gate_grad, ffn_up_grad = unpack_units(both_block, unit)
         if step == 2:
-            attn_z, hidden_x, hidden_near = order((attn_z, hidden_x, hidden_near), (ffn_gate_grad, layer_output))
+            attn_z, hidden_near = order((attn_z, hidden_near), (layer_x,))
             grad_hidden_one = hidden_near + hidden_x.astype(f32)
             normed, inv_one = row_norm(tokens)
             norm_one_partial = jnp.sum(grad_hidden_one * normed, 0)
@@ -787,15 +782,20 @@
             vectors_got = exchange(vectors, ALL)
             input_grad = grad_middle + norm_back(grad_hidden_one * gain_one, normed, inv_one)
         if step == 3:
-            attn_z, down_scattered = order((attn_z, down_scattered), (vectors_got,))
+            (attn_z,) = order((attn_z,), (vectors_got, ffn_gate_grad))
+            layer_output = (middle + (layer_near + layer_x.astype(f32))).astype(bf16)
         attn_total = attn_kept[step].astype(f32) + attn_got[step].astype(f32) + attn_z.astype(f32)
-    ffn_down_grad = down_scattered.astype(f32)
-    forget_got = forget_got.astype(f32).reshape(Z * size_w * 2, 2, size_r, 2, rows, LANES).sum((0, 2))
-    forget_grad = forget_got[..., :LOCAL_HEADS].reshape(GROUP, rows, LOCAL_HEADS).transpose(1, 0, 2).reshape(rows, H)
+    forget_got = forget_got.reshape(Z * size_w * 2, 2, size_r, 2, 8, rows).sum((0, 2))
+    forget_grad = forget_got[:, :, :LOCAL_HEADS].reshape(H, rows).T
     vectors_sum = jnp.sum(vectors_got, 0)
     norm_one_grad, norm_two_grad = vectors_sum[:rows], vectors_sum[rows : 2 * rows]
     forget_bias_grad = vectors_sum[2 * rows :]
-    attn_sum = sum_over_rest(attn_total).astype(bf16)
+    if alone:
+        ffn_down_grad = attn_total[0, 0, 5 * rows :]
+        attn_sum = attn_total[0, 0, : 5 * rows].astype(bf16)
+    else:
+        ffn_down_grad = down_scattered.astype(f32)
+        attn_sum = sum_over_rest(attn_total).astype(bf16)
     w_output_grad = transpose_quarters(attn_sum[4 * rows :]).astype(f32)
     query_grad, key_grad, value_grad, gate_out_grad = unpack_heads(
         exchange(attn_sum[: 4 * rows].reshape(4, rows, width), ("c", "x")), 4

time: 528 us -> 515 us (0.975)
  waiting for transfers between devices: 175 us -> 164 us
    all_to_all x7, waiting for transfers between devices: 46.4 us -> 24.2 us  [exchange(): return lax.all_to_all(shares, axes, 0, 0, tiled=True)]
    ppermute x38 -> x37, starting transfers between devices: 33.4 us -> 26.6 us  [swap(): return lax.ppermute(value, axis, [(0, 1), (1, 0)])]
    ppermute x38 -> x37, waiting for transfers between devices: 85.6 us -> 92.2 us  [swap(): return lax.ppermute(value, axis, [(0, 1), (1, 0)])]
    ppermute x9, starting transfers between devices: 7 us -> 12.4 us  [along_z(): return lax.ppermute(block, 'z', [(0, 1), (1, 3), (3, 2), (2, 0)])]
    convert_element_type x5 -> x3, other arithmetic: 11.8 us -> 7.09 us  [the longest x1 2.63 us: shards(): layer_output = (middle + (layer_near + layer_x.astype(f32))).astype(bf16)]
    unnamed x170 -> x190, local copies, waits for them, and re-layouts: 36.3 us -> 39.3 us
  transfers between devices with their start and end apart: 59 -> 57, of which waited for: 26 -> 29; matrix products, arithmetic and copies ran while one was open for 26% -> 25% of each run, Pallas kernels for 13% -> 13%
where the time goes in v3:
time: 515 us; the launch traced here: 507 us
  waiting for transfers between devices  164 us (32%)
  Pallas kernels  85.2 us (17%)
  starting transfers between devices  68.5 us (13%)
  local copies, waits for them, and re-layouts  60.6 us (12%)
  other arithmetic  58.6 us (11%)
  matrix products  54.6 us (11%)
  between operations  15.4 us (3%)
    ppermute x37, waiting for transfers between devices, swap(): return lax.ppermute(value, axis, [(0, 1), (1, 0)])  92.2 us
    ppermute x9, waiting for transfers between devices, along_z(): return lax.ppermute(block, 'z', [(0, 1), (1, 3), (3, 2), (2, 0)])  41 us
    unnamed x190, local copies, waits for them, and re-layouts  39.3 us
    all_to_all x7, starting transfers between devices, exchange(): return lax.all_to_all(shares, axes, 0, 0, tiled=True)  28 us
    ppermute x37, starting transfers between devices, swap(): return lax.ppermute(value, axis, [(0, 1), (1, 0)])  26.6 us
    all_to_all x7, waiting for transfers between devices, exchange(): return lax.all_to_all(shares, axes, 0, 0, tiled=True)  24.2 us
    dot_general x3, matrix products, product_tn(): lax.dot_general(left, right, (((0,), (0,)), ((), ())), preferred_element_...  21.6 us
    pallas_call x2, Pallas kernels, attend_back(): pl.pallas_call(attend_back_kernel, grid=(tokens // length,), in_specs=[co...  19.9 us
  transfers between devices with their start and end apart: 57, of which 29 were waited for; matrix products, arithmetic and copies ran while one was open for 25% of the time, Pallas kernels for 13%

profile of v3, /device:TPU:0, one launch (start us, length us, event | category | flops | bytes accessed | tf_op | source)
XLA Modules:
  0.0 506.9 jit_solution(16231706800126803454)
XLA Ops:
  7.2 3.0 collective-permute-start.1
  12.2 3.6 all-to-all-start
  20.6 5.9 %all-to-all-done.refs_1_ = bf16[4,48,1536]{2,1,0:T(8,128)(2,1)S(1)} async-done(((bf16[4,48,1536]{2,1,0:T(8,128)(2,1)}), bf16[4,48,1536]{2,1,0:T(8,128)(2,1)S(1)}, u32[]{:S(2)}, u32[]{:S(2)}) %all-to-all-start) | async-done | bytes 589856 | tf_op jit(solution)/shard_map/all_to_all | solution.py:157
  35.6 3.6 all-to-all-start.1
  41.0 9.0 %collective-permute-done.6.refs_1_ = bf16[1,1,240,1536]{3,2,1,0:T(8,128)(2,1)S(1)} collective-permute-done((bf16[1,1,240,1536]{3,2,1,0:T(8,128)(2,1)}, bf16[1,1,240,1536]{3,2,1,0:T(8,128)(2,1)S(1)}, u32[]{:S(2)}, u32[]{:S(2)}) %collective-permute-start.6) | collective-permute-done | bytes 737312 | tf_op jit(solution)/shard_map/ppermute | solution.py:67
  58.7 4.9 all-to-all-start.2
  66.1 4.8 collective-permute-done.8.refs_3_
  70.9 7.2 %collective-permute-done.7.refs_0_ = bf16[1,1,240,1536]{3,2,1,0:T(8,128)(2,1)} collective-permute-done((bf16[1,1,240,1536]{3,2,1,0:T(8,128)(2,1)}, bf16[1,1,240,1536]{3,2,1,0:T(8,128)(2,1)}, u32[]{:S(2)}, u32[]{:S(2)}) %collective-permute-start.7) | collective-permute-done | bytes 737312 | tf_op jit(solution)/shard_map/ppermute | solution.py:63
  87.2 3.9 collective-permute-done.10.refs_2_
  91.1 7.3 %collective-permute-done.9.refs_0_ = bf16[1,1,240,1536]{3,2,1,0:T(8,128)(2,1)S(1)} collective-permute-done((bf16[1,1,240,1536]{3,2,1,0:T(8,128)(2,1)}, bf16[1,1,240,1536]{3,2,1,0:T(8,128)(2,1)S(1)}, u32[]{:S(2)}, u32[]{:S(2)}) %collective-permute-start.9) | collective-permute-done | bytes 737312 | tf_op jit(solution)/shard_map/ppermute | solution.py:63
  100.2 3.6 fusion.2.refs_0_
  106.1 9.3 %collective-permute-done.12 = bf16[1,1,240,1536]{3,2,1,0:T(8,128)(2,1)S(1)} collective-permute-done((bf16[1,1,240,1536]{3,2,1,0:T(8,128)(2,1)}, bf16[1,1,240,1536]{3,2,1,0:T(8,128)(2,1)S(1)}, u32[]{:S(2)}, u32[]{:S(2)}) %collective-permute-start.12) | collective-permute-done | bytes 737312 | tf_op jit(solution)/shard_map/ppermute | solution.py:67
  115.4 4.3 arrange.2
  120.6 7.0 %fusion.3.v_ref.gate_ref = f32[1024,768]{1,0:T(8,128)} fusion(bf16[1024,1536]{1,0:T(8,128)(2,1)} %get-tuple-element.79.hidden_ref, bf16[1536,1536]{1,0:T(8,128)(2,1)} %get-tuple-element.80.weight_ref), kind=kOutput, calls=%fused_computation.15 | convolution fusion | flops 2415919104 | bytes 8650752 | tf_op jit(solution)/shard_map/dot_general | solution.py:39
  127.7 2.6 fusion.16.q_ref.k_ref
  133.0 9.3 %attend.1 = (bf16[1024,384]{1,0:T(8,128)(2,1)S(1)}, f32[1024,384]{1,0:T(8,128)S(1)}, f32[1024,128]{1,0:T(8,128)S(1)}) custom-call(bf16[1024,768]{1,0:T(8,128)(2,1)S(1)} %fusion.16.q_ref.k_ref, bf16[1024,768]{1,0:T(8,128)(2,1)S(1)} %fusion.16.q_ref.k_ref, f32[1024,768]{1,0:T(8,128)} %fusion.3.v_ref.gate_ref, f32[1024,768]{1,0:T(8,128)} %fusion.3.v_ref.gate_ref, ...), custom_call_target="tpu_custom_call" | custom-call | flops 402653184 | bytes 5505024 | tf_op jit(solution)/shard_map/attend/pallas_call | solution.py:360
  142.3 3.5 convolution_convert_fusion.2.refs_0_
  149.7 2.7 fusion.37
  154.3 3.0 collective-permute-start.21
  157.8 3.4 convert_add_fusion.9
  162.3 11.2 %collective-permute-done.22.refs_3_.refs_1_ = bf16[192,2048]{1,0:T(8,128)(2,1)S(1)} collective-permute-done((bf16[192,2048]{1,0:T(8,128)(2,1)S(1)}, bf16[192,2048]{1,0:T(8,128)(2,1)S(1)}, u32[]{:S(2)}, u32[]{:S(2)}) %collective-permute-start.22) | collective-permute-done | bytes 786464 | tf_op jit(solution)/shard_map/ppermute | solution.py:67
  174.4 21.4 %collective-permute-done.21.refs_2_ = bf16[192,2048]{1,0:T(8,128)(2,1)S(1)} collective-permute-done((bf16[192,2048]{1,0:T(8,128)(2,1)}, bf16[192,2048]{1,0:T(8,128)(2,1)S(1)}, u32[]{:S(2)}, u32[]{:S(2)}) %collective-permute-start.21) | collective-permute-done | bytes 786464 | tf_op jit(solution)/shard_map/ppermute | solution.py:63
  196.7 2.5 multiply_reduce_fusion.2
  201.3 10.3 %collective-permute-done.25.refs_2_ = bf16[256,1536]{1,0:T(8,128)(2,1)} collective-permute-done((bf16[256,1536]{1,0:T(8,128)(2,1)S(1)}, bf16[256,1536]{1,0:T(8,128)(2,1)}, u32[]{:S(2)}, u32[]{:S(2)}) %collective-permute-start.25) | collective-permute-done | bytes 786464 | tf_op jit(solution)/shard_map/ppermute | solution.py:67
  213.8 4.6 arrange.3.refs_5_
  219.3 6.6 %all-gather.2.cloned.1.call-done.refs_6_ = bf16[1024,1536]{1,0:T(8,128)(2,1)} async-done(((bf16[256,1536]{1,0:T(8,128)(2,1)}), bf16[1024,1536]{1,0:T(8,128)(2,1)}) %all-gather.2.cloned.1.call-update) | async-done | bytes 3145744 | tf_op jit(solution)/shard_map/all_gather | solution.py:617
  228.2 15.9 %feed_forward.1 = (bf16[1024,1536]{1,0:T(8,128)(2,1)}, bf16[1024,1024]{1,0:T(8,128)(2,1)S(1)}, bf16[1024,2048]{1,0:T(8,128)(2,1)}) custom-call(bf16[256,1536]{1,0:T(8,128)(2,1)S(1)} %copy-done.44, bf16[256,1536]{1,0:T(8,128)(2,1)S(1)} %copy-done.49, bf16[256,1536]{1,0:T(8,128)(2,1)} %collective-permute-done.25.refs_2_, ...), custom_call_target="tpu_custom_call" | custom-call | flops 9663676416 | bytes 18874368 | tf_op jit(solution)/shard_map/feed_forward/pallas_call | solution.py:507
  245.5 11.2 %convolution_convert_fusion.refs_2_ = bf16[1536,2048]{1,0:T(8,128)(2,1)} fusion(bf16[1024,1536]{1,0:T(8,128)(2,1)} %get-tuple-element.92, bf16[1024,2048]{1,0:T(8,128)(2,1)} %get-tuple-element.90.refs_0_), kind=kOutput, calls=%fused_computation.2 | convolution fusion | flops 6445596672 | bytes 13631488 | tf_op jit(solution)/shard_map/dot_general | solution.py:49
  256.8 10.1 %convolution_convert_fusion.1 = bf16[1024,1536]{1,0:T(8,128)(2,1)S(1)} fusion(bf16[1024,2048]{1,0:T(8,128)(2,1)} %get-tuple-element.93, bf16[1536,2048]{1,0:T(8,128)(2,1)} %arrange.3.refs_5_), kind=kOutput, calls=%fused_computation.6 | convolution fusion | flops 6444023808 | bytes 13631488 | tf_op jit(solution)/shard_map/dot_general | solution.py:43
  273.4 7.9 %convolution_convert_fusion.3.refs_3_.down_ref = bf16[1024,1536]{1,0:T(8,128)(2,1)} fusion(bf16[1024,1024]{1,0:T(8,128)(2,1)} %order.33, bf16[1024,1536]{1,0:T(8,128)(2,1)} %constant_dynamic-update-slice_fusion.refs_3_.refs_4_), kind=kOutput, calls=%fused_computation.8 | convolution fusion | flops 3222798336 | bytes 8388608 | tf_op jit(solution)/shard_map/dot_general | solution.py:49
  281.3 5.0 convolution_convert_fusion.4.refs_2_
  286.3 5.7 %collective-permute-done.29.refs_0_ = bf16[256,1536]{1,0:T(8,128)(2,1)S(1)} collective-permute-done((bf16[256,1536]{1,0:T(8,128)(2,1)}, bf16[256,1536]{1,0:T(8,128)(2,1)S(1)}, u32[]{:S(2)}, u32[]{:S(2)}) %collective-permute-start.29) | collective-permute-done | bytes 786464 | tf_op jit(solution)/shard_map/ppermute | solution.py:67
  292.9 2.8 multiply_reduce_fusion
  296.2 3.1 fusion.34
  302.0 2.8 fusion.31.grad_ref
  304.8 9.9 %attend_back.2 = (bf16[512,1536]{1,0:T(8,128)(2,1)S(1)}, bf16[512,128]{1,0:T(8,128)(2,1)S(1)}) custom-call(bf16[1024,768]{1,0:T(8,128)(2,1)S(1)} %fusion.16.q_ref.k_ref, bf16[1024,768]{1,0:T(8,128)(2,1)S(1)} %fusion.16.q_ref.k_ref, f32[1024,768]{1,0:T(8,128)} %fusion.3.v_ref.gate_ref, f32[1024,768]{1,0:T(8,128)} %fusion.3.v_ref.gate_ref, ...), custom_call_target="tpu_custom_call" | custom-call | tf_op jit(solution)/shard_map/attend_back/pallas_call | solution.py:382
  316.6 3.1 collective-permute-done.31.refs_0_
  319.7 2.4 fusion.35
  328.4 10.0 %attend_back.3 = (bf16[512,1536]{1,0:T(8,128)(2,1)S(1)}, bf16[512,128]{1,0:T(8,128)(2,1)S(1)}) custom-call(bf16[1024,768]{1,0:T(8,128)(2,1)S(1)} %fusion.16.q_ref.k_ref, bf16[1024,768]{1,0:T(8,128)(2,1)S(1)} %fusion.16.q_ref.k_ref, f32[1024,768]{1,0:T(8,128)} %fusion.3.v_ref.gate_ref, f32[1024,768]{1,0:T(8,128)} %fusion.3.v_ref.gate_ref, ...), custom_call_target="tpu_custom_call" | custom-call | tf_op jit(solution)/shard_map/attend_back/pallas_call | solution.py:382
  338.4 11.9 %attn_terms.1.refs_0_ = bf16[8,368,1536]{2,1,0:T(8,128)(2,1)} custom-call(bf16[1024,1536]{1,0:T(8,128)(2,1)} %get-tuple-element.79.hidden_ref, bf16[512,1536]{1,0:T(8,128)(2,1)S(1)} %copy-done.1, bf16[512,1536]{1,0:T(8,128)(2,1)S(1)} %get-tuple-element.103.far_ref.refs_1_, bf16[1024,384]{1,0:T(8,128)(2,1)S(1)} %copy-done.40, ...), custom_call_target="tpu_custom_call" | custom-call | flops 6039797760 | bytes 15728640 | tf_op jit(solution)/shard_map/attn_terms/pallas_call | solution.py:426
  350.3 2.4 dynamic-slice_bitcast_fusion.3.refs_1_.refs_4_
  358.9 2.5 fusion.25
  362.4 3.8 all-to-all-start.3
  366.2 3.8 dynamic-slice_bitcast_fusion
  370.0 6.4 %collective-permute-done.35.refs_5_.refs_2_ = bf16[256,1536]{1,0:T(8,128)(2,1)S(1)} collective-permute-done((bf16[256,1536]{1,0:T(8,128)(2,1)}, bf16[256,1536]{1,0:T(8,128)(2,1)S(1)}, u32[]{:S(2)}, u32[]{:S(2)}) %collective-permute-start.35) | collective-permute-done | bytes 786464 | tf_op jit(solution)/shard_map/ppermute | solution.py:67
  376.4 4.3 collective-permute-done.37.refs_0_
  383.0 2.6 fusion.10.refs_2_
  390.0 3.8 pad_maximum_fusion.1.heads_ref
  393.8 10.7 %back_through_heads.1 = (bf16[256,1536]{1,0:T(8,128)(2,1)S(1)}, bf16[256,1536]{1,0:T(8,128)(2,1)S(1)}, bf16[256,1536]{1,0:T(8,128)(2,1)S(1)}, bf16[256,1536]{1,0:T(8,128)(2,1)S(1)}) custom-call(bf16[1024,1536]{1,0:T(8,128)(2,1)} %pad_maximum_fusion.1.heads_ref, bf16[1024,128]{1,0:T(8,128)(2,1)S(1)} %constant_dynamic-update-slice_fusion.6.forget_ref, ...), custom_call_target="tpu_custom_call" | custom-call | flops 4831838208 | bytes 12582912 | tf_op jit(solution)/shard_map/back_through_heads/pallas_call | solution.py:458
  409.7 3.6 collective-permute-done.39.refs_0_
  413.8 3.5 fusion.12
  418.4 4.2 all-to-all-start.5
  422.6 2.6 add_convert_fusion.1
  425.3 9.2 %collective-permute-done.44.refs_1_ = bf16[1,1,368,1536]{3,2,1,0:T(8,128)(2,1)S(1)} collective-permute-done((bf16[1,1,368,1536]{3,2,1,0:T(8,128)(2,1)}, bf16[1,1,368,1536]{3,2,1,0:T(8,128)(2,1)S(1)}, u32[]{:S(2)}, u32[]{:S(2)}) %collective-permute-start.44) | collective-permute-done | bytes 1130528 | tf_op jit(solution)/shard_map/ppermute | solution.py:67
  436.5 2.4 unpack_units.1
  442.4 2.5 convert_add_fusion.6.refs_1_
  446.1 3.2 fusion.8
  450.9 7.6 %collective-permute-done.43 = bf16[256,1536]{1,0:T(8,128)(2,1)} collective-permute-done((bf16[256,1536]{1,0:T(8,128)(2,1)}, bf16[256,1536]{1,0:T(8,128)(2,1)}, u32[]{:S(2)}, u32[]{:S(2)}) %collective-permute-start.43) | collective-permute-done | bytes 786464 | tf_op jit(solution)/shard_map/ppermute | solution.py:67
  461.1 4.4 all-to-all-start.4
  465.5 3.2 fusion.22
  468.7 8.3 %all-to-all-done.4 = f32[32,1,120]{2,1,0:T(1,128)S(1)} async-done(((f32[32,1,120]{2,1,0:T(1,128)}), f32[32,1,120]{2,1,0:T(1,128)S(1)}, u32[]{:S(2)}, u32[]{:S(2)}) %all-to-all-start.4) | async-done | bytes 15392 | tf_op jit(solution)/shard_map/all_to_all | solution.py:157
  479.3 2.4 fusion.32
  482.5 3.5 all-to-all-start.6
  488.4 8.3 %all-to-all-done.6.ref = bf16[4,48,1536]{2,1,0:T(8,128)(2,1)S(1)} async-done(((bf16[4,48,1536]{2,1,0:T(8,128)(2,1)}), bf16[4,48,1536]{2,1,0:T(8,128)(2,1)S(1)}, u32[]{:S(2)}, u32[]{:S(2)}) %all-to-all-start.6) | async-done | bytes 589856 | tf_op jit(solution)/shard_map/all_to_all | solution.py:157
  (369 shorter events, 122.1 us)
Async XLA Ops:
  7.2 12.4 %collective-permute-start.1 = (bf16[128,1536]{1,0:T(8,128)(2,1)}, bf16[128,1536]{1,0:T(8,128)(2,1)S(1)}, u32[]{:S(2)}, u32[]{:S(2)}) collective-permute-start(bf16[128,1536]{1,0:T(8,128)(2,1)} %param.28), channel_id=1, source_target_pairs={{0,4},{4,0},{1,5},{5,1},{2,6},{6,2},{3,7},{7,3},{8,12},{12,8},{9,1... | collective-permute-start | bytes 1179656 | tf_op jit(solution)/shard_map/ppermute | solution.py:67
  12.2 14.3 %all-to-all-start = ((bf16[4,48,1536]{2,1,0:T(8,128)(2,1)}), bf16[4,48,1536]{2,1,0:T(8,128)(2,1)S(1)}, u32[]{:S(2)}, u32[]{:S(2)}) async-start(bf16[4,48,1536]{2,1,0:T(8,128)(2,1)} %pack_heads.1), calls=%async_computation | async-start | bytes 1179648 | tf_op jit(solution)/shard_map/all_to_all | solution.py:157
  15.9 13.6 %collective-permute-start.4 = (bf16[48,1536]{1,0:T(8,128)(2,1)S(1)}, bf16[48,1536]{1,0:T(8,128)(2,1)S(1)}, u32[]{:S(2)}, u32[]{:S(2)}) collective-permute-start(bf16[48,1536]{1,0:T(8,128)(2,1)S(1)} %copy-done.86), channel_id=1, source_target_pairs={{0,0},{1,8},{2,16},{3,24},{8,1},{9,9},{10,17},{11,25},{16,2},{17,1... | collective-permute-start | bytes 442376 | tf_op jit(solution)/shard_map/ppermute | solution.py:161
  27.4 26.7 %collective-permute-start.2 = (bf16[256,1536]{1,0:T(8,128)(2,1)}, bf16[256,1536]{1,0:T(8,128)(2,1)}, u32[]{:S(2)}, u32[]{:S(2)}) collective-permute-start(bf16[256,1536]{1,0:T(8,128)(2,1)} %order.23), channel_id=1, source_target_pairs={{0,1},{1,0},{2,3},{3,2},{4,5},{5,4},{6,7},{7,6},{8,9},{9,8},{10,11... | collective-permute-start | bytes 2359304 | tf_op jit(solution)/shard_map/ppermute | solution.py:67
  31.5 18.4 %collective-permute-start.6 = (bf16[1,1,240,1536]{3,2,1,0:T(8,128)(2,1)}, bf16[1,1,240,1536]{3,2,1,0:T(8,128)(2,1)S(1)}, u32[]{:S(2)}, u32[]{:S(2)}) collective-permute-start(bf16[1,1,240,1536]{3,2,1,0:T(8,128)(2,1)} %get-tuple-element.163), channel_id=1, source_target_pairs={{0,4},{4,0},{1,5},{5,1},{2,6},{6,2},{3,7},{7,3},{8,12},{12,8},{9,1... | collective-permute-start | bytes 2211848 | tf_op jit(solution)/shard_map/ppermute | solution.py:67
  31.5 19.5 %collective-permute-start.5 = (bf16[1,1,240,1536]{3,2,1,0:T(8,128)(2,1)}, bf16[1,1,240,1536]{3,2,1,0:T(8,128)(2,1)S(1)}, u32[]{:S(2)}, u32[]{:S(2)}) collective-permute-start(bf16[1,1,240,1536]{3,2,1,0:T(8,128)(2,1)} %get-tuple-element.163), channel_id=1, source_target_pairs={{0,8},{8,24},{24,16},{16,0},{1,9},{9,25},{25,17},{17,1},{2,10},{10... | collective-permute-start | bytes 2211848 | tf_op jit(solution)/shard_map/ppermute | solution.py:63
  35.6 20.6 %all-to-all-start.1 = ((bf16[4,48,2048]{2,1,0:T(8,128)(2,1)}), bf16[4,48,2048]{2,1,0:T(8,128)(2,1)S(1)}, u32[]{:S(2)}, u32[]{:S(2)}) async-start(bf16[4,48,2048]{2,1,0:T(8,128)(2,1)} %order.24), calls=%async_computation.1 | async-start | bytes 1572864 | tf_op jit(solution)/shard_map/all_to_all | solution.py:157
  39.2 42.1 %collective-permute-start = (bf16[256,1536]{1,0:T(8,128)(2,1)}, bf16[256,1536]{1,0:T(8,128)(2,1)}, u32[]{:S(2)}, u32[]{:S(2)}) collective-permute-start(bf16[256,1536]{1,0:T(8,128)(2,1)} %param.15), channel_id=1, source_target_pairs={{0,2},{2,0},{1,3},{3,1},{4,6},{6,4},{5,7},{7,5},{8,10},{10,8},{9,1... | collective-permute-start | bytes 2359304 | tf_op jit(solution)/shard_map/ppermute | solution.py:67
  39.7 25.2 %collective-permute-start.16 = (bf16[256,1536]{1,0:T(8,128)(2,1)}, bf16[256,1536]{1,0:T(8,128)(2,1)}, u32[]{:S(2)}, u32[]{:S(2)}) collective-permute-start(bf16[256,1536]{1,0:T(8,128)(2,1)} %param.29), channel_id=1, source_target_pairs={{0,2},{2,0},{1,3},{3,1},{4,6},{6,4},{5,7},{7,5},{8,10},{10,8},{9,1... | collective-permute-start | bytes 2359304 | tf_op jit(solution)/shard_map/ppermute | solution.py:67
  41.0 15.2 %copy-start.87 = (s32[1,256]{1,0:T(1,128)S(1)}, s32[1,256]{1,0:T(1,128)}, u32[]{:S(2)}) copy-start(s32[1,256]{1,0:T(1,128)} %param.16) | copy-start | bytes 3076
  51.9 19.0 %collective-permute-start.8 = (bf16[1,1,240,1536]{3,2,1,0:T(8,128)(2,1)}, bf16[1,1,240,1536]{3,2,1,0:T(8,128)(2,1)S(1)}, u32[]{:S(2)}, u32[]{:S(2)}) collective-permute-start(bf16[1,1,240,1536]{3,2,1,0:T(8,128)(2,1)} %order.26), channel_id=1, source_target_pairs={{0,4},{4,0},{1,5},{5,1},{2,6},{6,2},{3,7},{7,3},{8,12},{12,8},{9,1... | collective-permute-start | bytes 2211848 | tf_op jit(solution)/shard_map/ppermute | solution.py:67
  53.5 24.6 %collective-permute-start.7 = (bf16[1,1,240,1536]{3,2,1,0:T(8,128)(2,1)}, bf16[1,1,240,1536]{3,2,1,0:T(8,128)(2,1)}, u32[]{:S(2)}, u32[]{:S(2)}) collective-permute-start(bf16[1,1,240,1536]{3,2,1,0:T(8,128)(2,1)} %order.26), channel_id=1, source_target_pairs={{0,8},{8,24},{24,16},{16,0},{1,9},{9,25},{25,17},{17,1},{2,10},{10... | collective-permute-start | bytes 2211848 | tf_op jit(solution)/shard_map/ppermute | solution.py:63
  54.0 27.4 %collective-permute-start.3 = (bf16[256,1536]{1,0:T(8,128)(2,1)}, bf16[256,1536]{1,0:T(8,128)(2,1)}, u32[]{:S(2)}, u32[]{:S(2)}) collective-permute-start(bf16[256,1536]{1,0:T(8,128)(2,1)} %collective-permute-done.2.refs_4_), channel_id=1, source_target_pairs={{0,2},{2,0},{1,3},{3,1},{4,6},{6,4},{5,7},{7,5},{8,10},{10,8},{9,1... | collective-permute-start | bytes 2359304 | tf_op jit(solution)/shard_map/ppermute | solution.py:67
  58.7 26.6 %all-to-all-start.2 = ((bf16[32,64,128]{2,1,0:T(8,128)(2,1)}), bf16[32,64,128]{2,1,0:T(8,128)(2,1)S(1)}, u32[]{:S(2)}, u32[]{:S(2)}) async-start(bf16[32,64,128]{2,1,0:T(8,128)(2,1)} %broadcast_in_dim.25), calls=%async_computation.2 | async-start | bytes 1048576 | tf_op jit(solution)/shard_map/all_to_all | solution.py:157
  63.6 162.3 %all-gather.2.cloned.1.call-start = ((), (), s32[]{:S(2)}) async-start(), calls=%async_computation.8 | async-start | bytes 3932160 | tf_op jit(solution)/shard_map/all_gather | solution.py:617
  78.1 13.0 %collective-permute-start.10 = (bf16[1,1,240,1536]{3,2,1,0:T(8,128)(2,1)}, bf16[1,1,240,1536]{3,2,1,0:T(8,128)(2,1)S(1)}, u32[]{:S(2)}, u32[]{:S(2)}) collective-permute-start(bf16[1,1,240,1536]{3,2,1,0:T(8,128)(2,1)} %get-tuple-element.74), channel_id=1, source_target_pairs={{0,4},{4,0},{1,5},{5,1},{2,6},{6,2},{3,7},{7,3},{8,12},{12,8},{9,1... | collective-permute-start | bytes 2211848 | tf_op jit(solution)/shard_map/ppermute | solution.py:67
  78.1 20.4 %collective-permute-start.9 = (bf16[1,1,240,1536]{3,2,1,0:T(8,128)(2,1)}, bf16[1,1,240,1536]{3,2,1,0:T(8,128)(2,1)S(1)}, u32[]{:S(2)}, u32[]{:S(2)}) collective-permute-start(bf16[1,1,240,1536]{3,2,1,0:T(8,128)(2,1)} %get-tuple-element.74), channel_id=1, source_target_pairs={{0,8},{8,24},{24,16},{16,0},{1,9},{9,25},{25,17},{17,1},{2,10},{10... | collective-permute-start | bytes 2211848 | tf_op jit(solution)/shard_map/ppermute | solution.py:63
  79.5 24.4 %collective-permute-start.13 = (bf16[256,1536]{1,0:T(8,128)(2,1)}, bf16[256,1536]{1,0:T(8,128)(2,1)}, u32[]{:S(2)}, u32[]{:S(2)}) collective-permute-start(bf16[256,1536]{1,0:T(8,128)(2,1)} %get-tuple-element.78), channel_id=1, source_target_pairs={{0,1},{1,0},{2,3},{3,2},{4,5},{5,4},{6,7},{7,6},{8,9},{9,8},{10,11... | collective-permute-start | bytes 2359304 | tf_op jit(solution)/shard_map/ppermute | solution.py:67
  86.7 218.1 %copy-start.7 = (f32[1,1024]{0,1:T(8,128)}, f32[1,1024]{0,1:T(8,128)S(1)}, u32[]{:S(2)}) copy-start(f32[1,1024]{0,1:T(8,128)S(1)} %copy.111) | copy-start | bytes 12292
  99.3 16.1 %collective-permute-start.12 = (bf16[1,1,240,1536]{3,2,1,0:T(8,128)(2,1)}, bf16[1,1,240,1536]{3,2,1,0:T(8,128)(2,1)S(1)}, u32[]{:S(2)}, u32[]{:S(2)}) collective-permute-start(bf16[1,1,240,1536]{3,2,1,0:T(8,128)(2,1)} %get-tuple-element.76), channel_id=1, source_target_pairs={{0,4},{4,0},{1,5},{5,1},{2,6},{6,2},{3,7},{7,3},{8,12},{12,8},{9,1... | collective-permute-start | bytes 2211848 | tf_op jit(solution)/shard_map/ppermute | solution.py:67
  100.1 19.6 %collective-permute-start.11 = (bf16[192,2048]{1,0:T(8,128)(2,1)}, bf16[192,2048]{1,0:T(8,128)(2,1)S(1)}, u32[]{:S(2)}, u32[]{:S(2)}) collective-permute-start(bf16[192,2048]{1,0:T(8,128)(2,1)} %get-tuple-element.75.refs_1_), channel_id=1, source_target_pairs={{0,8},{8,24},{24,16},{16,0},{1,9},{9,25},{25,17},{17,1},{2,10},{10... | collective-permute-start | bytes 2359304 | tf_op jit(solution)/shard_map/ppermute | solution.py:63
  100.2 15.2 %copy-start.36 = (bf16[1,1,240,1536]{3,2,1,0:T(8,128)(2,1)S(1)}, bf16[1,1,240,1536]{3,2,1,0:T(8,128)(2,1)}, u32[]{:S(2)}) copy-start(bf16[1,1,240,1536]{3,2,1,0:T(8,128)(2,1)} %copy-done.35) | copy-start | bytes 2211844
  103.9 41.9 %collective-permute-start.17 = (bf16[256,1536]{1,0:T(8,128)(2,1)}, bf16[256,1536]{1,0:T(8,128)(2,1)}, u32[]{:S(2)}, u32[]{:S(2)}) collective-permute-start(bf16[256,1536]{1,0:T(8,128)(2,1)} %collective-permute-done.13.refs_4_), channel_id=1, source_target_pairs={{0,2},{2,0},{1,3},{3,1},{4,6},{6,4},{5,7},{7,5},{8,10},{10,8},{9,1... | collective-permute-start | bytes 2359304 | tf_op jit(solution)/shard_map/ppermute | solution.py:67
  130.3 17.6 %collective-permute-start.14 = (bf16[192,2048]{1,0:T(8,128)(2,1)S(1)}, bf16[192,2048]{1,0:T(8,128)(2,1)S(1)}, u32[]{:S(2)}, u32[]{:S(2)}) collective-permute-start(bf16[192,2048]{1,0:T(8,128)(2,1)S(1)} %copy-done.17), channel_id=1, source_target_pairs={{0,8},{8,24},{24,16},{16,0},{1,9},{9,25},{25,17},{17,1},{2,10},{10... | collective-permute-start | bytes 2359304 | tf_op jit(solution)/shard_map/ppermute | solution.py:63
  130.9 17.9 %collective-permute-start.15 = (bf16[192,2048]{1,0:T(8,128)(2,1)S(1)}, bf16[192,2048]{1,0:T(8,128)(2,1)S(1)}, u32[]{:S(2)}, u32[]{:S(2)}) collective-permute-start(bf16[192,2048]{1,0:T(8,128)(2,1)S(1)} %copy-done.17), channel_id=1, source_target_pairs={{0,4},{4,0},{1,5},{5,1},{2,6},{6,2},{3,7},{7,3},{8,12},{12,8},{9,1... | collective-permute-start | bytes 2359304 | tf_op jit(solution)/shard_map/ppermute | solution.py:67
  133.0 171.8 %copy-start.5 = (f32[1024,128]{1,0:T(8,128)}, f32[1024,128]{1,0:T(8,128)S(1)}, u32[]{:S(2)}) copy-start(f32[1024,128]{1,0:T(8,128)S(1)} %convolution_add_fusion.forget_ref) | copy-start | bytes 1572868
  152.5 5.3 %collective-permute-start.18 = (bf16[256,1536]{1,0:T(8,128)(2,1)}, bf16[256,1536]{1,0:T(8,128)(2,1)}, u32[]{:S(2)}, u32[]{:S(2)}) collective-permute-start(bf16[256,1536]{1,0:T(8,128)(2,1)} %get-tuple-element.158), channel_id=1, source_target_pairs={{0,2},{2,0},{1,3},{3,1},{4,6},{6,4},{5,7},{7,5},{8,10},{10,8},{9,1... | collective-permute-start | bytes 2359304 | tf_op jit(solution)/shard_map/ppermute | solution.py:67
  152.5 5.3 %collective-permute-start.20 = (bf16[256,1536]{1,0:T(8,128)(2,1)}, bf16[256,1536]{1,0:T(8,128)(2,1)}, u32[]{:S(2)}, u32[]{:S(2)}) collective-permute-start(bf16[256,1536]{1,0:T(8,128)(2,1)} %get-tuple-element.157), channel_id=1, source_target_pairs={{0,2},{2,0},{1,3},{3,1},{4,6},{6,4},{5,7},{7,5},{8,10},{10,8},{9,1... | collective-permute-start | bytes 2359304 | tf_op jit(solution)/shard_map/ppermute | solution.py:67
  153.0 260.3 %reduce-scatter.2.cloned.1.call-start = ((), (), s32[]{:S(2)}) async-start(), calls=%async_computation.9 | async-start | bytes 7077888 | tf_op jit(solution)/shard_map/reduce_scatter | solution.py:174
  153.1 20.5 %collective-permute-start.22 = (bf16[192,2048]{1,0:T(8,128)(2,1)S(1)}, bf16[192,2048]{1,0:T(8,128)(2,1)S(1)}, u32[]{:S(2)}, u32[]{:S(2)}) collective-permute-start(bf16[192,2048]{1,0:T(8,128)(2,1)S(1)} %copy-done.4), channel_id=1, source_target_pairs={{0,4},{4,0},{1,5},{5,1},{2,6},{6,2},{3,7},{7,3},{8,12},{12,8},{9,1... | collective-permute-start | bytes 2359304 | tf_op jit(solution)/shard_map/ppermute | solution.py:67
  154.3 41.5 %collective-permute-start.21 = (bf16[192,2048]{1,0:T(8,128)(2,1)}, bf16[192,2048]{1,0:T(8,128)(2,1)S(1)}, u32[]{:S(2)}, u32[]{:S(2)}) collective-permute-start(bf16[192,2048]{1,0:T(8,128)(2,1)} %get-tuple-element.84.refs_4_), channel_id=1, source_target_pairs={{0,8},{8,24},{24,16},{16,0},{1,9},{9,25},{25,17},{17,1},{2,10},{10... | collective-permute-start | bytes 2359304 | tf_op jit(solution)/shard_map/ppermute | solution.py:63
  157.3 39.4 %collective-permute-start.23 = (bf16[192,2048]{1,0:T(8,128)(2,1)}, bf16[192,2048]{1,0:T(8,128)(2,1)}, u32[]{:S(2)}, u32[]{:S(2)}) collective-permute-start(bf16[192,2048]{1,0:T(8,128)(2,1)} %get-tuple-element.84.refs_4_), channel_id=1, source_target_pairs={{0,4},{4,0},{1,5},{5,1},{2,6},{6,2},{3,7},{7,3},{8,12},{12,8},{9,1... | collective-permute-start | bytes 2359304 | tf_op jit(solution)/shard_map/ppermute | solution.py:67
  161.2 35.4 %collective-permute-start.19 = (bf16[256,1536]{1,0:T(8,128)(2,1)S(1)}, bf16[256,1536]{1,0:T(8,128)(2,1)}, u32[]{:S(2)}, u32[]{:S(2)}) collective-permute-start(bf16[256,1536]{1,0:T(8,128)(2,1)S(1)} %get-tuple-element.156), channel_id=1, source_target_pairs={{0,1},{1,0},{2,3},{3,2},{4,5},{5,4},{6,7},{7,6},{8,9},{9,8},{10,11... | collective-permute-start | bytes 2359304 | tf_op jit(solution)/shard_map/ppermute | solution.py:67
  196.7 17.1 %copy-start.24 = (bf16[192,2048]{1,0:T(8,128)(2,1)S(1)}, bf16[192,2048]{1,0:T(8,128)(2,1)}, u32[]{:S(2)}) copy-start(bf16[192,2048]{1,0:T(8,128)(2,1)} %copy-done.23) | copy-start | bytes 2359300
  196.7 17.1 %copy-start.26 = (bf16[192,2048]{1,0:T(8,128)(2,1)S(1)}, bf16[192,2048]{1,0:T(8,128)(2,1)}, u32[]{:S(2)}) copy-start(bf16[192,2048]{1,0:T(8,128)(2,1)} %get-tuple-element.84.refs_4_) | copy-start | bytes 2359300
  199.4 19.0 %copy-start.43 = (bf16[256,1536]{1,0:T(8,128)(2,1)}, bf16[256,1536]{1,0:T(8,128)(2,1)S(1)}, u32[]{:S(2)}) copy-start(bf16[256,1536]{1,0:T(8,128)(2,1)S(1)} %multiply_convert_fusion.refs_0_) | copy-start | bytes 2359300
  199.4 12.2 %collective-permute-start.25 = (bf16[256,1536]{1,0:T(8,128)(2,1)S(1)}, bf16[256,1536]{1,0:T(8,128)(2,1)}, u32[]{:S(2)}, u32[]{:S(2)}) collective-permute-start(bf16[256,1536]{1,0:T(8,128)(2,1)S(1)} %multiply_convert_fusion.refs_0_), channel_id=1, source_target_pairs={{0,1},{1,0},{2,3},{3,2},{4,5},{5,4},{6,7},{7,6},{8,9},{9,8},{10,11... | collective-permute-start | bytes 2359304 | tf_op jit(solution)/shard_map/ppermute | solution.py:67
  200.9 12.0 %collective-permute-start.27 = (bf16[192,2048]{1,0:T(8,128)(2,1)S(1)}, bf16[192,2048]{1,0:T(8,128)(2,1)S(1)}, u32[]{:S(2)}, u32[]{:S(2)}) collective-permute-start(bf16[192,2048]{1,0:T(8,128)(2,1)S(1)} %copy-done.15), channel_id=1, source_target_pairs={{0,4},{4,0},{1,5},{5,1},{2,6},{6,2},{3,7},{7,3},{8,12},{12,8},{9,1... | collective-permute-start | bytes 2359304 | tf_op jit(solution)/shard_map/ppermute | solution.py:67
  201.3 17.1 %collective-permute-start.24 = (bf16[256,1536]{1,0:T(8,128)(2,1)S(1)}, bf16[256,1536]{1,0:T(8,128)(2,1)S(1)}, u32[]{:S(2)}, u32[]{:S(2)}) collective-permute-start(bf16[256,1536]{1,0:T(8,128)(2,1)S(1)} %multiply_convert_fusion.refs_0_), channel_id=1, source_target_pairs={{0,2},{2,0},{1,3},{3,1},{4,6},{6,4},{5,7},{7,5},{8,10},{10,8},{9,1... | collective-permute-start | bytes 2359304 | tf_op jit(solution)/shard_map/ppermute | solution.py:67
  211.6 14.3 %collective-permute-start.26 = (bf16[256,1536]{1,0:T(8,128)(2,1)}, bf16[256,1536]{1,0:T(8,128)(2,1)}, u32[]{:S(2)}, u32[]{:S(2)}) collective-permute-start(bf16[256,1536]{1,0:T(8,128)(2,1)} %collective-permute-done.25.refs_2_), channel_id=1, source_target_pairs={{0,2},{2,0},{1,3},{3,1},{4,6},{6,4},{5,7},{7,5},{8,10},{10,8},{9,1... | collective-permute-start | bytes 2359304 | tf_op jit(solution)/shard_map/ppermute | solution.py:67
  267.0 2.4 collective-permute-start.28
  267.1 3.4 collective-permute-start.30
  272.2 19.8 %collective-permute-start.29 = (bf16[256,1536]{1,0:T(8,128)(2,1)}, bf16[256,1536]{1,0:T(8,128)(2,1)S(1)}, u32[]{:S(2)}, u32[]{:S(2)}) collective-permute-start(bf16[256,1536]{1,0:T(8,128)(2,1)} %get-tuple-element.152.refs_1_), channel_id=1, source_target_pairs={{0,1},{1,0},{2,3},{3,2},{4,5},{5,4},{6,7},{7,6},{8,9},{9,8},{10,11... | collective-permute-start | bytes 2359304 | tf_op jit(solution)/shard_map/ppermute | solution.py:67
  299.4 2.6 collective-permute-start.32
  299.4 20.3 %collective-permute-start.31 = (bf16[256,1536]{1,0:T(8,128)(2,1)}, bf16[256,1536]{1,0:T(8,128)(2,1)}, u32[]{:S(2)}, u32[]{:S(2)}) collective-permute-start(bf16[256,1536]{1,0:T(8,128)(2,1)} %get-tuple-element.142), channel_id=1, source_target_pairs={{0,1},{1,0},{2,3},{3,2},{4,5},{5,4},{6,7},{7,6},{8,9},{9,8},{10,11... | collective-permute-start | bytes 2359304 | tf_op jit(solution)/shard_map/ppermute | solution.py:67
  319.7 5.6 %collective-permute-start.36 = (bf16[256,1536]{1,0:T(8,128)(2,1)}, bf16[256,1536]{1,0:T(8,128)(2,1)S(1)}, u32[]{:S(2)}, u32[]{:S(2)}) collective-permute-start(bf16[256,1536]{1,0:T(8,128)(2,1)} %get-tuple-element.102), channel_id=1, source_target_pairs={{0,2},{2,0},{1,3},{3,1},{4,6},{6,4},{5,7},{7,5},{8,10},{10,8},{9,1... | collective-permute-start | bytes 2359304 | tf_op jit(solution)/shard_map/ppermute | solution.py:67
  322.0 31.9 %collective-permute-start.34 = (bf16[256,1536]{1,0:T(8,128)(2,1)S(1)}, bf16[256,1536]{1,0:T(8,128)(2,1)S(1)}, u32[]{:S(2)}, u32[]{:S(2)}) collective-permute-start(bf16[256,1536]{1,0:T(8,128)(2,1)S(1)} %get-tuple-element.150), channel_id=1, source_target_pairs={{0,2},{2,0},{1,3},{3,1},{4,6},{6,4},{5,7},{7,5},{8,10},{10,8},{9,1... | collective-permute-start | bytes 2359304 | tf_op jit(solution)/shard_map/ppermute | solution.py:67
  322.5 100.1 %collective-permute-start.33 = (bf16[256,1536]{1,0:T(8,128)(2,1)}, bf16[256,1536]{1,0:T(8,128)(2,1)}, u32[]{:S(2)}, u32[]{:S(2)}) collective-permute-start(bf16[256,1536]{1,0:T(8,128)(2,1)} %get-tuple-element.149), channel_id=1, source_target_pairs={{0,2},{2,0},{1,3},{3,1},{4,6},{6,4},{5,7},{7,5},{8,10},{10,8},{9,1... | collective-permute-start | bytes 2359304 | tf_op jit(solution)/shard_map/ppermute | solution.py:67
  352.6 28.0 %collective-permute-start.37 = (bf16[1,1,368,1536]{3,2,1,0:T(8,128)(2,1)}, bf16[1,1,368,1536]{3,2,1,0:T(8,128)(2,1)S(1)}, u32[]{:S(2)}, u32[]{:S(2)}) collective-permute-start(bf16[1,1,368,1536]{3,2,1,0:T(8,128)(2,1)} %dynamic-slice_bitcast_fusion.3.refs_1_.refs_4_), channel_id=1, source_target_pairs={{0,4},{4,0},{1,5},{5,1},{2,6},{6,2},{3,7},{7,3},{8,12},{12,8},{9,1... | collective-permute-start | bytes 3391496 | tf_op jit(solution)/shard_map/ppermute | solution.py:67
  356.1 20.3 %collective-permute-start.35 = (bf16[256,1536]{1,0:T(8,128)(2,1)}, bf16[256,1536]{1,0:T(8,128)(2,1)S(1)}, u32[]{:S(2)}, u32[]{:S(2)}) collective-permute-start(bf16[256,1536]{1,0:T(8,128)(2,1)} %add_convert_fusion.2), channel_id=1, source_target_pairs={{0,1},{1,0},{2,3},{3,2},{4,5},{5,4},{6,7},{7,6},{8,9},{9,8},{10,11... | collective-permute-start | bytes 2359304 | tf_op jit(solution)/shard_map/ppermute | solution.py:67
  362.4 25.6 %all-to-all-start.3 = ((f32[32,1,384]{2,1,0:T(1,128)}), f32[32,1,384]{2,1,0:T(1,128)S(1)}, u32[]{:S(2)}, u32[]{:S(2)}) async-start(f32[32,1,384]{2,1,0:T(1,128)} %reshape.320), calls=%async_computation.4 | async-start | bytes 98304 | tf_op jit(solution)/shard_map/all_to_all | solution.py:157
  381.7 26.8 %collective-permute-start.38 = (bf16[1,1,368,1536]{3,2,1,0:T(8,128)(2,1)}, bf16[1,1,368,1536]{3,2,1,0:T(8,128)(2,1)}, u32[]{:S(2)}, u32[]{:S(2)}) collective-permute-start(bf16[1,1,368,1536]{3,2,1,0:T(8,128)(2,1)} %order.39), channel_id=1, source_target_pairs={{0,4},{4,0},{1,5},{5,1},{2,6},{6,2},{3,7},{7,3},{8,12},{12,8},{9,1... | collective-permute-start | bytes 3391496 | tf_op jit(solution)/shard_map/ppermute | solution.py:67
  385.5 27.7 %collective-permute-start.39 = (bf16[1,1,368,1536]{3,2,1,0:T(8,128)(2,1)}, bf16[1,1,368,1536]{3,2,1,0:T(8,128)(2,1)}, u32[]{:S(2)}, u32[]{:S(2)}) collective-permute-start(bf16[1,1,368,1536]{3,2,1,0:T(8,128)(2,1)} %fusion.10.refs_2_), channel_id=1, source_target_pairs={{0,8},{8,24},{24,16},{16,0},{1,9},{9,25},{25,17},{17,1},{2,10},{10... | collective-permute-start | bytes 3391496 | tf_op jit(solution)/shard_map/ppermute | solution.py:63
  408.5 25.9 %collective-permute-start.44 = (bf16[1,1,368,1536]{3,2,1,0:T(8,128)(2,1)}, bf16[1,1,368,1536]{3,2,1,0:T(8,128)(2,1)S(1)}, u32[]{:S(2)}, u32[]{:S(2)}) collective-permute-start(bf16[1,1,368,1536]{3,2,1,0:T(8,128)(2,1)} %order.43), channel_id=1, source_target_pairs={{0,4},{4,0},{1,5},{5,1},{2,6},{6,2},{3,7},{7,3},{8,12},{12,8},{9,1... | collective-permute-start | bytes 3391496 | tf_op jit(solution)/shard_map/ppermute | solution.py:67
  413.3 29.1 %collective-permute-start.41 = (bf16[256,1536]{1,0:T(8,128)(2,1)}, bf16[256,1536]{1,0:T(8,128)(2,1)}, u32[]{:S(2)}, u32[]{:S(2)}) collective-permute-start(bf16[256,1536]{1,0:T(8,128)(2,1)} %get-tuple-element.120), channel_id=1, source_target_pairs={{0,2},{2,0},{1,3},{3,1},{4,6},{6,4},{5,7},{7,5},{8,10},{10,8},{9,1... | collective-permute-start | bytes 2359304 | tf_op jit(solution)/shard_map/ppermute | solution.py:67
  413.3 25.6 %collective-permute-start.42 = (bf16[256,1536]{1,0:T(8,128)(2,1)}, bf16[256,1536]{1,0:T(8,128)(2,1)}, u32[]{:S(2)}, u32[]{:S(2)}) collective-permute-start(bf16[256,1536]{1,0:T(8,128)(2,1)} %get-tuple-element.123), channel_id=1, source_target_pairs={{0,2},{2,0},{1,3},{3,1},{4,6},{6,4},{5,7},{7,5},{8,10},{10,8},{9,1... | collective-permute-start | bytes 2359304 | tf_op jit(solution)/shard_map/ppermute | solution.py:67
  417.3 28.0 %collective-permute-start.40 = (bf16[1,1,368,1536]{3,2,1,0:T(8,128)(2,1)}, bf16[1,1,368,1536]{3,2,1,0:T(8,128)(2,1)}, u32[]{:S(2)}, u32[]{:S(2)}) collective-permute-start(bf16[1,1,368,1536]{3,2,1,0:T(8,128)(2,1)} %fusion.12), channel_id=1, source_target_pairs={{0,8},{8,24},{24,16},{16,0},{1,9},{9,25},{25,17},{17,1},{2,10},{10... | collective-permute-start | bytes 3391496 | tf_op jit(solution)/shard_map/ppermute | solution.py:63
  418.4 18.1 %all-to-all-start.5 = ((bf16[4,48,2048]{2,1,0:T(8,128)(2,1)}), bf16[4,48,2048]{2,1,0:T(8,128)(2,1)}, u32[]{:S(2)}, u32[]{:S(2)}) async-start(bf16[4,48,2048]{2,1,0:T(8,128)(2,1)} %bitcast.114), calls=%async_computation.6 | async-start | bytes 1572864 | tf_op jit(solution)/shard_map/all_to_all | solution.py:157
  435.5 43.8 %collective-permute-start.45 = (bf16[1,1,368,1536]{3,2,1,0:T(8,128)(2,1)}, bf16[1,1,368,1536]{3,2,1,0:T(8,128)(2,1)}, u32[]{:S(2)}, u32[]{:S(2)}) collective-permute-start(bf16[1,1,368,1536]{3,2,1,0:T(8,128)(2,1)} %order.44), channel_id=1, source_target_pairs={{0,4},{4,0},{1,5},{5,1},{2,6},{6,2},{3,7},{7,3},{8,12},{12,8},{9,1... | collective-permute-start | bytes 3391496 | tf_op jit(solution)/shard_map/ppermute | solution.py:67
  441.1 17.4 %collective-permute-start.43 = (bf16[256,1536]{1,0:T(8,128)(2,1)}, bf16[256,1536]{1,0:T(8,128)(2,1)}, u32[]{:S(2)}, u32[]{:S(2)}) collective-permute-start(bf16[256,1536]{1,0:T(8,128)(2,1)} %add_convert_fusion), channel_id=1, source_target_pairs={{0,1},{1,0},{2,3},{3,2},{4,5},{5,4},{6,7},{7,6},{8,9},{9,8},{10,11... | collective-permute-start | bytes 2359304 | tf_op jit(solution)/shard_map/ppermute | solution.py:67
  449.3 28.9 %collective-permute-start.46 = (bf16[1,1,368,1536]{3,2,1,0:T(8,128)(2,1)}, bf16[1,1,368,1536]{3,2,1,0:T(8,128)(2,1)S(1)}, u32[]{:S(2)}, u32[]{:S(2)}) collective-permute-start(bf16[1,1,368,1536]{3,2,1,0:T(8,128)(2,1)} %fusion.8), channel_id=1, source_target_pairs={{0,8},{8,24},{24,16},{16,0},{1,9},{9,25},{25,17},{17,1},{2,10},{10... | collective-permute-start | bytes 3391496 | tf_op jit(solution)/shard_map/ppermute | solution.py:63
  461.1 15.9 %all-to-all-start.4 = ((f32[32,1,120]{2,1,0:T(1,128)}), f32[32,1,120]{2,1,0:T(1,128)S(1)}, u32[]{:S(2)}, u32[]{:S(2)}) async-start(f32[32,1,120]{2,1,0:T(1,128)} %bitcast.32), calls=%async_computation.5 | async-start | bytes 32768 | tf_op jit(solution)/shard_map/all_to_all | solution.py:157
  482.5 14.2 %all-to-all-start.6 = ((bf16[4,48,1536]{2,1,0:T(8,128)(2,1)}), bf16[4,48,1536]{2,1,0:T(8,128)(2,1)S(1)}, u32[]{:S(2)}, u32[]{:S(2)}) async-start(bf16[4,48,1536]{2,1,0:T(8,128)(2,1)} %bitcast.37), calls=%async_computation.7 | async-start | bytes 1179648 | tf_op jit(solution)/shard_map/all_to_all | solution.py:157
  486.0 1.6 collective-permute-start.47
  (82 other events, 368.5 us)
Sparse Core Ops, SparseCore 0:
  153.1 72.7 all-gather.1
  256.9 118.1 reduce-scatter.1

commit v4 on v3

--- a/solution.py
+++ b/solution.py
@@ -474,7 +474,7 @@
     )(grad_heads, grad_forget, weight_heads, forget_weight)
 
 
-def ffn_tile(hidden_ref, out_grad_ref, both_ref, down_ref, act_ref, dboth_ref):
+def ffn_tile(hidden_ref, out_grad_ref, both_ref, down_ref, act_ref, dboth_ref, term_ref):
     both = product(hidden_ref[...], both_ref[...])
     gate_ffn, up_ffn = both[:, :TILE], both[:, TILE:]
     grad_act = product_nt(out_grad_ref[...], down_ref[...])
@@ -484,6 +484,7 @@
     grad_gate = grad_act * up_ffn * sigmoid_gate * (1.0 + gate_ffn * (1.0 - sigmoid_gate))
     dboth_ref[:, :TILE] = grad_gate.astype(bf16)
     dboth_ref[:, TILE:] = (grad_act * silu).astype(bf16)
+    term_ref[...] = product_tn(hidden_ref[...], dboth_ref[...]).astype(bf16)
 
 
 def feed_forward(parts, out_grad, weight_both, weight_down):
@@ -517,11 +518,13 @@
             whole,
             pl.BlockSpec((tokens, TILE), lambda j: (0, j)),
             pl.BlockSpec((tokens, 2 * TILE), lambda j: (0, j)),
+            pl.BlockSpec((width, 2 * TILE), lambda j: (0, j)),
         ],
         out_shape=[
             jax.ShapeDtypeStruct((tokens, width), bf16),
             jax.ShapeDtypeStruct((tokens, units), bf16),
             jax.ShapeDtypeStruct((tokens, 2 * units), bf16),
+            jax.ShapeDtypeStruct((width, 2 * units), bf16),
         ],
         compiler_params=kernel_params,
         cost_estimate=pl.CostEstimate(
@@ -674,9 +677,7 @@
         arrivals = [(step, other, (both, both_y)[other][step]) for step in range(Z) for other in range(2)]
         (weight_both,) = arrange(arrivals, "y", ((width, 2 * units),), None, both_spots)
 
-    hidden_two, activation, grad_both = feed_forward(hidden_parts, out_grad_all, weight_both, weight_down)
-    both_term = product_tn(hidden_two, grad_both).astype(bf16)
-    grad_both, activation = order((grad_both, activation), (both_term,))
+    hidden_two, activation, grad_both, both_term = feed_forward(hidden_parts, out_grad_all, weight_both, weight_down)
     both_scattered = scatter_units(both_term, 2, rows, ("z", "y"))
     grad_hidden = product_nt(grad_both, weight_both).astype(bf16)
     near_sent = near_sum(grad_hidden[far:]).astype(bf16)

time: 515 us -> 516 us (level)
  Pallas kernels: 85.2 us -> 98.3 us
  matrix products: 54.6 us -> 43.4 us
    pallas_call x1, Pallas kernels: 15.9 us -> 28.9 us  [feed_forward(): pl.pallas_call(kernel, grid=(steps,), in_specs=[first] * GROUP + [whole,...]
    dot_general x3 -> x2, matrix products: 21.6 us -> 10.4 us  [product_tn(): lax.dot_general(left, right, (((0,), (0,)), ((), ())), preferred_element_...]
    unnamed x190 -> x186, local copies, waits for them, and re-layouts: 39.3 us -> 38.3 us
where the time goes in v4:
time: 516 us; the launch traced here: 508 us
  waiting for transfers between devices  164 us (32%)
  Pallas kernels  98.3 us (19%)
  starting transfers between devices  68.5 us (13%)
  local copies, waits for them, and re-layouts  59.6 us (12%)
  other arithmetic  58.6 us (11%)
  matrix products  43.4 us (8%)
  between operations  15.4 us (3%)
    ppermute x37, waiting for transfers between devices, swap(): return lax.ppermute(value, axis, [(0, 1), (1, 0)])  92.1 us
    ppermute x9, waiting for transfers between devices, along_z(): return lax.ppermute(block, 'z', [(0, 1), (1, 3), (3, 2), (2, 0)])  40.9 us
    unnamed x186, local copies, waits for them, and re-layouts  38.3 us
    pallas_call x1, Pallas kernels, feed_forward(): pl.pallas_call(kernel, grid=(steps,), in_specs=[first] * GROUP + [whole,...  28.9 us
    all_to_all x7, starting transfers between devices, exchange(): return lax.all_to_all(shares, axes, 0, 0, tiled=True)  28.1 us
    ppermute x37, starting transfers between devices, swap(): return lax.ppermute(value, axis, [(0, 1), (1, 0)])  26.6 us
    all_to_all x7, waiting for transfers between devices, exchange(): return lax.all_to_all(shares, axes, 0, 0, tiled=True)  24.3 us
    pallas_call x2, Pallas kernels, attend_back(): pl.pallas_call(attend_back_kernel, grid=(tokens // length,), in_specs=[co...  19.9 us
  transfers between devices with their start and end apart: 57, of which 29 were waited for; matrix products, arithmetic and copies ran while one was open for 25% of the time, Pallas kernels for 13%

profile of v4, /device:TPU:0, one launch (start us, length us, event | category | flops | bytes accessed | tf_op | source)
XLA Modules:
  0.0 507.5 jit_solution(16686924342274445168)
XLA Ops:
  7.2 3.0 collective-permute-start.1
  12.2 3.6 all-to-all-start
  20.6 5.9 %all-to-all-done.refs_1_ = bf16[4,48,1536]{2,1,0:T(8,128)(2,1)S(1)} async-done(((bf16[4,48,1536]{2,1,0:T(8,128)(2,1)}), bf16[4,48,1536]{2,1,0:T(8,128)(2,1)S(1)}, u32[]{:S(2)}, u32[]{:S(2)}) %all-to-all-start) | async-done | bytes 589856 | tf_op jit(solution)/shard_map/all_to_all | solution.py:157
  35.6 3.6 all-to-all-start.1
  41.0 9.0 %collective-permute-done.6.refs_1_ = bf16[1,1,240,1536]{3,2,1,0:T(8,128)(2,1)S(1)} collective-permute-done((bf16[1,1,240,1536]{3,2,1,0:T(8,128)(2,1)}, bf16[1,1,240,1536]{3,2,1,0:T(8,128)(2,1)S(1)}, u32[]{:S(2)}, u32[]{:S(2)}) %collective-permute-start.6) | collective-permute-done | bytes 737312 | tf_op jit(solution)/shard_map/ppermute | solution.py:67
  58.7 4.9 all-to-all-start.2
  66.1 4.8 collective-permute-done.8.refs_3_
  70.9 7.2 %collective-permute-done.7.refs_0_ = bf16[1,1,240,1536]{3,2,1,0:T(8,128)(2,1)} collective-permute-done((bf16[1,1,240,1536]{3,2,1,0:T(8,128)(2,1)}, bf16[1,1,240,1536]{3,2,1,0:T(8,128)(2,1)}, u32[]{:S(2)}, u32[]{:S(2)}) %collective-permute-start.7) | collective-permute-done | bytes 737312 | tf_op jit(solution)/shard_map/ppermute | solution.py:63
  87.3 3.9 collective-permute-done.10.refs_2_
  91.1 7.3 %collective-permute-done.9.refs_0_ = bf16[1,1,240,1536]{3,2,1,0:T(8,128)(2,1)S(1)} collective-permute-done((bf16[1,1,240,1536]{3,2,1,0:T(8,128)(2,1)}, bf16[1,1,240,1536]{3,2,1,0:T(8,128)(2,1)S(1)}, u32[]{:S(2)}, u32[]{:S(2)}) %collective-permute-start.9) | collective-permute-done | bytes 737312 | tf_op jit(solution)/shard_map/ppermute | solution.py:63
  100.2 3.6 fusion.2.refs_0_
  106.1 9.3 %collective-permute-done.12 = bf16[1,1,240,1536]{3,2,1,0:T(8,128)(2,1)S(1)} collective-permute-done((bf16[1,1,240,1536]{3,2,1,0:T(8,128)(2,1)}, bf16[1,1,240,1536]{3,2,1,0:T(8,128)(2,1)S(1)}, u32[]{:S(2)}, u32[]{:S(2)}) %collective-permute-start.12) | collective-permute-done | bytes 737312 | tf_op jit(solution)/shard_map/ppermute | solution.py:67
  115.4 4.3 arrange.2
  120.6 7.0 %fusion.3.v_ref.gate_ref = f32[1024,768]{1,0:T(8,128)} fusion(bf16[1024,1536]{1,0:T(8,128)(2,1)} %get-tuple-element.77.hidden_ref, bf16[1536,1536]{1,0:T(8,128)(2,1)} %get-tuple-element.78.weight_ref), kind=kOutput, calls=%fused_computation.14 | convolution fusion | flops 2415919104 | bytes 8650752 | tf_op jit(solution)/shard_map/dot_general | solution.py:39
  127.6 2.6 fusion.16.q_ref.k_ref
  133.0 9.3 %attend.1 = (bf16[1024,384]{1,0:T(8,128)(2,1)S(1)}, f32[1024,384]{1,0:T(8,128)S(1)}, f32[1024,128]{1,0:T(8,128)S(1)}) custom-call(bf16[1024,768]{1,0:T(8,128)(2,1)S(1)} %fusion.16.q_ref.k_ref, bf16[1024,768]{1,0:T(8,128)(2,1)S(1)} %fusion.16.q_ref.k_ref, f32[1024,768]{1,0:T(8,128)} %fusion.3.v_ref.gate_ref, f32[1024,768]{1,0:T(8,128)} %fusion.3.v_ref.gate_ref, ...), custom_call_target="tpu_custom_call" | custom-call | flops 402653184 | bytes 5505024 | tf_op jit(solution)/shard_map/attend/pallas_call | solution.py:360
  142.3 3.5 convolution_convert_fusion.1.refs_0_
  148.8 2.7 fusion.37
  153.3 3.0 collective-permute-start.21
  156.8 3.4 convert_add_fusion.9
  161.4 11.2 %collective-permute-done.22.refs_3_.refs_1_ = bf16[192,2048]{1,0:T(8,128)(2,1)S(1)} collective-permute-done((bf16[192,2048]{1,0:T(8,128)(2,1)S(1)}, bf16[192,2048]{1,0:T(8,128)(2,1)S(1)}, u32[]{:S(2)}, u32[]{:S(2)}) %collective-permute-start.22) | collective-permute-done | bytes 786464 | tf_op jit(solution)/shard_map/ppermute | solution.py:67
  173.5 21.3 %collective-permute-done.21.refs_2_ = bf16[192,2048]{1,0:T(8,128)(2,1)S(1)} collective-permute-done((bf16[192,2048]{1,0:T(8,128)(2,1)}, bf16[192,2048]{1,0:T(8,128)(2,1)S(1)}, u32[]{:S(2)}, u32[]{:S(2)}) %collective-permute-start.21) | collective-permute-done | bytes 786464 | tf_op jit(solution)/shard_map/ppermute | solution.py:63
  195.7 2.4 multiply_reduce_fusion.2
  200.3 10.3 %collective-permute-done.25.refs_2_ = bf16[256,1536]{1,0:T(8,128)(2,1)} collective-permute-done((bf16[256,1536]{1,0:T(8,128)(2,1)S(1)}, bf16[256,1536]{1,0:T(8,128)(2,1)}, u32[]{:S(2)}, u32[]{:S(2)}) %collective-permute-start.25) | collective-permute-done | bytes 786464 | tf_op jit(solution)/shard_map/ppermute | solution.py:67
  212.8 4.8 arrange.3.refs_5_
  218.5 6.4 %all-gather.2.cloned.1.call-done.refs_6_ = bf16[1024,1536]{1,0:T(8,128)(2,1)} async-done(((bf16[256,1536]{1,0:T(8,128)(2,1)}), bf16[1024,1536]{1,0:T(8,128)(2,1)}) %all-gather.2.cloned.1.call-update) | async-done | bytes 3145744 | tf_op jit(solution)/shard_map/all_gather | solution.py:620
  227.2 28.9 %feed_forward.1 = (bf16[1024,1536]{1,0:T(8,128)(2,1)}, bf16[1024,1024]{1,0:T(8,128)(2,1)S(1)}, bf16[1024,2048]{1,0:T(8,128)(2,1)}, bf16[1536,2048]{1,0:T(8,128)(2,1)}) custom-call(bf16[256,1536]{1,0:T(8,128)(2,1)S(1)} %copy-done.42, bf16[256,1536]{1,0:T(8,128)(2,1)S(1)} %copy-done.47, bf16[256,1536]{1,0:T(8,128)(2,1)} %collective-permute-done.25.refs_2_, ...), custom_call_target="tpu_custom_call" | custom-call | flops 9663676416 | bytes 18874368 | tf_op jit(solution)/shard_map/feed_forward/pallas_call | solution.py:508
  257.5 10.1 %convolution_convert_fusion = bf16[1024,1536]{1,0:T(8,128)(2,1)S(1)} fusion(bf16[1024,2048]{1,0:T(8,128)(2,1)} %get-tuple-element.88, bf16[1536,2048]{1,0:T(8,128)(2,1)} %arrange.3.refs_5_), kind=kOutput, calls=%fused_computation.5 | convolution fusion | flops 6444023808 | bytes 13631488 | tf_op jit(solution)/shard_map/dot_general | solution.py:43
  274.1 7.9 %convolution_convert_fusion.2.refs_3_.down_ref = bf16[1024,1536]{1,0:T(8,128)(2,1)} fusion(bf16[1024,1024]{1,0:T(8,128)(2,1)} %order.31, bf16[1024,1536]{1,0:T(8,128)(2,1)} %constant_dynamic-update-slice_fusion.refs_3_.refs_4_), kind=kOutput, calls=%fused_computation.7 | convolution fusion | flops 3222798336 | bytes 8388608 | tf_op jit(solution)/shard_map/dot_general | solution.py:49
  282.0 5.0 convolution_convert_fusion.3.refs_2_
  287.0 5.7 %collective-permute-done.29.refs_0_ = bf16[256,1536]{1,0:T(8,128)(2,1)S(1)} collective-permute-done((bf16[256,1536]{1,0:T(8,128)(2,1)}, bf16[256,1536]{1,0:T(8,128)(2,1)S(1)}, u32[]{:S(2)}, u32[]{:S(2)}) %collective-permute-start.29) | collective-permute-done | bytes 786464 | tf_op jit(solution)/shard_map/ppermute | solution.py:67
  293.6 2.8 multiply_reduce_fusion
  297.0 3.1 fusion.34
  302.7 2.8 fusion.31.grad_ref
  305.5 9.9 %attend_back.2 = (bf16[512,1536]{1,0:T(8,128)(2,1)S(1)}, bf16[512,128]{1,0:T(8,128)(2,1)S(1)}) custom-call(bf16[1024,768]{1,0:T(8,128)(2,1)S(1)} %fusion.16.q_ref.k_ref, bf16[1024,768]{1,0:T(8,128)(2,1)S(1)} %fusion.16.q_ref.k_ref, f32[1024,768]{1,0:T(8,128)} %fusion.3.v_ref.gate_ref, f32[1024,768]{1,0:T(8,128)} %fusion.3.v_ref.gate_ref, ...), custom_call_target="tpu_custom_call" | custom-call | tf_op jit(solution)/shard_map/attend_back/pallas_call | solution.py:382
  317.3 3.1 collective-permute-done.31.refs_0_
  320.4 2.4 fusion.35
  329.1 10.0 %attend_back.3 = (bf16[512,1536]{1,0:T(8,128)(2,1)S(1)}, bf16[512,128]{1,0:T(8,128)(2,1)S(1)}) custom-call(bf16[1024,768]{1,0:T(8,128)(2,1)S(1)} %fusion.16.q_ref.k_ref, bf16[1024,768]{1,0:T(8,128)(2,1)S(1)} %fusion.16.q_ref.k_ref, f32[1024,768]{1,0:T(8,128)} %fusion.3.v_ref.gate_ref, f32[1024,768]{1,0:T(8,128)} %fusion.3.v_ref.gate_ref, ...), custom_call_target="tpu_custom_call" | custom-call | tf_op jit(solution)/shard_map/attend_back/pallas_call | solution.py:382
  339.1 11.9 %attn_terms.1.refs_0_ = bf16[8,368,1536]{2,1,0:T(8,128)(2,1)} custom-call(bf16[1024,1536]{1,0:T(8,128)(2,1)} %get-tuple-element.77.hidden_ref, bf16[512,1536]{1,0:T(8,128)(2,1)S(1)} %copy-done.1, bf16[512,1536]{1,0:T(8,128)(2,1)S(1)} %get-tuple-element.98.far_ref.refs_1_, bf16[1024,384]{1,0:T(8,128)(2,1)S(1)} %copy-done.38, ...), custom_call_target="tpu_custom_call" | custom-call | flops 6039797760 | bytes 15728640 | tf_op jit(solution)/shard_map/attn_terms/pallas_call | solution.py:426
  351.0 2.4 dynamic-slice_bitcast_fusion.3.refs_1_.refs_4_
  359.6 2.5 fusion.25
  363.0 3.8 all-to-all-start.3
  366.9 3.8 dynamic-slice_bitcast_fusion
  370.7 6.4 %collective-permute-done.35.refs_5_.refs_2_ = bf16[256,1536]{1,0:T(8,128)(2,1)S(1)} collective-permute-done((bf16[256,1536]{1,0:T(8,128)(2,1)}, bf16[256,1536]{1,0:T(8,128)(2,1)S(1)}, u32[]{:S(2)}, u32[]{:S(2)}) %collective-permute-start.35) | collective-permute-done | bytes 786464 | tf_op jit(solution)/shard_map/ppermute | solution.py:67
  377.1 4.3 collective-permute-done.37.refs_0_
  383.6 2.5 fusion.10.refs_2_
  390.6 3.8 pad_maximum_fusion.1.heads_ref
  394.4 10.6 %back_through_heads.1 = (bf16[256,1536]{1,0:T(8,128)(2,1)S(1)}, bf16[256,1536]{1,0:T(8,128)(2,1)S(1)}, bf16[256,1536]{1,0:T(8,128)(2,1)S(1)}, bf16[256,1536]{1,0:T(8,128)(2,1)S(1)}) custom-call(bf16[1024,1536]{1,0:T(8,128)(2,1)} %pad_maximum_fusion.1.heads_ref, bf16[1024,128]{1,0:T(8,128)(2,1)S(1)} %constant_dynamic-update-slice_fusion.6.forget_ref, ...), custom_call_target="tpu_custom_call" | custom-call | flops 4831838208 | bytes 12582912 | tf_op jit(solution)/shard_map/back_through_heads/pallas_call | solution.py:458
  410.3 3.6 collective-permute-done.39.refs_0_
  414.4 3.5 fusion.12
  419.0 4.2 all-to-all-start.5
  423.3 2.6 add_convert_fusion.1
  425.9 9.2 %collective-permute-done.44.refs_1_ = bf16[1,1,368,1536]{3,2,1,0:T(8,128)(2,1)S(1)} collective-permute-done((bf16[1,1,368,1536]{3,2,1,0:T(8,128)(2,1)}, bf16[1,1,368,1536]{3,2,1,0:T(8,128)(2,1)S(1)}, u32[]{:S(2)}, u32[]{:S(2)}) %collective-permute-start.44) | collective-permute-done | bytes 1130528 | tf_op jit(solution)/shard_map/ppermute | solution.py:67
  437.1 2.4 unpack_units.1
  439.5 2.2 add_convert_fusion
  443.0 2.5 convert_add_fusion.6.refs_1_
  446.8 3.2 fusion.8
  451.6 7.5 %collective-permute-done.43 = bf16[256,1536]{1,0:T(8,128)(2,1)} collective-permute-done((bf16[256,1536]{1,0:T(8,128)(2,1)}, bf16[256,1536]{1,0:T(8,128)(2,1)}, u32[]{:S(2)}, u32[]{:S(2)}) %collective-permute-start.43) | collective-permute-done | bytes 786464 | tf_op jit(solution)/shard_map/ppermute | solution.py:67
  461.7 4.4 all-to-all-start.4
  466.0 3.2 fusion.22
  469.3 8.3 %all-to-all-done.4 = f32[32,1,120]{2,1,0:T(1,128)S(1)} async-done(((f32[32,1,120]{2,1,0:T(1,128)}), f32[32,1,120]{2,1,0:T(1,128)S(1)}, u32[]{:S(2)}, u32[]{:S(2)}) %all-to-all-start.4) | async-done | bytes 15392 | tf_op jit(solution)/shard_map/all_to_all | solution.py:157
  479.9 2.4 fusion.32
  483.1 3.5 all-to-all-start.6
  489.0 8.3 %all-to-all-done.6.ref = bf16[4,48,1536]{2,1,0:T(8,128)(2,1)S(1)} async-done(((bf16[4,48,1536]{2,1,0:T(8,128)(2,1)}), bf16[4,48,1536]{2,1,0:T(8,128)(2,1)S(1)}, u32[]{:S(2)}, u32[]{:S(2)}) %all-to-all-start.6) | async-done | bytes 589856 | tf_op jit(solution)/shard_map/all_to_all | solution.py:157
  (363 shorter events, 118.9 us)
Async XLA Ops:
  7.2 12.4 %collective-permute-start.1 = (bf16[128,1536]{1,0:T(8,128)(2,1)}, bf16[128,1536]{1,0:T(8,128)(2,1)S(1)}, u32[]{:S(2)}, u32[]{:S(2)}) collective-permute-start(bf16[128,1536]{1,0:T(8,128)(2,1)} %param.28), channel_id=1, source_target_pairs={{0,4},{4,0},{1,5},{5,1},{2,6},{6,2},{3,7},{7,3},{8,12},{12,8},{9,1... | collective-permute-start | bytes 1179656 | tf_op jit(solution)/shard_map/ppermute | solution.py:67
  12.2 14.3 %all-to-all-start = ((bf16[4,48,1536]{2,1,0:T(8,128)(2,1)}), bf16[4,48,1536]{2,1,0:T(8,128)(2,1)S(1)}, u32[]{:S(2)}, u32[]{:S(2)}) async-start(bf16[4,48,1536]{2,1,0:T(8,128)(2,1)} %pack_heads.1), calls=%async_computation | async-start | bytes 1179648 | tf_op jit(solution)/shard_map/all_to_all | solution.py:157
  15.9 13.6 %collective-permute-start.4 = (bf16[48,1536]{1,0:T(8,128)(2,1)S(1)}, bf16[48,1536]{1,0:T(8,128)(2,1)S(1)}, u32[]{:S(2)}, u32[]{:S(2)}) collective-permute-start(bf16[48,1536]{1,0:T(8,128)(2,1)S(1)} %copy-done.84), channel_id=1, source_target_pairs={{0,0},{1,8},{2,16},{3,24},{8,1},{9,9},{10,17},{11,25},{16,2},{17,1... | collective-permute-start | bytes 442376 | tf_op jit(solution)/shard_map/ppermute | solution.py:161
  27.4 26.7 %collective-permute-start.2 = (bf16[256,1536]{1,0:T(8,128)(2,1)}, bf16[256,1536]{1,0:T(8,128)(2,1)}, u32[]{:S(2)}, u32[]{:S(2)}) collective-permute-start(bf16[256,1536]{1,0:T(8,128)(2,1)} %order.22), channel_id=1, source_target_pairs={{0,1},{1,0},{2,3},{3,2},{4,5},{5,4},{6,7},{7,6},{8,9},{9,8},{10,11... | collective-permute-start | bytes 2359304 | tf_op jit(solution)/shard_map/ppermute | solution.py:67
  31.5 18.4 %collective-permute-start.6 = (bf16[1,1,240,1536]{3,2,1,0:T(8,128)(2,1)}, bf16[1,1,240,1536]{3,2,1,0:T(8,128)(2,1)S(1)}, u32[]{:S(2)}, u32[]{:S(2)}) collective-permute-start(bf16[1,1,240,1536]{3,2,1,0:T(8,128)(2,1)} %get-tuple-element.159), channel_id=1, source_target_pairs={{0,4},{4,0},{1,5},{5,1},{2,6},{6,2},{3,7},{7,3},{8,12},{12,8},{9,1... | collective-permute-start | bytes 2211848 | tf_op jit(solution)/shard_map/ppermute | solution.py:67
  31.5 19.5 %collective-permute-start.5 = (bf16[1,1,240,1536]{3,2,1,0:T(8,128)(2,1)}, bf16[1,1,240,1536]{3,2,1,0:T(8,128)(2,1)S(1)}, u32[]{:S(2)}, u32[]{:S(2)}) collective-permute-start(bf16[1,1,240,1536]{3,2,1,0:T(8,128)(2,1)} %get-tuple-element.159), channel_id=1, source_target_pairs={{0,8},{8,24},{24,16},{16,0},{1,9},{9,25},{25,17},{17,1},{2,10},{10... | collective-permute-start | bytes 2211848 | tf_op jit(solution)/shard_map/ppermute | solution.py:63
  35.6 20.6 %all-to-all-start.1 = ((bf16[4,48,2048]{2,1,0:T(8,128)(2,1)}), bf16[4,48,2048]{2,1,0:T(8,128)(2,1)S(1)}, u32[]{:S(2)}, u32[]{:S(2)}) async-start(bf16[4,48,2048]{2,1,0:T(8,128)(2,1)} %order.23), calls=%async_computation.1 | async-start | bytes 1572864 | tf_op jit(solution)/shard_map/all_to_all | solution.py:157
  39.2 42.1 %collective-permute-start = (bf16[256,1536]{1,0:T(8,128)(2,1)}, bf16[256,1536]{1,0:T(8,128)(2,1)}, u32[]{:S(2)}, u32[]{:S(2)}) collective-permute-start(bf16[256,1536]{1,0:T(8,128)(2,1)} %param.15), channel_id=1, source_target_pairs={{0,2},{2,0},{1,3},{3,1},{4,6},{6,4},{5,7},{7,5},{8,10},{10,8},{9,1... | collective-permute-start | bytes 2359304 | tf_op jit(solution)/shard_map/ppermute | solution.py:67
  39.7 25.2 %collective-permute-start.16 = (bf16[256,1536]{1,0:T(8,128)(2,1)}, bf16[256,1536]{1,0:T(8,128)(2,1)}, u32[]{:S(2)}, u32[]{:S(2)}) collective-permute-start(bf16[256,1536]{1,0:T(8,128)(2,1)} %param.29), channel_id=1, source_target_pairs={{0,2},{2,0},{1,3},{3,1},{4,6},{6,4},{5,7},{7,5},{8,10},{10,8},{9,1... | collective-permute-start | bytes 2359304 | tf_op jit(solution)/shard_map/ppermute | solution.py:67
  41.0 15.2 %copy-start.85 = (s32[1,256]{1,0:T(1,128)S(1)}, s32[1,256]{1,0:T(1,128)}, u32[]{:S(2)}) copy-start(s32[1,256]{1,0:T(1,128)} %param.16) | copy-start | bytes 3076
  51.9 19.0 %collective-permute-start.8 = (bf16[1,1,240,1536]{3,2,1,0:T(8,128)(2,1)}, bf16[1,1,240,1536]{3,2,1,0:T(8,128)(2,1)S(1)}, u32[]{:S(2)}, u32[]{:S(2)}) collective-permute-start(bf16[1,1,240,1536]{3,2,1,0:T(8,128)(2,1)} %order.25), channel_id=1, source_target_pairs={{0,4},{4,0},{1,5},{5,1},{2,6},{6,2},{3,7},{7,3},{8,12},{12,8},{9,1... | collective-permute-start | bytes 2211848 | tf_op jit(solution)/shard_map/ppermute | solution.py:67
  53.5 24.6 %collective-permute-start.7 = (bf16[1,1,240,1536]{3,2,1,0:T(8,128)(2,1)}, bf16[1,1,240,1536]{3,2,1,0:T(8,128)(2,1)}, u32[]{:S(2)}, u32[]{:S(2)}) collective-permute-start(bf16[1,1,240,1536]{3,2,1,0:T(8,128)(2,1)} %order.25), channel_id=1, source_target_pairs={{0,8},{8,24},{24,16},{16,0},{1,9},{9,25},{25,17},{17,1},{2,10},{10... | collective-permute-start | bytes 2211848 | tf_op jit(solution)/shard_map/ppermute | solution.py:63
  54.0 27.4 %collective-permute-start.3 = (bf16[256,1536]{1,0:T(8,128)(2,1)}, bf16[256,1536]{1,0:T(8,128)(2,1)}, u32[]{:S(2)}, u32[]{:S(2)}) collective-permute-start(bf16[256,1536]{1,0:T(8,128)(2,1)} %collective-permute-done.2.refs_4_), channel_id=1, source_target_pairs={{0,2},{2,0},{1,3},{3,1},{4,6},{6,4},{5,7},{7,5},{8,10},{10,8},{9,1... | collective-permute-start | bytes 2359304 | tf_op jit(solution)/shard_map/ppermute | solution.py:67
  58.7 26.6 %all-to-all-start.2 = ((bf16[32,64,128]{2,1,0:T(8,128)(2,1)}), bf16[32,64,128]{2,1,0:T(8,128)(2,1)S(1)}, u32[]{:S(2)}, u32[]{:S(2)}) async-start(bf16[32,64,128]{2,1,0:T(8,128)(2,1)} %broadcast_in_dim.25), calls=%async_computation.2 | async-start | bytes 1048576 | tf_op jit(solution)/shard_map/all_to_all | solution.py:157
  63.6 161.3 %all-gather.2.cloned.1.call-start = ((), (), s32[]{:S(2)}) async-start(), calls=%async_computation.8 | async-start | bytes 3932160 | tf_op jit(solution)/shard_map/all_gather | solution.py:620
  78.1 13.0 %collective-permute-start.10 = (bf16[1,1,240,1536]{3,2,1,0:T(8,128)(2,1)}, bf16[1,1,240,1536]{3,2,1,0:T(8,128)(2,1)S(1)}, u32[]{:S(2)}, u32[]{:S(2)}) collective-permute-start(bf16[1,1,240,1536]{3,2,1,0:T(8,128)(2,1)} %get-tuple-element.72), channel_id=1, source_target_pairs={{0,4},{4,0},{1,5},{5,1},{2,6},{6,2},{3,7},{7,3},{8,12},{12,8},{9,1... | collective-permute-start | bytes 2211848 | tf_op jit(solution)/shard_map/ppermute | solution.py:67
  78.1 20.4 %collective-permute-start.9 = (bf16[1,1,240,1536]{3,2,1,0:T(8,128)(2,1)}, bf16[1,1,240,1536]{3,2,1,0:T(8,128)(2,1)S(1)}, u32[]{:S(2)}, u32[]{:S(2)}) collective-permute-start(bf16[1,1,240,1536]{3,2,1,0:T(8,128)(2,1)} %get-tuple-element.72), channel_id=1, source_target_pairs={{0,8},{8,24},{24,16},{16,0},{1,9},{9,25},{25,17},{17,1},{2,10},{10... | collective-permute-start | bytes 2211848 | tf_op jit(solution)/shard_map/ppermute | solution.py:63
  79.5 24.3 %collective-permute-start.13 = (bf16[256,1536]{1,0:T(8,128)(2,1)}, bf16[256,1536]{1,0:T(8,128)(2,1)}, u32[]{:S(2)}, u32[]{:S(2)}) collective-permute-start(bf16[256,1536]{1,0:T(8,128)(2,1)} %get-tuple-element.76), channel_id=1, source_target_pairs={{0,1},{1,0},{2,3},{3,2},{4,5},{5,4},{6,7},{7,6},{8,9},{9,8},{10,11... | collective-permute-start | bytes 2359304 | tf_op jit(solution)/shard_map/ppermute | solution.py:67
  86.7 218.8 %copy-start.7 = (f32[1,1024]{0,1:T(8,128)}, f32[1,1024]{0,1:T(8,128)S(1)}, u32[]{:S(2)}) copy-start(f32[1,1024]{0,1:T(8,128)S(1)} %copy.109) | copy-start | bytes 12292
  99.3 16.1 %collective-permute-start.12 = (bf16[1,1,240,1536]{3,2,1,0:T(8,128)(2,1)}, bf16[1,1,240,1536]{3,2,1,0:T(8,128)(2,1)S(1)}, u32[]{:S(2)}, u32[]{:S(2)}) collective-permute-start(bf16[1,1,240,1536]{3,2,1,0:T(8,128)(2,1)} %get-tuple-element.74), channel_id=1, source_target_pairs={{0,4},{4,0},{1,5},{5,1},{2,6},{6,2},{3,7},{7,3},{8,12},{12,8},{9,1... | collective-permute-start | bytes 2211848 | tf_op jit(solution)/shard_map/ppermute | solution.py:67
  100.1 19.6 %collective-permute-start.11 = (bf16[192,2048]{1,0:T(8,128)(2,1)}, bf16[192,2048]{1,0:T(8,128)(2,1)S(1)}, u32[]{:S(2)}, u32[]{:S(2)}) collective-permute-start(bf16[192,2048]{1,0:T(8,128)(2,1)} %get-tuple-element.73.refs_1_), channel_id=1, source_target_pairs={{0,8},{8,24},{24,16},{16,0},{1,9},{9,25},{25,17},{17,1},{2,10},{10... | collective-permute-start | bytes 2359304 | tf_op jit(solution)/shard_map/ppermute | solution.py:63
  100.2 15.2 %copy-start.30 = (bf16[1,1,240,1536]{3,2,1,0:T(8,128)(2,1)S(1)}, bf16[1,1,240,1536]{3,2,1,0:T(8,128)(2,1)}, u32[]{:S(2)}) copy-start(bf16[1,1,240,1536]{3,2,1,0:T(8,128)(2,1)} %order.25) | copy-start | bytes 2211844
  100.2 15.2 %copy-start.32 = (bf16[1,1,240,1536]{3,2,1,0:T(8,128)(2,1)S(1)}, bf16[1,1,240,1536]{3,2,1,0:T(8,128)(2,1)}, u32[]{:S(2)}) copy-start(bf16[1,1,240,1536]{3,2,1,0:T(8,128)(2,1)} %copy-done.31) | copy-start | bytes 2211844
  103.8 42.0 %collective-permute-start.17 = (bf16[256,1536]{1,0:T(8,128)(2,1)}, bf16[256,1536]{1,0:T(8,128)(2,1)}, u32[]{:S(2)}, u32[]{:S(2)}) collective-permute-start(bf16[256,1536]{1,0:T(8,128)(2,1)} %collective-permute-done.13.refs_4_), channel_id=1, source_target_pairs={{0,2},{2,0},{1,3},{3,1},{4,6},{6,4},{5,7},{7,5},{8,10},{10,8},{9,1... | collective-permute-start | bytes 2359304 | tf_op jit(solution)/shard_map/ppermute | solution.py:67
  130.3 17.6 %collective-permute-start.14 = (bf16[192,2048]{1,0:T(8,128)(2,1)S(1)}, bf16[192,2048]{1,0:T(8,128)(2,1)S(1)}, u32[]{:S(2)}, u32[]{:S(2)}) collective-permute-start(bf16[192,2048]{1,0:T(8,128)(2,1)S(1)} %copy-done.15), channel_id=1, source_target_pairs={{0,8},{8,24},{24,16},{16,0},{1,9},{9,25},{25,17},{17,1},{2,10},{10... | collective-permute-start | bytes 2359304 | tf_op jit(solution)/shard_map/ppermute | solution.py:63
  130.9 17.0 %collective-permute-start.15 = (bf16[192,2048]{1,0:T(8,128)(2,1)S(1)}, bf16[192,2048]{1,0:T(8,128)(2,1)}, u32[]{:S(2)}, u32[]{:S(2)}) collective-permute-start(bf16[192,2048]{1,0:T(8,128)(2,1)S(1)} %copy-done.15), channel_id=1, source_target_pairs={{0,4},{4,0},{1,5},{5,1},{2,6},{6,2},{3,7},{7,3},{8,12},{12,8},{9,1... | collective-permute-start | bytes 2359304 | tf_op jit(solution)/shard_map/ppermute | solution.py:67
  133.0 172.6 %copy-start.5 = (f32[1024,128]{1,0:T(8,128)}, f32[1024,128]{1,0:T(8,128)S(1)}, u32[]{:S(2)}) copy-start(f32[1024,128]{1,0:T(8,128)S(1)} %convolution_add_fusion.forget_ref) | copy-start | bytes 1572868
  151.5 5.3 %collective-permute-start.18 = (bf16[256,1536]{1,0:T(8,128)(2,1)}, bf16[256,1536]{1,0:T(8,128)(2,1)}, u32[]{:S(2)}, u32[]{:S(2)}) collective-permute-start(bf16[256,1536]{1,0:T(8,128)(2,1)} %get-tuple-element.154), channel_id=1, source_target_pairs={{0,2},{2,0},{1,3},{3,1},{4,6},{6,4},{5,7},{7,5},{8,10},{10,8},{9,1... | collective-permute-start | bytes 2359304 | tf_op jit(solution)/shard_map/ppermute | solution.py:67
  151.5 5.3 %collective-permute-start.20 = (bf16[256,1536]{1,0:T(8,128)(2,1)}, bf16[256,1536]{1,0:T(8,128)(2,1)}, u32[]{:S(2)}, u32[]{:S(2)}) collective-permute-start(bf16[256,1536]{1,0:T(8,128)(2,1)} %get-tuple-element.153), channel_id=1, source_target_pairs={{0,2},{2,0},{1,3},{3,1},{4,6},{6,4},{5,7},{7,5},{8,10},{10,8},{9,1... | collective-permute-start | bytes 2359304 | tf_op jit(solution)/shard_map/ppermute | solution.py:67
  152.1 261.8 %reduce-scatter.2.cloned.1.call-start = ((), (), s32[]{:S(2)}) async-start(), calls=%async_computation.9 | async-start | bytes 7077888 | tf_op jit(solution)/shard_map/reduce_scatter | solution.py:174
  152.1 20.5 %collective-permute-start.22 = (bf16[192,2048]{1,0:T(8,128)(2,1)S(1)}, bf16[192,2048]{1,0:T(8,128)(2,1)S(1)}, u32[]{:S(2)}, u32[]{:S(2)}) collective-permute-start(bf16[192,2048]{1,0:T(8,128)(2,1)S(1)} %copy-done.4), channel_id=1, source_target_pairs={{0,4},{4,0},{1,5},{5,1},{2,6},{6,2},{3,7},{7,3},{8,12},{12,8},{9,1... | collective-permute-start | bytes 2359304 | tf_op jit(solution)/shard_map/ppermute | solution.py:67
  153.3 41.5 %collective-permute-start.21 = (bf16[192,2048]{1,0:T(8,128)(2,1)}, bf16[192,2048]{1,0:T(8,128)(2,1)S(1)}, u32[]{:S(2)}, u32[]{:S(2)}) collective-permute-start(bf16[192,2048]{1,0:T(8,128)(2,1)} %get-tuple-element.82.refs_4_), channel_id=1, source_target_pairs={{0,8},{8,24},{24,16},{16,0},{1,9},{9,25},{25,17},{17,1},{2,10},{10... | collective-permute-start | bytes 2359304 | tf_op jit(solution)/shard_map/ppermute | solution.py:63
  156.3 39.4 %collective-permute-start.23 = (bf16[192,2048]{1,0:T(8,128)(2,1)}, bf16[192,2048]{1,0:T(8,128)(2,1)}, u32[]{:S(2)}, u32[]{:S(2)}) collective-permute-start(bf16[192,2048]{1,0:T(8,128)(2,1)} %get-tuple-element.82.refs_4_), channel_id=1, source_target_pairs={{0,4},{4,0},{1,5},{5,1},{2,6},{6,2},{3,7},{7,3},{8,12},{12,8},{9,1... | collective-permute-start | bytes 2359304 | tf_op jit(solution)/shard_map/ppermute | solution.py:67
  160.3 35.4 %collective-permute-start.19 = (bf16[256,1536]{1,0:T(8,128)(2,1)S(1)}, bf16[256,1536]{1,0:T(8,128)(2,1)}, u32[]{:S(2)}, u32[]{:S(2)}) collective-permute-start(bf16[256,1536]{1,0:T(8,128)(2,1)S(1)} %get-tuple-element.152), channel_id=1, source_target_pairs={{0,1},{1,0},{2,3},{3,2},{4,5},{5,4},{6,7},{7,6},{8,9},{9,8},{10,11... | collective-permute-start | bytes 2359304 | tf_op jit(solution)/shard_map/ppermute | solution.py:67
  195.7 17.0 %copy-start.22 = (bf16[192,2048]{1,0:T(8,128)(2,1)S(1)}, bf16[192,2048]{1,0:T(8,128)(2,1)}, u32[]{:S(2)}) copy-start(bf16[192,2048]{1,0:T(8,128)(2,1)} %get-tuple-element.82.refs_4_) | copy-start | bytes 2359300
  198.4 19.2 %copy-start.41 = (bf16[256,1536]{1,0:T(8,128)(2,1)}, bf16[256,1536]{1,0:T(8,128)(2,1)S(1)}, u32[]{:S(2)}) copy-start(bf16[256,1536]{1,0:T(8,128)(2,1)S(1)} %multiply_convert_fusion.refs_0_) | copy-start | bytes 2359300
  198.4 12.2 %collective-permute-start.25 = (bf16[256,1536]{1,0:T(8,128)(2,1)S(1)}, bf16[256,1536]{1,0:T(8,128)(2,1)}, u32[]{:S(2)}, u32[]{:S(2)}) collective-permute-start(bf16[256,1536]{1,0:T(8,128)(2,1)S(1)} %multiply_convert_fusion.refs_0_), channel_id=1, source_target_pairs={{0,1},{1,0},{2,3},{3,2},{4,5},{5,4},{6,7},{7,6},{8,9},{9,8},{10,11... | collective-permute-start | bytes 2359304 | tf_op jit(solution)/shard_map/ppermute | solution.py:67
  199.9 12.0 %collective-permute-start.27 = (bf16[192,2048]{1,0:T(8,128)(2,1)S(1)}, bf16[192,2048]{1,0:T(8,128)(2,1)S(1)}, u32[]{:S(2)}, u32[]{:S(2)}) collective-permute-start(bf16[192,2048]{1,0:T(8,128)(2,1)S(1)} %copy-done.13), channel_id=1, source_target_pairs={{0,4},{4,0},{1,5},{5,1},{2,6},{6,2},{3,7},{7,3},{8,12},{12,8},{9,1... | collective-permute-start | bytes 2359304 | tf_op jit(solution)/shard_map/ppermute | solution.py:67
  200.3 17.3 %collective-permute-start.24 = (bf16[256,1536]{1,0:T(8,128)(2,1)S(1)}, bf16[256,1536]{1,0:T(8,128)(2,1)S(1)}, u32[]{:S(2)}, u32[]{:S(2)}) collective-permute-start(bf16[256,1536]{1,0:T(8,128)(2,1)S(1)} %multiply_convert_fusion.refs_0_), channel_id=1, source_target_pairs={{0,2},{2,0},{1,3},{3,1},{4,6},{6,4},{5,7},{7,5},{8,10},{10,8},{9,1... | collective-permute-start | bytes 2359304 | tf_op jit(solution)/shard_map/ppermute | solution.py:67
  210.6 14.4 %collective-permute-start.26 = (bf16[256,1536]{1,0:T(8,128)(2,1)}, bf16[256,1536]{1,0:T(8,128)(2,1)}, u32[]{:S(2)}, u32[]{:S(2)}) collective-permute-start(bf16[256,1536]{1,0:T(8,128)(2,1)} %collective-permute-done.25.refs_2_), channel_id=1, source_target_pairs={{0,2},{2,0},{1,3},{3,1},{4,6},{6,4},{5,7},{7,5},{8,10},{10,8},{9,1... | collective-permute-start | bytes 2359304 | tf_op jit(solution)/shard_map/ppermute | solution.py:67
  267.7 2.4 collective-permute-start.28
  267.8 3.4 collective-permute-start.30
  273.0 19.8 %collective-permute-start.29 = (bf16[256,1536]{1,0:T(8,128)(2,1)}, bf16[256,1536]{1,0:T(8,128)(2,1)S(1)}, u32[]{:S(2)}, u32[]{:S(2)}) collective-permute-start(bf16[256,1536]{1,0:T(8,128)(2,1)} %get-tuple-element.148.refs_1_), channel_id=1, source_target_pairs={{0,1},{1,0},{2,3},{3,2},{4,5},{5,4},{6,7},{7,6},{8,9},{9,8},{10,11... | collective-permute-start | bytes 2359304 | tf_op jit(solution)/shard_map/ppermute | solution.py:67
  300.1 2.6 collective-permute-start.32
  300.1 20.3 %collective-permute-start.31 = (bf16[256,1536]{1,0:T(8,128)(2,1)}, bf16[256,1536]{1,0:T(8,128)(2,1)}, u32[]{:S(2)}, u32[]{:S(2)}) collective-permute-start(bf16[256,1536]{1,0:T(8,128)(2,1)} %get-tuple-element.138), channel_id=1, source_target_pairs={{0,1},{1,0},{2,3},{3,2},{4,5},{5,4},{6,7},{7,6},{8,9},{9,8},{10,11... | collective-permute-start | bytes 2359304 | tf_op jit(solution)/shard_map/ppermute | solution.py:67
  320.4 5.6 %collective-permute-start.36 = (bf16[256,1536]{1,0:T(8,128)(2,1)}, bf16[256,1536]{1,0:T(8,128)(2,1)S(1)}, u32[]{:S(2)}, u32[]{:S(2)}) collective-permute-start(bf16[256,1536]{1,0:T(8,128)(2,1)} %get-tuple-element.97), channel_id=1, source_target_pairs={{0,2},{2,0},{1,3},{3,1},{4,6},{6,4},{5,7},{7,5},{8,10},{10,8},{9,1... | collective-permute-start | bytes 2359304 | tf_op jit(solution)/shard_map/ppermute | solution.py:67
  322.7 31.9 %collective-permute-start.34 = (bf16[256,1536]{1,0:T(8,128)(2,1)S(1)}, bf16[256,1536]{1,0:T(8,128)(2,1)S(1)}, u32[]{:S(2)}, u32[]{:S(2)}) collective-permute-start(bf16[256,1536]{1,0:T(8,128)(2,1)S(1)} %get-tuple-element.146), channel_id=1, source_target_pairs={{0,2},{2,0},{1,3},{3,1},{4,6},{6,4},{5,7},{7,5},{8,10},{10,8},{9,1... | collective-permute-start | bytes 2359304 | tf_op jit(solution)/shard_map/ppermute | solution.py:67
  323.2 100.0 %collective-permute-start.33 = (bf16[256,1536]{1,0:T(8,128)(2,1)}, bf16[256,1536]{1,0:T(8,128)(2,1)}, u32[]{:S(2)}, u32[]{:S(2)}) collective-permute-start(bf16[256,1536]{1,0:T(8,128)(2,1)} %get-tuple-element.145), channel_id=1, source_target_pairs={{0,2},{2,0},{1,3},{3,1},{4,6},{6,4},{5,7},{7,5},{8,10},{10,8},{9,1... | collective-permute-start | bytes 2359304 | tf_op jit(solution)/shard_map/ppermute | solution.py:67
  353.3 28.0 %collective-permute-start.37 = (bf16[1,1,368,1536]{3,2,1,0:T(8,128)(2,1)}, bf16[1,1,368,1536]{3,2,1,0:T(8,128)(2,1)S(1)}, u32[]{:S(2)}, u32[]{:S(2)}) collective-permute-start(bf16[1,1,368,1536]{3,2,1,0:T(8,128)(2,1)} %dynamic-slice_bitcast_fusion.3.refs_1_.refs_4_), channel_id=1, source_target_pairs={{0,4},{4,0},{1,5},{5,1},{2,6},{6,2},{3,7},{7,3},{8,12},{12,8},{9,1... | collective-permute-start | bytes 3391496 | tf_op jit(solution)/shard_map/ppermute | solution.py:67
  356.8 20.3 %collective-permute-start.35 = (bf16[256,1536]{1,0:T(8,128)(2,1)}, bf16[256,1536]{1,0:T(8,128)(2,1)S(1)}, u32[]{:S(2)}, u32[]{:S(2)}) collective-permute-start(bf16[256,1536]{1,0:T(8,128)(2,1)} %add_convert_fusion.2), channel_id=1, source_target_pairs={{0,1},{1,0},{2,3},{3,2},{4,5},{5,4},{6,7},{7,6},{8,9},{9,8},{10,11... | collective-permute-start | bytes 2359304 | tf_op jit(solution)/shard_map/ppermute | solution.py:67
  363.0 25.5 %all-to-all-start.3 = ((f32[32,1,384]{2,1,0:T(1,128)}), f32[32,1,384]{2,1,0:T(1,128)S(1)}, u32[]{:S(2)}, u32[]{:S(2)}) async-start(f32[32,1,384]{2,1,0:T(1,128)} %reshape.320), calls=%async_computation.4 | async-start | bytes 98304 | tf_op jit(solution)/shard_map/all_to_all | solution.py:157
  382.4 26.8 %collective-permute-start.38 = (bf16[1,1,368,1536]{3,2,1,0:T(8,128)(2,1)}, bf16[1,1,368,1536]{3,2,1,0:T(8,128)(2,1)}, u32[]{:S(2)}, u32[]{:S(2)}) collective-permute-start(bf16[1,1,368,1536]{3,2,1,0:T(8,128)(2,1)} %order.37), channel_id=1, source_target_pairs={{0,4},{4,0},{1,5},{5,1},{2,6},{6,2},{3,7},{7,3},{8,12},{12,8},{9,1... | collective-permute-start | bytes 3391496 | tf_op jit(solution)/shard_map/ppermute | solution.py:67
  386.2 27.7 %collective-permute-start.39 = (bf16[1,1,368,1536]{3,2,1,0:T(8,128)(2,1)}, bf16[1,1,368,1536]{3,2,1,0:T(8,128)(2,1)}, u32[]{:S(2)}, u32[]{:S(2)}) collective-permute-start(bf16[1,1,368,1536]{3,2,1,0:T(8,128)(2,1)} %fusion.10.refs_2_), channel_id=1, source_target_pairs={{0,8},{8,24},{24,16},{16,0},{1,9},{9,25},{25,17},{17,1},{2,10},{10... | collective-permute-start | bytes 3391496 | tf_op jit(solution)/shard_map/ppermute | solution.py:63
  409.2 25.9 %collective-permute-start.44 = (bf16[1,1,368,1536]{3,2,1,0:T(8,128)(2,1)}, bf16[1,1,368,1536]{3,2,1,0:T(8,128)(2,1)S(1)}, u32[]{:S(2)}, u32[]{:S(2)}) collective-permute-start(bf16[1,1,368,1536]{3,2,1,0:T(8,128)(2,1)} %order.41), channel_id=1, source_target_pairs={{0,4},{4,0},{1,5},{5,1},{2,6},{6,2},{3,7},{7,3},{8,12},{12,8},{9,1... | collective-permute-start | bytes 3391496 | tf_op jit(solution)/shard_map/ppermute | solution.py:67
  413.9 29.1 %collective-permute-start.41 = (bf16[256,1536]{1,0:T(8,128)(2,1)}, bf16[256,1536]{1,0:T(8,128)(2,1)}, u32[]{:S(2)}, u32[]{:S(2)}) collective-permute-start(bf16[256,1536]{1,0:T(8,128)(2,1)} %get-tuple-element.116), channel_id=1, source_target_pairs={{0,2},{2,0},{1,3},{3,1},{4,6},{6,4},{5,7},{7,5},{8,10},{10,8},{9,1... | collective-permute-start | bytes 2359304 | tf_op jit(solution)/shard_map/ppermute | solution.py:67
  413.9 25.6 %collective-permute-start.42 = (bf16[256,1536]{1,0:T(8,128)(2,1)}, bf16[256,1536]{1,0:T(8,128)(2,1)}, u32[]{:S(2)}, u32[]{:S(2)}) collective-permute-start(bf16[256,1536]{1,0:T(8,128)(2,1)} %get-tuple-element.119), channel_id=1, source_target_pairs={{0,2},{2,0},{1,3},{3,1},{4,6},{6,4},{5,7},{7,5},{8,10},{10,8},{9,1... | collective-permute-start | bytes 2359304 | tf_op jit(solution)/shard_map/ppermute | solution.py:67
  417.9 28.0 %collective-permute-start.40 = (bf16[1,1,368,1536]{3,2,1,0:T(8,128)(2,1)}, bf16[1,1,368,1536]{3,2,1,0:T(8,128)(2,1)}, u32[]{:S(2)}, u32[]{:S(2)}) collective-permute-start(bf16[1,1,368,1536]{3,2,1,0:T(8,128)(2,1)} %fusion.12), channel_id=1, source_target_pairs={{0,8},{8,24},{24,16},{16,0},{1,9},{9,25},{25,17},{17,1},{2,10},{10... | collective-permute-start | bytes 3391496 | tf_op jit(solution)/shard_map/ppermute | solution.py:63
  419.0 18.0 %all-to-all-start.5 = ((bf16[4,48,2048]{2,1,0:T(8,128)(2,1)}), bf16[4,48,2048]{2,1,0:T(8,128)(2,1)}, u32[]{:S(2)}, u32[]{:S(2)}) async-start(bf16[4,48,2048]{2,1,0:T(8,128)(2,1)} %bitcast.112), calls=%async_computation.6 | async-start | bytes 1572864 | tf_op jit(solution)/shard_map/all_to_all | solution.py:157
  436.1 43.8 %collective-permute-start.45 = (bf16[1,1,368,1536]{3,2,1,0:T(8,128)(2,1)}, bf16[1,1,368,1536]{3,2,1,0:T(8,128)(2,1)}, u32[]{:S(2)}, u32[]{:S(2)}) collective-permute-start(bf16[1,1,368,1536]{3,2,1,0:T(8,128)(2,1)} %order.42), channel_id=1, source_target_pairs={{0,4},{4,0},{1,5},{5,1},{2,6},{6,2},{3,7},{7,3},{8,12},{12,8},{9,1... | collective-permute-start | bytes 3391496 | tf_op jit(solution)/shard_map/ppermute | solution.py:67
  441.7 17.4 %collective-permute-start.43 = (bf16[256,1536]{1,0:T(8,128)(2,1)}, bf16[256,1536]{1,0:T(8,128)(2,1)}, u32[]{:S(2)}, u32[]{:S(2)}) collective-permute-start(bf16[256,1536]{1,0:T(8,128)(2,1)} %add_convert_fusion), channel_id=1, source_target_pairs={{0,1},{1,0},{2,3},{3,2},{4,5},{5,4},{6,7},{7,6},{8,9},{9,8},{10,11... | collective-permute-start | bytes 2359304 | tf_op jit(solution)/shard_map/ppermute | solution.py:67
  450.0 28.9 %collective-permute-start.46 = (bf16[1,1,368,1536]{3,2,1,0:T(8,128)(2,1)}, bf16[1,1,368,1536]{3,2,1,0:T(8,128)(2,1)S(1)}, u32[]{:S(2)}, u32[]{:S(2)}) collective-permute-start(bf16[1,1,368,1536]{3,2,1,0:T(8,128)(2,1)} %fusion.8), channel_id=1, source_target_pairs={{0,8},{8,24},{24,16},{16,0},{1,9},{9,25},{25,17},{17,1},{2,10},{10... | collective-permute-start | bytes 3391496 | tf_op jit(solution)/shard_map/ppermute | solution.py:63
  461.7 16.0 %all-to-all-start.4 = ((f32[32,1,120]{2,1,0:T(1,128)}), f32[32,1,120]{2,1,0:T(1,128)S(1)}, u32[]{:S(2)}, u32[]{:S(2)}) async-start(f32[32,1,120]{2,1,0:T(1,128)} %bitcast.32), calls=%async_computation.5 | async-start | bytes 32768 | tf_op jit(solution)/shard_map/all_to_all | solution.py:157
  483.1 14.2 %all-to-all-start.6 = ((bf16[4,48,1536]{2,1,0:T(8,128)(2,1)}), bf16[4,48,1536]{2,1,0:T(8,128)(2,1)S(1)}, u32[]{:S(2)}, u32[]{:S(2)}) async-start(bf16[4,48,1536]{2,1,0:T(8,128)(2,1)} %bitcast.37), calls=%async_computation.7 | async-start | bytes 1179648 | tf_op jit(solution)/shard_map/all_to_all | solution.py:157
  486.6 1.6 collective-permute-start.47
  (80 other events, 352.3 us)
Sparse Core Ops, SparseCore 0:
  152.2 72.7 all-gather.1
  257.6 118.1 reduce-scatter.1
